TPU v7x, 32 devices: a whole 2x2x4 slice. The times are simulated.
32 devices in a mesh: dp: 16 (over z, x, core), tensor: 2 (over y).
Axes of the slice: x: 2, y: 2, z: 4, core: 2. Of those that a mesh axis runs over, the one named last changes fastest.
Arguments:
- tokens: bfloat16 [32768, 768], P(('dp', 'tensor')), may hold values from -6 to 6
- segment: int32 [32768], P('dp'), may hold values from 0 to 16, as said below
- weight_qkv: bfloat16 [3, 768, 768], P(None, 'dp', 'tensor'), may hold values from -0.3125 to 0.3125
- weight_out: bfloat16 [768, 768], P('tensor', 'dp'), may hold values from -0.625 to 0.625
- weight_in: bfloat16 [768, 3072], P('dp', 'tensor'), may hold values from -0.21875 to 0.21875
- weight_down: bfloat16 [3072, 768], P('tensor', 'dp'), may hold values from -0.15625 to 0.15625
- gain_one: bfloat16 [768], P('dp'), may hold values from 0.5 to 1.5
- shift_one: bfloat16 [768], P('dp'), may hold values from -3 to 3
- gain_two: bfloat16 [768], P('dp'), may hold values from 0.5 to 1.5
- shift_two: bfloat16 [768], P('dp'), may hold values from -3 to 3
- cotangent: bfloat16 [32768, 768], P(('dp', 'tensor')), may hold values from -6 to 6
Outputs:
- output: bfloat16 [32768, 768], P(('dp', 'tensor'))
- input_grad: bfloat16 [32768, 768], P(('dp', 'tensor'))
- grad_weight_qkv: float32 [3, 768, 768], P(None, 'dp', 'tensor')
- grad_weight_out: float32 [768, 768], P('tensor', 'dp')
- grad_weight_in: float32 [768, 3072], P('dp', 'tensor')
- grad_weight_down: float32 [3072, 768], P('tensor', 'dp')
- grad_gain_one: float32 [768], P('dp')
- grad_shift_one: float32 [768], P('dp')
- grad_gain_two: float32 [768], P('dp')
- grad_shift_two: float32 [768], P('dp')
Inputs may be any that keep to these rules, and one draw needn't show every extreme that they name: `segment`: segment numbers start at 0 in each sequence of 512 consecutive tokens and rise by one at each document's first token; each document has 20 to 200 tokens except the last of a sequence, which may be cut shorter; every sequence holds a document of exactly 200 tokens.
All inputs are finite; a program needn't handle non-finite values.
Results may differ from a plain program's by a relative error of at most 0.02.
Values may be sent and summed in bfloat16 or wider, within the bound.
No kernel may reach another device: no remote copies, remote signals or barrier semaphores. Data moves between devices by JAX's collectives and lax.ppermute only.
A program may use at most 192 MiB of HBM per device.

v0:
```python
import jax
import jax.numpy as jnp
from jax import lax
from jax.sharding import PartitionSpec as P

HDIM = 64
SEQ = 512


epsilon = 1e-05


def layer_norm(value, gain, shift):
    centered = value - jnp.mean(value, axis=-1, keepdims=True)
    inverse = lax.rsqrt(jnp.mean(centered * centered, axis=-1, keepdims=True) + epsilon)
    scaled = centered * inverse
    return (scaled * gain + shift, scaled, inverse)


def norm_back(grad_output, scaled, inverse, gain):
    grad_scaled = grad_output * gain
    centered_grad = grad_scaled - jnp.mean(grad_scaled, axis=-1, keepdims=True)
    return inverse * (
        centered_grad - scaled * jnp.mean(grad_scaled * scaled, axis=-1, keepdims=True)
    )


def norm_stats(grad_output, scaled, tensor_count):
    stats = jnp.stack([jnp.sum(grad_output * scaled, axis=0), jnp.sum(grad_output, axis=0)])
    return jnp.broadcast_to(stats[None], (tensor_count,) + stats.shape)


def contract_rows(left, right):
    return lax.dot_general(
        left, right, (((0,), (0,)), ((), ())), preferred_element_type=jnp.float32
    )


def contract_cols(left, right):
    return lax.dot_general(
        left, right, (((1,), (1,)), ((), ())), preferred_element_type=jnp.float32
    )


def masked_scores(queries, key_rows, numbers):
    scaling = HDIM ** (-0.5)
    scores = (
        jnp.einsum("qhd,khd->hqk", queries, key_rows, preferred_element_type=jnp.float32) * scaling
    )
    same_doc = numbers[:, None] == numbers[None, :]
    return jnp.where(same_doc[None, :, :], scores, -1e30)


def attend_forward(block):
    queries, key_rows, value_rows, numbers = block
    scores = masked_scores(queries, key_rows, numbers)
    largest = jnp.max(scores, axis=-1, keepdims=True)
    weights = jnp.exp(scores - largest)
    row_sums = jnp.sum(weights, axis=-1, keepdims=True)
    attention = weights / row_sums
    mixed = jnp.einsum(
        "hqk,khd->qhd",
        attention.astype(jnp.bfloat16),
        value_rows,
        preferred_element_type=jnp.float32,
    )
    return (mixed.astype(jnp.bfloat16), largest + jnp.log(row_sums))


def attend_backward(block):
    queries, key_rows, value_rows, grad_mixed, log_total, numbers = block
    scaling = HDIM ** (-0.5)
    attention = jnp.exp(masked_scores(queries, key_rows, numbers) - log_total)
    grad_attention = jnp.einsum(
        "qhd,khd->hqk", grad_mixed, value_rows, preferred_element_type=jnp.float32
    )
    centre = jnp.sum(attention * grad_attention, axis=-1, keepdims=True)
    grad_scores = (attention * (grad_attention - centre)).astype(jnp.bfloat16)
    grad_queries = (
        jnp.einsum("hqk,khd->qhd", grad_scores, key_rows, preferred_element_type=jnp.float32)
        * scaling
    )
    grad_keys = (
        jnp.einsum("hqk,qhd->khd", grad_scores, queries, preferred_element_type=jnp.float32)
        * scaling
    )
    grad_values = jnp.einsum(
        "hqk,qhd->khd",
        attention.astype(jnp.bfloat16),
        grad_mixed,
        preferred_element_type=jnp.float32,
    )
    return (
        grad_queries.astype(jnp.bfloat16),
        grad_keys.astype(jnp.bfloat16),
        grad_values.astype(jnp.bfloat16),
    )


def shards(
    tokens,
    segment,
    weight_qkv,
    weight_out,
    weight_in,
    weight_down,
    gain_one,
    shift_one,
    gain_two,
    shift_two,
    cotangent,
):
    tensor_count = lax.axis_size("tensor")
    gathered = (
        lax.all_gather(weight_qkv, "dp", axis=1, tiled=True),
        lax.all_gather(weight_out, "dp", axis=1, tiled=True),
        lax.all_gather(weight_in, "dp", axis=0, tiled=True),
        lax.all_gather(weight_down, "dp", axis=1, tiled=True),
        lax.all_gather(gain_one, "dp", axis=0, tiled=True),
        lax.all_gather(shift_one, "dp", axis=0, tiled=True),
        lax.all_gather(gain_two, "dp", axis=0, tiled=True),
        lax.all_gather(shift_two, "dp", axis=0, tiled=True),
    )
    qkv_full, out_full, in_full, down_full = (gathered[0], gathered[1], gathered[2], gathered[3])
    gain_first, shift_first, gain_second, shift_second = [
        piece.astype(jnp.float32) for piece in gathered[4:]
    ]
    token_rows = lax.all_gather(tokens, "tensor", axis=0, tiled=True)
    row_count = token_rows.shape[0]
    seq_count = row_count // SEQ
    local_width = qkv_full.shape[2]
    heads_here = local_width // HDIM
    projected = jnp.einsum(
        "td,jde->jte", token_rows, qkv_full, preferred_element_type=jnp.float32
    ).astype(jnp.bfloat16)
    projected = projected.reshape(3, seq_count, SEQ, heads_here, HDIM)
    numbers = segment.reshape(seq_count, SEQ)
    mixed, log_total = lax.map(attend_forward, (projected[0], projected[1], projected[2], numbers))
    attended = mixed.reshape(row_count, local_width)
    branch_terms = jnp.dot(attended, out_full, preferred_element_type=jnp.float32)
    branch = lax.psum_scatter(
        branch_terms.astype(jnp.bfloat16), "tensor", scatter_dimension=0, tiled=True
    ).astype(jnp.float32)
    first, scaled_one, inverse_one = layer_norm(
        tokens.astype(jnp.float32) + branch, gain_first, shift_first
    )
    first_rows = lax.all_gather(first.astype(jnp.bfloat16), "tensor", axis=0, tiled=True)
    inner = jnp.dot(first_rows, in_full, preferred_element_type=jnp.float32)
    hidden = jax.nn.gelu(inner, approximate=False).astype(jnp.bfloat16)
    second_terms = jnp.dot(hidden, down_full, preferred_element_type=jnp.float32)
    second = lax.psum_scatter(
        second_terms.astype(jnp.bfloat16), "tensor", scatter_dimension=0, tiled=True
    ).astype(jnp.float32)
    final, scaled_two, inverse_two = layer_norm(first + second, gain_second, shift_second)
    output = final.astype(jnp.bfloat16)
    again = (
        lax.all_gather(weight_qkv, "dp", axis=1, tiled=True),
        lax.all_gather(weight_out, "dp", axis=1, tiled=True),
        lax.all_gather(weight_in, "dp", axis=0, tiled=True),
        lax.all_gather(weight_down, "dp", axis=1, tiled=True),
    )
    qkv_back, out_back, in_back, down_back = (again[0], again[1], again[2], again[3])
    grad_final = cotangent.astype(jnp.float32)
    stats_two = norm_stats(grad_final, scaled_two, tensor_count)
    grad_resid_two = norm_back(grad_final, scaled_two, inverse_two, gain_second)
    grad_rows = lax.all_gather(grad_resid_two.astype(jnp.bfloat16), "tensor", axis=0, tiled=True)
    grad_down = contract_rows(hidden, grad_rows)
    grad_hidden = contract_cols(grad_rows, down_back)
    gelu_pull = jax.vjp(lambda value: jax.nn.gelu(value, approximate=False), inner)[1]
    grad_inner = gelu_pull(grad_hidden)[0].astype(jnp.bfloat16)
    grad_in = contract_rows(first_rows, grad_inner)
    first_terms = contract_cols(grad_inner, in_back)
    back_first, stats_two = (
        lax.psum_scatter(
            first_terms.astype(jnp.bfloat16), "tensor", scatter_dimension=0, tiled=True
        ).astype(jnp.float32),
        lax.psum_scatter(
            stats_two.astype(jnp.bfloat16), "tensor", scatter_dimension=0, tiled=True
        ).astype(jnp.float32),
    )
    grad_first = grad_resid_two + back_first
    stats_one = norm_stats(grad_first, scaled_one, tensor_count)
    grad_resid_one = norm_back(grad_first, scaled_one, inverse_one, gain_first)
    branch_rows = lax.all_gather(grad_resid_one.astype(jnp.bfloat16), "tensor", axis=0, tiled=True)
    grad_out = contract_rows(attended, branch_rows)
    grad_attended = (
        contract_cols(branch_rows, out_back)
        .astype(jnp.bfloat16)
        .reshape(seq_count, SEQ, heads_here, HDIM)
    )
    grad_queries, grad_keys, grad_values = lax.map(
        attend_backward,
        (projected[0], projected[1], projected[2], grad_attended, log_total, numbers),
    )
    grad_projected = jnp.stack([grad_queries, grad_keys, grad_values]).reshape(
        3, row_count, local_width
    )
    grad_qkv = jnp.einsum(
        "td,jte->jde", token_rows, grad_projected, preferred_element_type=jnp.float32
    )
    token_terms = jnp.einsum(
        "jte,jde->td", grad_projected, qkv_back, preferred_element_type=jnp.float32
    )
    back_tokens, stats_one = (
        lax.psum_scatter(
            token_terms.astype(jnp.bfloat16), "tensor", scatter_dimension=0, tiled=True
        ).astype(jnp.float32),
        lax.psum_scatter(
            stats_one.astype(jnp.bfloat16), "tensor", scatter_dimension=0, tiled=True
        ).astype(jnp.float32),
    )
    input_grad = (grad_resid_one + back_tokens).astype(jnp.bfloat16)
    stats_one = stats_one[0]
    stats_two = stats_two[0]
    all_sums = (
        lax.psum_scatter(grad_qkv, "dp", scatter_dimension=1, tiled=True),
        lax.psum_scatter(grad_out, "dp", scatter_dimension=1, tiled=True),
        lax.psum_scatter(grad_in, "dp", scatter_dimension=0, tiled=True),
        lax.psum_scatter(grad_down, "dp", scatter_dimension=1, tiled=True),
        lax.psum_scatter(stats_one[0], "dp", scatter_dimension=0, tiled=True),
        lax.psum_scatter(stats_one[1], "dp", scatter_dimension=0, tiled=True),
        lax.psum_scatter(stats_two[0], "dp", scatter_dimension=0, tiled=True),
        lax.psum_scatter(stats_two[1], "dp", scatter_dimension=0, tiled=True),
    )
    return (
        output,
        input_grad,
        all_sums[0],
        all_sums[1],
        all_sums[2],
        all_sums[3],
        all_sums[4],
        all_sums[5],
        all_sums[6],
        all_sums[7],
    )


def solution(mesh):
    return jax.shard_map(
        shards,
        mesh=mesh,
        in_specs=(
            P(("dp", "tensor"), None),
            P("dp"),
            P(None, "dp", "tensor"),
            P("tensor", "dp"),
            P("dp", "tensor"),
            P("tensor", "dp"),
            P("dp"),
            P("dp"),
            P("dp"),
            P("dp"),
            P(("dp", "tensor"), None),
        ),
        out_specs=(
            P(("dp", "tensor"), None),
            P(("dp", "tensor"), None),
            P(None, "dp", "tensor"),
            P("tensor", "dp"),
            P("dp", "tensor"),
            P("tensor", "dp"),
            P("dp"),
            P("dp"),
            P("dp"),
            P("dp"),
        ),
        check_vma=False,
    )
```

profile of v0, /device:TPU:0, one launch (start us, length us, event | category | flops | bytes accessed | tf_op | source)
XLA Modules:
  0.0 1064.2 jit_solution(14832064894492131447)
XLA Ops:
  9.4 26.4 %all_gather.42 = bf16[384,768]{0,1:T(8,128)(2,1)} all-gather(bf16[384,48]{0,1:T(8,128)(2,1)} %param.18), channel_id=1, replica_groups=mesh['dp'=16,'tensor'=2] {'dp'}, dimensions={1}, use_global_device_ids=true | all-gather | bytes 626688 | tf_op jit(solution)/shard_map/all_gather | solution.py:116
  35.8 21.4 %all-gather.10.cloned.1.call-done = bf16[2048,768]{1,0:T(8,128)(2,1)} async-done(((bf16[1024,768]{1,0:T(8,128)(2,1)}), bf16[2048,768]{1,0:T(8,128)(2,1)}) %all-gather.10.cloned.1.call-update) | async-done | bytes 3145744 | tf_op jit(solution)/shard_map/all_gather | solution.py:128
  57.2 42.7 %all-gather.8.cloned.1.call-done = bf16[3,768,384]{2,1,0:T(8,128)(2,1)} async-done(((bf16[3,48,384]{2,1,0:T(8,128)(2,1)}), bf16[3,768,384]{2,1,0:T(8,128)(2,1)}) %all-gather.8.cloned.1.call-update) | async-done | bytes 1769488 | tf_op jit(solution)/shard_map/all_gather | solution.py:115
  100.0 6.3 convert_bitcast_fusion
  107.9 4.0 squeeze.53
  111.9 2.9 copy.62
  118.9 2.4 squeeze.55
  124.3 28.3 %while.26 = (s32[]{:T(128)}, bf16[4,512,6,64]{1,3,2,0:T(8,128)(2,1)}, f32[4,6,512,1]{2,1,3,0:T(8,128)}, bf16[4,512,6,64]{1,3,2,0:T(8,128)(2,1)}, s32[4,512]{1,0:...) while((s32[]{:T(128)}, ...), condition=%wide.region_3.4_spmd, body=%wide.region_0.3_spmd.sunk | while | flops 421983232 | bytes 21606500 | solution.py:138
  127.0 3.7 fusion.136
  134.1 3.7 fusion.136
  141.2 3.7 fusion.136
  148.3 3.7 fusion.136
  152.6 3.8 copy.65
  158.0 3.5 convolution_convert_fusion
  164.4 32.3 %all-reduce.12 = (bf16[768]{0:T(1024)(128)(2,1)S(1)}, bf16[768]{0:T(1024)(128)(2,1)S(1)}, bf16[768]{0:T(1024)(128)(2,1)S(1)}, bf16[768]{0:T(1024)(128)(2,1)S(1)}) all-reduce(bf16[768]{0:T(1024)(128)(2,1)S(1)} %dynamic-update-slice.1, bf16[768]{0:T(1024)(128)(2,1)S(1)} %dynamic-update-slice, ...), channel_id=1, replica_groups=mesh['dp'=16,'tensor'=2] {'dp'}, use_global_device_ids=true, to_apply=%add.1 | all-reduce | flops 3072 | bytes 12288
  196.7 7.3 reduce-scatter.8.cloned.1.call-done
  209.3 39.4 %all-gather.14.cloned.1.call-done = bf16[768,1536]{1,0:T(8,128)(2,1)} async-done(((bf16[48,1536]{1,0:T(8,128)(2,1)}), bf16[768,1536]{1,0:T(8,128)(2,1)}) %all-gather.14.cloned.1.call-update) | async-done | bytes 2359312 | tf_op jit(solution)/shard_map/all_gather | solution.py:117
  248.7 45.8 %all-gather.12.cloned.1.call-done = bf16[2048,768]{1,0:T(8,128)(2,1)} async-done(((bf16[1024,768]{1,0:T(8,128)(2,1)}), bf16[2048,768]{1,0:T(8,128)(2,1)}) %all-gather.12.cloned.1.call-update) | async-done | bytes 3145744 | tf_op jit(solution)/shard_map/all_gather | solution.py:147
  294.5 34.4 %multiply_convert_fusion.1 = (bf16[2048,1536]{1,0:T(8,128)(2,1)}, f32[2048,1536]{1,0:T(8,128)}, f32[2048,1536]{1,0:T(8,128)}) fusion(bf16[2048,768]{1,0:T(8,128)(2,1)} %all-gather.12.cloned.1.call-done, bf16[768,1536]{1,0:T(8,128)(2,1)} %all-gather.14.cloned.1.call-done), kind=kOutput, calls=%fused_computation.69 | convolution fusion | flops 5036310528 | bytes 36962304 | tf_op jit(solution)/shard_map/dot_general | solution.py:148
  328.9 10.4 all-gather.16.cloned.1.call-done
  339.2 9.1 convolution_convert_fusion.2
  348.4 42.2 %reduce-scatter.10.cloned.1.call-done = bf16[1024,768]{1,0:T(8,128)(2,1)} async-done(((bf16[2048,768]{1,0:T(8,128)(2,1)}), bf16[1024,768]{1,0:T(8,128)(2,1)}) %reduce-scatter.10.cloned.1.call-update) | async-done | bytes 1572880 | tf_op jit(solution)/shard_map/reduce_scatter | solution.py:151
  390.6 2.6 fusion.88
  396.6 3.4 fusion.86
  400.0 45.0 %all-gather.18.cloned.1.call-done = bf16[2048,768]{1,0:T(8,128)(2,1)} async-done(((bf16[1024,768]{1,0:T(8,128)(2,1)}), bf16[2048,768]{1,0:T(8,128)(2,1)}) %all-gather.18.cloned.1.call-update) | async-done | bytes 3145744 | tf_op jit(solution)/shard_map/all_gather | solution.py:166
  445.1 16.6 %add_convert_fusion = bf16[2048,1536]{1,0:T(8,128)(2,1)S(1)} fusion(f32[2048,1536]{1,0:T(8,128)} %get-tuple-element.250, f32[2048,1536]{1,0:T(8,128)} %get-tuple-element.261, bf16[2048,768]{1,0:T(8,128)(2,1)} %all-gather.18.cloned.1.call-done, bf16[1536,768]{0,1:T(8,128)(2,1)} %all-gather.16.cloned.1.call-done), kind=kOutput, calls=%fused_computation.68 | convolution fusion | flops 4875878400 | bytes 36962304 | tf_op jit(solution)/shard_map/dot_general | solution.py:40
  461.7 2.6 copy-done.29
  464.3 6.5 convolution_convert_fusion.1
  470.9 43.5 %reduce-scatter.12.cloned.1.call-done = bf16[1024,768]{1,0:T(8,128)(2,1)} async-done(((bf16[2048,768]{1,0:T(8,128)(2,1)}), bf16[1024,768]{1,0:T(8,128)(2,1)}) %reduce-scatter.12.cloned.1.call-update) | async-done | bytes 1572880 | tf_op jit(solution)/shard_map/reduce_scatter | solution.py:174
  514.3 3.8 multiply_reduce_fusion.1
  518.2 3.0 fusion.85
  521.2 45.0 %all-gather.20.cloned.1.call-done = bf16[2048,768]{1,0:T(8,128)(2,1)} async-done(((bf16[1024,768]{1,0:T(8,128)(2,1)}), bf16[2048,768]{1,0:T(8,128)(2,1)}) %all-gather.20.cloned.1.call-update) | async-done | bytes 3145744 | tf_op jit(solution)/shard_map/all_gather | solution.py:184
  566.2 3.8 convolution_convert_fusion.3
  576.6 68.1 %while.27 = (s32[]{:T(128)}, bf16[4,512,6,64]{1,3,2,0:T(8,128)(2,1)}, bf16[4,512,6,64]{1,3,2,0:T(8,128)(2,1)}, bf16[4,512,6,64]{1,3,2,0:T(8,128)(2,1)}, bf16[4,5...) while((s32[]{:T(128)}, ...), condition=%wide.region_17.18_spmd, body=%wide.region_15.17_spmd.sunk | while | flops 1031468032 | bytes 64851124 | solution.py:191
  580.5 3.2 multiply_reduce_fusion.7
  585.7 2.4 fusion.146
  589.9 3.7 fusion.148
  597.5 3.2 multiply_reduce_fusion.7
  602.7 2.4 fusion.146
  606.9 3.7 fusion.148
  614.5 3.2 multiply_reduce_fusion.7
  619.7 2.4 fusion.146
  623.9 3.7 fusion.148
  631.6 3.2 multiply_reduce_fusion.7
  636.8 2.4 fusion.146
  641.0 3.7 fusion.148
  644.7 2.6 copy.73
  647.3 2.5 stack.38
  649.8 2.8 copy.76
  656.2 2.6 copy.75
  662.7 7.3 fusion.79
  670.0 4.0 copy.78
  675.9 7.9 bitcast_convert_fusion
  685.8 9.6 fusion.93
  697.3 9.6 fusion.94
  708.3 4.8 fusion.92
  714.8 7.0 all-reduce.13
  723.2 60.8 %all-reduce.11 = (f32[768]{0:T(1024)S(1)}, f32[768]{0:T(1024)S(1)}, f32[768]{0:T(1024)S(1)}, f32[768]{0:T(1024)S(1)}) all-reduce(f32[768]{0:T(1024)S(1)} %get-tuple-element.198, f32[768]{0:T(1024)S(1)} %get-tuple-element.197, f32[768]{0:T(1024)S(1)} %get-tuple-element.196, ...), channel_id=11, replica_groups=mesh['dp'=16,'tensor'=2] {'dp'}, use_global_device_ids=true, to_apply=%region_26.27.clone | all-reduce | flops 3072 | bytes 24576
  786.3 5.3 all-reduce.16.cloned.1.call-done
  793.3 43.5 %reduce-scatter.14.cloned.1.call-done = bf16[1024,768]{1,0:T(8,128)(2,1)} async-done(((bf16[2048,768]{1,0:T(8,128)(2,1)}), bf16[1024,768]{1,0:T(8,128)(2,1)}) %reduce-scatter.14.cloned.1.call-update) | async-done | bytes 1572880 | tf_op jit(solution)/shard_map/reduce_scatter | solution.py:205
  836.8 3.8 add_convert_fusion.1
  840.6 76.2 %reduce-scatter.18.cloned.1.call-done = f32[48,1536]{1,0:T(8,128)} async-done(((f32[768,1536]{1,0:T(8,128)}), f32[48,1536]{1,0:T(8,128)}) %reduce-scatter.18.cloned.1.call-update) | async-done | bytes 294928 | tf_op jit(solution)/shard_map/reduce_scatter | solution.py:218
  916.8 79.4 %reduce-scatter.20.cloned.1.call-done = f32[1536,48]{0,1:T(8,128)} async-done(((f32[1536,768]{0,1:T(8,128)}), f32[1536,48]{0,1:T(8,128)}) %reduce-scatter.20.cloned.1.call-update) | async-done | bytes 294928 | tf_op jit(solution)/shard_map/reduce_scatter | solution.py:219
  996.2 61.2 %reduce-scatter.16.cloned.1.call-done = f32[384,48]{0,1:T(8,128)} async-done(((f32[384,768]{0,1:T(8,128)}), f32[384,48]{0,1:T(8,128)}) %reduce-scatter.16.cloned.1.call-update) | async-done | bytes 73744 | tf_op jit(solution)/shard_map/reduce_scatter | solution.py:217
  (209 shorter events, 95.2 us)
Async XLA Ops:
  7.2 50.0 %all-gather.10.cloned.1.call-start = ((), (), s32[]{:S(2)}) async-start(), calls=%async_computation.8 | async-start | bytes 4718592 | tf_op jit(solution)/shard_map/all_gather | solution.py:128
  7.9 92.1 %all-gather.8.cloned.1.call-start = ((), (), s32[]{:S(2)}) async-start(), calls=%async_computation.7 | async-start | bytes 1880064 | tf_op jit(solution)/shard_map/all_gather | solution.py:115
  8.7 195.3 %reduce-scatter.8.cloned.1.call-start = ((), (), s32[]{:S(2)}) async-start(), calls=%async_computation.9 | async-start | bytes 4718592 | tf_op jit(solution)/shard_map/reduce_scatter | solution.py:141
  152.6 4.2 copy-start.2
  152.6 4.2 copy-start.18
  152.6 8.9 copy-start.4
  152.6 5.4 copy-start.17
  156.8 1.1 copy-start.13
  161.5 0.7 copy-start.20
  161.5 2.0 copy-start.24
  161.5 2.2 copy-start.25
  161.5 2.4 copy-start.26
  161.5 2.7 copy-start.27
  161.5 42.5 %copy-start = (bf16[1024,768]{1,0:T(8,128)(2,1)S(1)}, bf16[1024,768]{1,0:T(8,128)(2,1)}, u32[]{:S(2)}) copy-start(bf16[1024,768]{1,0:T(8,128)(2,1)} %param.15) | copy-start | bytes 4718596
  161.5 87.2 %all-gather.14.cloned.1.call-start = ((), (), s32[]{:S(2)}) async-start(), calls=%async_computation.11 | async-start | bytes 2506752 | tf_op jit(solution)/shard_map/all_gather | solution.py:117
  162.1 132.4 %all-gather.12.cloned.1.call-start = ((), (), s32[]{:S(2)}) async-start(), calls=%async_computation.10 | async-start | bytes 4718592 | tf_op jit(solution)/shard_map/all_gather | solution.py:147
  203.9 2.0 copy-start.1
  208.7 130.5 %all-gather.16.cloned.1.call-start = ((), (), s32[]{:S(2)}) async-start(), calls=%async_computation.12 | async-start | bytes 2506752 | tf_op jit(solution)/shard_map/all_gather | solution.py:118
  209.3 181.3 %reduce-scatter.10.cloned.1.call-start = ((), (), s32[]{:S(2)}) async-start(), calls=%async_computation.13 | async-start | bytes 4718592 | tf_op jit(solution)/shard_map/reduce_scatter | solution.py:151
  348.3 96.7 %all-gather.18.cloned.1.call-start = ((), (), s32[]{:S(2)}) async-start(), calls=%async_computation.14 | async-start | bytes 4718592 | tf_op jit(solution)/shard_map/all_gather | solution.py:166
  393.3 1.4 copy-start.6
  400.0 114.4 %reduce-scatter.12.cloned.1.call-start = ((), (), s32[]{:S(2)}) async-start(), calls=%async_computation.15 | async-start | bytes 4718592 | tf_op jit(solution)/shard_map/reduce_scatter | solution.py:174
  445.1 19.3 %copy-start.23 = (bf16[768,1536]{1,0:T(8,128)(2,1)S(1)}, bf16[768,1536]{1,0:T(8,128)(2,1)}, u32[]{:S(2)}) copy-start(bf16[768,1536]{1,0:T(8,128)(2,1)} %all-gather.14.cloned.1.call-done) | copy-start | bytes 7077892
  461.7 2.6 copy-start.29
  470.8 95.4 %all-gather.20.cloned.1.call-start = ((), (), s32[]{:S(2)}) async-start(), calls=%async_computation.16 | async-start | bytes 4718592 | tf_op jit(solution)/shard_map/all_gather | solution.py:184
  514.3 3.8 copy-start.5
  514.3 3.8 copy-start.12
  521.1 270.4 %all-reduce.16.cloned.1.call-start = ((), (), s32[]{:S(2)}) async-start(), calls=%async_computation.21 | async-start | bytes 9437184
  572.5 4.0 copy-start.3
  576.6 3.9 copy-start.8
  589.9 3.7 copy-start.9
  593.6 3.9 copy-start.8
  606.9 3.7 copy-start.9
  610.6 3.9 copy-start.8
  623.9 3.7 copy-start.9
  627.6 3.9 copy-start.8
  641.0 3.7 copy-start.9
  647.3 5.3 copy-start.11
  653.8 5.0 copy-start.10
  674.0 1.4 copy-start.15
  674.0 1.9 copy-start.16
  674.0 162.7 %reduce-scatter.14.cloned.1.call-start = ((), (), s32[]{:S(2)}) async-start(), calls=%async_computation.17 | async-start | bytes 4718592 | tf_op jit(solution)/shard_map/reduce_scatter | solution.py:205
  683.8 1.9 copy-start.21
  683.9 232.9 %reduce-scatter.18.cloned.1.call-start = ((), (), s32[]{:S(2)}) async-start(), calls=%async_computation.19 | async-start | bytes 5013504 | tf_op jit(solution)/shard_map/reduce_scatter | solution.py:218
  695.4 1.9 copy-start.22
  695.4 300.8 %reduce-scatter.20.cloned.1.call-start = ((), (), s32[]{:S(2)}) async-start(), calls=%async_computation.20 | async-start | bytes 5013504 | tf_op jit(solution)/shard_map/reduce_scatter | solution.py:219
  706.9 1.4 copy-start.14
  706.9 6.2 copy-start.7
  706.9 6.5 copy-start.28
  706.9 7.7 copy-start.19
  707.0 350.5 %reduce-scatter.16.cloned.1.call-start = ((), (), s32[]{:S(2)}) async-start(), calls=%async_computation.18 | async-start | bytes 1253376 | tf_op jit(solution)/shard_map/reduce_scatter | solution.py:217
Sparse Core Ops, SparseCore 0:
  9.6 47.6 all-gather.9
  59.5 40.3 all-gather.7
  161.6 42.2 reduce-scatter.7
  206.3 42.3 all-gather.13
  250.7 43.7 all-gather.11
  296.9 42.3 all-gather.15
  348.4 42.1 reduce-scatter.9
  400.1 44.9 all-gather.17
  470.9 43.3 reduce-scatter.11
  521.3 44.9 all-gather.19
  674.1 117.3 all-reduce.15
  793.7 42.9 reduce-scatter.13
  841.2 75.5 reduce-scatter.17
  921.6 74.5 reduce-scatter.19
  1000.2 57.1 reduce-scatter.15
where the time goes:
time: 1070 us; the launch traced here: 1060 us
  waiting for transfers between devices  611 us (57%)
  matrix products  193 us (18%)
  blocking collectives  126 us (12%)
  local copies, waits for them, and re-layouts  74.7 us (7%)
  other arithmetic  42.5 us (4%)
  between operations  16 us (1%)
    unnamed x3, blocking collectives  100 us
    reduce_scatter x1, waiting for transfers between devices, shards(): lax.psum_scatter(grad_down, 'dp', scatter_dimension=1, tiled=True)  79.4 us
    reduce_scatter x1, waiting for transfers between devices, shards(): lax.psum_scatter(grad_in, 'dp', scatter_dimension=0, tiled=True)  76.2 us
    reduce_scatter x1, waiting for transfers between devices, shards(): lax.psum_scatter(grad_out, 'dp', scatter_dimension=1, tiled=True)  61.2 us
    all_gather x1, waiting for transfers between devices, shards(): lax.all_gather(first.astype(jnp.bfloat16), 'tensor', axis=0, tiled=True)  45.8 us
    all_gather x1, waiting for transfers between devices, shards(): lax.all_gather(grad_resid_one.astype(jnp.bfloat16), 'tensor', axis=0, til...  45 us
    all_gather x1, waiting for transfers between devices, shards(): lax.all_gather(grad_resid_two.astype(jnp.bfloat16), 'tensor', axis=0, til...  45 us
    reduce_scatter x1, waiting for transfers between devices, shards(): lax.psum_scatter(token_terms.astype(jnp.bfloat16), 'tensor', scatter_dime...  43.5 us
  transfers between devices with their start and end apart: 15, of which 15 were waited for; matrix products, arithmetic and copies ran while one was open for 8% of the time, Pallas kernels for 0%

commit v1 on v0

v1 whole, which is shorter than its diff:
```python
import jax
import jax.numpy as jnp
from jax import lax
from jax.sharding import PartitionSpec as P

HDIM = 64
SEQ = 512
epsilon = 1e-05
ALL = ("tensor", "dp")


def layer_norm(value, gain, shift):
    centered = value - jnp.mean(value, axis=-1, keepdims=True)
    inverse = lax.rsqrt(jnp.mean(centered * centered, axis=-1, keepdims=True) + epsilon)
    scaled = centered * inverse
    return (scaled * gain + shift, scaled, inverse)


def norm_back(grad_output, scaled, inverse, gain):
    grad_scaled = grad_output * gain
    centered_grad = grad_scaled - jnp.mean(grad_scaled, axis=-1, keepdims=True)
    return inverse * (
        centered_grad - scaled * jnp.mean(grad_scaled * scaled, axis=-1, keepdims=True)
    )


def norm_stats(grad_output, scaled):
    return jnp.stack([jnp.sum(grad_output * scaled, axis=0), jnp.sum(grad_output, axis=0)])


def dot_nn(left, right):
    return lax.dot_general(left, right, (((1,), (0,)), ((), ())), preferred_element_type=jnp.float32)


def dot_tn(left, right):
    return lax.dot_general(left, right, (((0,), (0,)), ((), ())), preferred_element_type=jnp.float32)


def dot_nt(left, right):
    return lax.dot_general(left, right, (((1,), (1,)), ((), ())), preferred_element_type=jnp.float32)


def gather(piece):
    full = lax.all_gather(piece, ALL, axis=0, tiled=True)
    return full.reshape(2, full.shape[0] // 2, full.shape[1])


def scatter(full):
    full = full.astype(jnp.bfloat16).reshape(-1, full.shape[-1])
    return lax.psum_scatter(full, ALL, scatter_dimension=0, tiled=True).astype(jnp.float32)


def masked_scores(queries, key_rows, same_doc):
    scores = jnp.einsum("bqhd,bkhd->bhqk", queries, key_rows, preferred_element_type=jnp.float32)
    return jnp.where(same_doc[:, None], scores * HDIM ** (-0.5), -1e30)


def shards(
    tokens,
    segment,
    weight_qkv,
    weight_out,
    weight_in,
    weight_down,
    gain_one,
    shift_one,
    gain_two,
    shift_two,
    cotangent,
):
    rows, width = tokens.shape
    seqs = rows // SEQ
    own = weight_qkv.shape[1]
    qkv = gather(jnp.transpose(weight_qkv, (1, 0, 2)).reshape(own, -1))
    out = gather(weight_out.T)
    win = gather(weight_in)
    down = gather(weight_down.T)
    norms = jnp.stack([gain_one, shift_one, gain_two, shift_two])
    norms = lax.all_gather(norms, "dp", axis=1, tiled=True).astype(jnp.float32)
    gain_first, shift_first, gain_second, shift_second = [norms[i] for i in range(4)]

    numbers = lax.dynamic_slice_in_dim(segment, lax.axis_index("tensor") * rows, rows)
    numbers = numbers.reshape(seqs, SEQ)
    same_doc = numbers[:, :, None] == numbers[:, None, :]

    sides = range(2)
    parts = []
    for t in sides:
        prod = dot_nn(tokens, qkv[t]).astype(jnp.bfloat16)
        third = prod.shape[1] // 3
        parts.append([prod[:, j * third : (j + 1) * third].reshape(seqs, SEQ, -1, HDIM) for j in range(3)])

    attended, kept = [], []
    for t in sides:
        queries, key_rows, value_rows = parts[t]
        scores = masked_scores(queries, key_rows, same_doc)
        largest = jnp.max(scores, axis=-1, keepdims=True)
        weights = jnp.exp(scores - largest)
        row_sums = jnp.sum(weights, axis=-1, keepdims=True)
        attention = weights / row_sums
        mixed = jnp.einsum(
            "bhqk,bkhd->bqhd", attention.astype(jnp.bfloat16), value_rows, preferred_element_type=jnp.float32
        )
        attended.append(mixed.astype(jnp.bfloat16).reshape(rows, -1))
        kept.append(largest + jnp.log(row_sums))

    branch = dot_nt(attended[0], out[0]) + dot_nt(attended[1], out[1])
    first, scaled_one, inverse_one = layer_norm(
        tokens.astype(jnp.float32) + branch, gain_first, shift_first
    )
    first_low = first.astype(jnp.bfloat16)
    inner = [dot_nn(first_low, win[t]) for t in sides]
    hidden = [jax.nn.gelu(inner[t], approximate=False).astype(jnp.bfloat16) for t in sides]
    second = dot_nt(hidden[0], down[0]) + dot_nt(hidden[1], down[1])
    final, scaled_two, inverse_two = layer_norm(first + second, gain_second, shift_second)
    output = final.astype(jnp.bfloat16)

    grad_final = cotangent.astype(jnp.float32)
    stats_two = norm_stats(grad_final, scaled_two)
    grad_resid_two = norm_back(grad_final, scaled_two, inverse_two, gain_second)
    grad_second = grad_resid_two.astype(jnp.bfloat16)
    sum_down = scatter(jnp.stack([dot_tn(grad_second, hidden[t]) for t in sides]))
    grad_inner = []
    for t in sides:
        pull = jax.vjp(lambda value: jax.nn.gelu(value, approximate=False), inner[t])[1]
        grad_inner.append(pull(dot_nn(grad_second, down[t]))[0].astype(jnp.bfloat16))
    sum_in = scatter(jnp.stack([dot_tn(first_low, grad_inner[t]) for t in sides]))
    grad_first = grad_resid_two + dot_nt(grad_inner[0], win[0]) + dot_nt(grad_inner[1], win[1])
    stats_one = norm_stats(grad_first, scaled_one)
    grad_resid_one = norm_back(grad_first, scaled_one, inverse_one, gain_first)
    grad_branch = grad_resid_one.astype(jnp.bfloat16)
    sum_out = scatter(jnp.stack([dot_tn(grad_branch, attended[t]) for t in sides]))
    back = grad_resid_one
    grad_qkv = []
    for t in sides:
        grad_mixed = dot_nn(grad_branch, out[t]).astype(jnp.bfloat16).reshape(seqs, SEQ, -1, HDIM)
        queries, key_rows, value_rows = parts[t]
        attention = jnp.exp(masked_scores(queries, key_rows, same_doc) - kept[t])
        grad_attention = jnp.einsum("bqhd,bkhd->bhqk", grad_mixed, value_rows, preferred_element_type=jnp.float32)
        centre = jnp.sum(attention * grad_attention, axis=-1, keepdims=True)
        grad_scores = (attention * (grad_attention - centre)).astype(jnp.bfloat16)
        scaling = HDIM ** (-0.5)
        grad_queries = scaling * jnp.einsum("bhqk,bkhd->bqhd", grad_scores, key_rows, preferred_element_type=jnp.float32)
        grad_keys = scaling * jnp.einsum("bhqk,bqhd->bkhd", grad_scores, queries, preferred_element_type=jnp.float32)
        grad_values = jnp.einsum(
            "bhqk,bqhd->bkhd", attention.astype(jnp.bfloat16), grad_mixed, preferred_element_type=jnp.float32
        )
        grad_parts = jnp.concatenate(
            [g.astype(jnp.bfloat16).reshape(rows, -1) for g in (grad_queries, grad_keys, grad_values)], axis=1
        )
        grad_qkv.append(dot_tn(tokens, grad_parts))
        back = back + dot_nt(grad_parts, qkv[t])
    sum_qkv = scatter(jnp.stack(grad_qkv))
    input_grad = back.astype(jnp.bfloat16)
    stats = lax.psum(jnp.concatenate([stats_one, stats_two]), ("tensor",))
    stats = lax.psum_scatter(stats, "dp", scatter_dimension=1, tiled=True)
    return (
        output,
        input_grad,
        jnp.transpose(sum_qkv.reshape(own, 3, -1), (1, 0, 2)),
        sum_out.T,
        sum_in,
        sum_down.T,
        stats[0],
        stats[1],
        stats[2],
        stats[3],
    )


def solution(mesh):
    both = P(("dp", "tensor"), None)
    split = P("dp")
    qkv_spec = P(None, "dp", "tensor")
    row_spec = P("tensor", "dp")
    in_spec = P("dp", "tensor")
    return jax.shard_map(
        shards,
        mesh=mesh,
        in_specs=(both, split, qkv_spec, row_spec, in_spec, row_spec, split, split, split, split, both),
        out_specs=(both, both, qkv_spec, row_spec, in_spec, row_spec, split, split, split, split),
        check_vma=False,
    )
```

time: 1070 us -> 882 us (0.82)
  blocking collectives: 126 us -> 28 us
  waiting for transfers between devices: 611 us -> 545 us
  matrix products: 193 us -> 172 us
    all_gather x7 -> x4, waiting for transfers between devices: 250 us -> 129 us  [gather(): full = lax.all_gather(piece, ALL, axis=0, tiled=True)]
    unnamed x3 -> x0, blocking collectives: 100 us -> none
    reduce_scatter x7 -> x4, waiting for transfers between devices: 353 us -> 415 us  [scatter(): lax.psum_scatter(full, ALL, scatter_dimension=0, tiled=True)]
    dot_general x40 -> x36, matrix products: 193 us -> 172 us  [the longest x8 64.8 us: dot_nn(): lax.dot_general(left, right, (((1,), (0,)), ((), ())), preferred_element_...]
    another operation x10 -> x0, local copies, waits for them, and re-layouts: 18.3 us -> none  [the longest x6 13 us: shards(): jnp.stack([grad_queries, grad_keys, grad_values])]
    reshape x2 -> x9, local copies, waits for them, and re-layouts: 1.89 us -> 18.4 us  [the longest x6 9.88 us: shards(): prod[:, j * third:(j + 1) * third].reshape(seqs, SEQ, -1, HDIM)]
    while x24 -> x0, local copies, waits for them, and re-layouts: 15.6 us -> none  [the longest x4 10.2 us: shards(): lax.map(attend_forward, (projected[0], projected[1], projected[2], numbers))]
    convert_element_type x1 -> x11, local copies, waits for them, and re-layouts: 0.93 us -> 12.4 us  [the longest x6 6.07 us: shards(): g.astype(jnp.bfloat16).reshape(rows, -1)]
  transfers between devices with their start and end apart: 15 -> 9, of which waited for: 15 -> 8; matrix products, arithmetic and copies ran while one was open for 8% -> 18% of each run, Pallas kernels for 0% -> 0%
where the time goes in v1:
time: 882 us; the launch traced here: 872 us
  waiting for transfers between devices  545 us (62%)
  matrix products  172 us (20%)
  local copies, waits for them, and re-layouts  70.1 us (8%)
  other arithmetic  40.3 us (5%)
  blocking collectives  28 us (3%)
  between operations  15.3 us (2%)
    reduce_scatter x4, waiting for transfers between devices, scatter(): lax.psum_scatter(full, ALL, scatter_dimension=0, tiled=True)  415 us
    all_gather x4, waiting for transfers between devices, gather(): full = lax.all_gather(piece, ALL, axis=0, tiled=True)  129 us
    dot_general x8, matrix products, dot_nn(): lax.dot_general(left, right, (((1,), (0,)), ((), ())), preferred_element_...  64.8 us
    unnamed x147, local copies, waits for them, and re-layouts  29.4 us
    dot_general x8, matrix products, dot_nt(): lax.dot_general(left, right, (((1,), (1,)), ((), ())), preferred_element_...  27.9 us
    dot_general x8, matrix products, dot_tn(): lax.dot_general(left, right, (((0,), (0,)), ((), ())), preferred_element_...  24.1 us
    all_gather x1, blocking collectives, shards(): norms = lax.all_gather(norms, 'dp', axis=1, tiled=True).astype(jnp.float32)  23.1 us
    dot_general x2, matrix products, shards(): jnp.einsum('bqhd,bkhd->bhqk', grad_mixed, value_rows, preferred_element_t...  17.9 us
  transfers between devices with their start and end apart: 9, of which 8 were waited for; matrix products, arithmetic and copies ran while one was open for 18% of the time, Pallas kernels for 0%

profile of v1, /device:TPU:0, one launch (start us, length us, event | category | flops | bytes accessed | tf_op | source)
XLA Modules:
  0.0 872.1 jit_solution(4716942325598474487)
XLA Ops:
  12.5 23.1 %all-gather = bf16[16,48,4]{1,2,0:T(4,128)(2,1)S(1)} all-gather(bf16[1,48,4]{1,2,0:T(4,128)(2,1)S(1)} %maximum_bitcast_fusion), channel_id=1, replica_groups=mesh['dp'=16,'tensor'=2] {'dp'}, dimensions={0}, use_global_device_ids=true | all-gather | bytes 6528 | tf_op jit(solution)/shard_map/all_gather | solution.py:79
  37.4 2.6 copy.174
  41.6 32.6 %all-gather.6.cloned.1.call-done = bf16[1536,1152]{1,0:T(8,128)(2,1)} async-done(((bf16[48,1152]{1,0:T(8,128)(2,1)}), bf16[1536,1152]{1,0:T(8,128)(2,1)}) %all-gather.6.cloned.1.call-update) | async-done | bytes 3538960 | tf_op jit(solution)/shard_map/all_gather | solution.py:44
  74.2 3.7 convolution_convert_fusion
  82.6 4.2 convolution_convert_fusion.1
  88.2 2.6 reshape.173
  92.0 3.3 reshape.175
  96.1 4.0 fusion.118
  102.0 2.7 copy-done.1
  104.7 2.4 fusion.85
  108.0 2.6 fusion.119
  112.5 2.7 copy-done
  115.1 2.8 fusion.86
  119.7 10.2 %all-gather.8.cloned.1.call-done = bf16[1536,384]{1,0:T(8,128)(2,1)} async-done(((bf16[48,384]{1,0:T(8,128)(2,1)}), bf16[1536,384]{1,0:T(8,128)(2,1)}) %all-gather.8.cloned.1.call-update) | async-done | bytes 1179664 | tf_op jit(solution)/shard_map/all_gather | solution.py:44
  129.9 2.2 fusion.110
  132.2 2.5 fusion.120
  137.3 58.1 %all-gather.10.cloned.1.call-done = bf16[1536,1536]{1,0:T(8,128)(2,1)} async-done(((bf16[48,1536]{1,0:T(8,128)(2,1)}), bf16[1536,1536]{1,0:T(8,128)(2,1)}) %all-gather.10.cloned.1.call-update) | async-done | bytes 4718608 | tf_op jit(solution)/shard_map/all_gather | solution.py:44
  195.4 20.0 %multiply_convert_fusion.2 = (bf16[1024,1536]{1,0:T(8,128)(2,1)}, f32[1024,1536]{1,0:T(8,128)}, f32[1024,1536]{1,0:T(8,128)}) fusion(bf16[1024,768]{0,1:T(8,128)(2,1)} %fusion.37, bf16[1536,1536]{1,0:T(8,128)(2,1)} %all-gather.10.cloned.1.call-done), kind=kOutput, calls=%fused_computation.26 | convolution fusion | flops 2518155264 | bytes 19660800 | tf_op jit(solution)/shard_map/dot_general | solution.py:32
  215.4 17.4 %multiply_convert_fusion.3 = (bf16[1024,1536]{1,0:T(8,128)(2,1)}, f32[1024,1536]{1,0:T(8,128)}, f32[1024,1536]{1,0:T(8,128)}) fusion(bf16[1024,768]{0,1:T(8,128)(2,1)S(1)} %copy-done.32, bf16[1536,1536]{1,0:T(8,128)(2,1)S(1)} %copy-done.48), kind=kOutput, calls=%fused_computation.39 | convolution fusion | flops 2518155264 | bytes 19660800 | tf_op jit(solution)/shard_map/dot_general | solution.py:32
  232.8 27.7 %all-gather.12.cloned.1.call-done = bf16[1536,1536]{1,0:T(8,128)(2,1)} async-done(((bf16[48,1536]{1,0:T(8,128)(2,1)}), bf16[1536,1536]{1,0:T(8,128)(2,1)}) %all-gather.12.cloned.1.call-update) | async-done | bytes 4718608 | tf_op jit(solution)/shard_map/all_gather | solution.py:44
  260.6 5.4 fusion.40
  266.0 2.8 fusion.121
  271.6 2.4 fusion.112
  273.9 8.1 add_convert_fusion
  282.0 2.6 fusion.44
  284.7 7.7 add_convert_fusion.1
  292.4 3.9 multiply_reduce_fusion.2
  301.7 1.9 convolution_convert_fusion.9
  303.6 2.3 copy.177
  305.9 3.6 reshape.181
  309.6 7.9 fusion.78
  317.5 9.0 %multiply_reduce_fusion.1 = (f32[2,6,512]{2,1,0:T(8,128)S(1)}, f32[2,6,512,512]{2,3,1,0:T(8,128)}) fusion(f32[2,6,512,512]{2,3,1,0:T(8,128)} %copy-done.1, f32[2,6,512]{2,1,0:T(8,128)S(1)} %log_add_fusion.1, bf16[2,512,6,64]{1,0,3,2:T(2,128)(2,1)S(1)} %copy-done.8, bf16[2,512,6,64]{1,0,3,2:T(2,128)(2,1)S(1)} %copy-done.3), kind=kOutput, calls=%fused_computation.4 | convolution fusion | flops 412084224 | bytes 26787840 | tf_op jit(solution)/shard_map/bqhd,bkhd->bhqk/dot_general | solution.py:139
  326.5 6.9 multiply_convert_fusion.1
  333.5 2.9 fusion.82
  336.4 2.0 fusion.81
  338.5 1.9 convolution_convert_fusion.8
  340.3 2.3 copy.190
  342.6 3.2 reshape.185
  345.9 7.9 fusion.75
  353.8 9.0 %multiply_reduce_fusion = (f32[2,6,512]{2,1,0:T(8,128)S(1)}, f32[2,6,512,512]{2,3,1,0:T(8,128)}) fusion(f32[2,6,512,512]{2,3,1,0:T(8,128)} %copy-done, f32[2,6,512]{2,1,0:T(8,128)S(1)} %copy-done.42, bf16[2,512,6,64]{1,0,3,2:T(2,128)(2,1)S(1)} %copy-done.6, bf16[2,512,6,64]{1,0,3,2:T(2,128)(2,1)S(1)} %copy-done.4), kind=kOutput, calls=%fused_computation.1 | convolution fusion | flops 412084224 | bytes 26787840 | tf_op jit(solution)/shard_map/bqhd,bkhd->bhqk/dot_general | solution.py:139
  362.8 7.1 multiply_convert_fusion
  369.8 2.9 fusion.84
  372.7 2.0 fusion.83
  375.9 2.0 copy.182
  388.0 2.2 constant_dynamic-update-slice_fusion.1
  390.2 2.1 constant_dynamic-update-slice_fusion
  395.2 2.3 fusion.35
  397.5 2.3 fusion.36
  399.8 2.2 pad_maximum_fusion.2
  402.1 5.1 fusion.34
  407.2 2.8 fusion.33
  410.1 2.6 pad_maximum_fusion.1
  413.0 5.1 fusion.31
  418.1 2.8 fusion.32
  421.0 2.6 pad_maximum_fusion
  423.6 2.6 copy.203
  426.2 4.6 fusion.60
  431.1 4.0 add_convert_fusion.2
  435.1 2.6 copy.204
  438.5 4.9 psum.8
  443.9 87.4 %reduce-scatter.10.cloned.1.call-done = bf16[48,384]{1,0:T(8,128)(2,1)} async-done(((bf16[1536,384]{1,0:T(8,128)(2,1)}), bf16[48,384]{1,0:T(8,128)(2,1)}) %reduce-scatter.10.cloned.1.call-update) | async-done | bytes 36880 | tf_op jit(solution)/shard_map/reduce_scatter | solution.py:50
  532.7 106.9 %reduce-scatter.8.cloned.1.call-done = bf16[48,1152]{1,0:T(8,128)(2,1)} async-done(((bf16[1536,1152]{1,0:T(8,128)(2,1)}), bf16[48,1152]{1,0:T(8,128)(2,1)}) %reduce-scatter.8.cloned.1.call-update) | async-done | bytes 110608 | tf_op jit(solution)/shard_map/reduce_scatter | solution.py:50
  641.3 110.6 %reduce-scatter.14.cloned.1.call-done = bf16[48,1536]{1,0:T(8,128)(2,1)} async-done(((bf16[1536,1536]{1,0:T(8,128)(2,1)}), bf16[48,1536]{1,0:T(8,128)(2,1)}) %reduce-scatter.14.cloned.1.call-update) | async-done | bytes 147472 | tf_op jit(solution)/shard_map/reduce_scatter | solution.py:50
  753.5 109.9 %reduce-scatter.12.cloned.1.call-done = bf16[48,1536]{1,0:T(8,128)(2,1)} async-done(((bf16[1536,1536]{1,0:T(8,128)(2,1)}), bf16[48,1536]{1,0:T(8,128)(2,1)}) %reduce-scatter.12.cloned.1.call-update) | async-done | bytes 147472 | tf_op jit(solution)/shard_map/reduce_scatter | solution.py:50
  (220 shorter events, 56.5 us)
Async XLA Ops:
  7.2 32.8 %copy-start.30 = (bf16[1024,768]{1,0:T(8,128)(2,1)S(1)}, bf16[1024,768]{1,0:T(8,128)(2,1)}, u32[]{:S(2)}) copy-start(bf16[1024,768]{1,0:T(8,128)(2,1)} %param.11) | copy-start | bytes 4718596
  7.2 67.0 %all-gather.6.cloned.1.call-start = ((), (), s32[]{:S(2)}) async-start(), calls=%async_computation.5 | async-start | bytes 3649536 | tf_op jit(solution)/shard_map/all_gather | solution.py:44
  8.9 121.0 %all-gather.8.cloned.1.call-start = ((), (), s32[]{:S(2)}) async-start(), calls=%async_computation.6 | async-start | bytes 1216512 | tf_op jit(solution)/shard_map/all_gather | solution.py:44
  9.7 185.7 %all-gather.10.cloned.1.call-start = ((), (), s32[]{:S(2)}) async-start(), calls=%async_computation.7 | async-start | bytes 4866048 | tf_op jit(solution)/shard_map/all_gather | solution.py:44
  10.4 250.2 %all-gather.12.cloned.1.call-start = ((), (), s32[]{:S(2)}) async-start(), calls=%async_computation.8 | async-start | bytes 4866048 | tf_op jit(solution)/shard_map/all_gather | solution.py:44
  11.0 426.7 %reduce-scatter.16.cloned.1.call-start = ((), (), s32[]{:S(2)}) async-start(), calls=%async_computation.13 | async-start | bytes 417792
  79.0 33.4 %copy-start.5 = (bf16[2,512,6,64]{1,0,3,2:T(2,128)(2,1)}, bf16[2,512,6,64]{1,0,3,2:T(2,128)(2,1)S(1)}, u32[]{:S(2)}) copy-start(bf16[2,512,6,64]{1,0,3,2:T(2,128)(2,1)S(1)} %reshape.177) | copy-start | bytes 2359300
  90.7 11.2 %copy-start.7 = (bf16[2,512,6,64]{1,0,3,2:T(2,128)(2,1)}, bf16[2,512,6,64]{1,0,3,2:T(2,128)(2,1)S(1)}, u32[]{:S(2)}) copy-start(bf16[2,512,6,64]{1,0,3,2:T(2,128)(2,1)S(1)} %reshape.173) | copy-start | bytes 2359300
  96.1 4.0 copy-start.23
  100.2 4.5 copy-start.1
  104.7 3.3 copy-start.18
  104.7 3.3 copy-start.20
  104.7 3.3 copy-start.41
  108.0 21.9 %copy-start.16 = (bf16[48,8,2,512]{3,1,2,0:T(8,128)(2,1)}, bf16[48,8,2,512]{3,1,2,0:T(8,128)(2,1)S(1)}, u32[]{:S(2)}) copy-start(bf16[48,8,2,512]{3,1,2,0:T(8,128)(2,1)S(1)} %copy.221) | copy-start | bytes 2359300
  110.6 4.5 copy-start
  129.9 2.2 copy-start.36
  195.4 20.0 %copy-start.32 = (bf16[1024,768]{0,1:T(8,128)(2,1)S(1)}, bf16[1024,768]{0,1:T(8,128)(2,1)}, u32[]{:S(2)}) copy-start(bf16[1024,768]{0,1:T(8,128)(2,1)} %fusion.37) | copy-start | bytes 4718596
  195.4 20.0 %copy-start.48 = (bf16[1536,1536]{1,0:T(8,128)(2,1)S(1)}, bf16[1536,1536]{1,0:T(8,128)(2,1)}, u32[]{:S(2)}) copy-start(bf16[1536,1536]{1,0:T(8,128)(2,1)} %all-gather.10.cloned.1.call-done) | copy-start | bytes 14155780
  260.6 5.4 copy-start.49
  260.6 5.4 copy-start.51
  266.0 3.3 copy-start.46
  268.9 2.7 copy-start.47
  271.5 10.4 %slice-start.6 = ((s8[4718592]{0:T(1024)(128)(4,1)}), s8[4194304]{0:T(1024)(128)(4,1)S(1)}, s32[]{:S(2)}) async-start(s8[4718592]{0:T(1024)(128)(4,1)} %bitcast.201), calls=%async_computation.20 | async-start | bytes 8388608
  273.9 10.8 %copy-start.34 = (bf16[1024,768]{0,1:T(8,128)(2,1)}, bf16[1024,768]{0,1:T(8,128)(2,1)S(1)}, u32[]{:S(2)}) copy-start(bf16[1024,768]{0,1:T(8,128)(2,1)S(1)} %get-tuple-element.66) | copy-start | bytes 4718596
  273.9 8.1 slice-start.7
  282.0 2.6 copy-start.53
  292.4 3.9 copy-start.55
  298.1 3.7 copy-start.28
  298.1 3.7 copy-start.37
  309.6 8.0 copy-start.3
  309.6 7.9 copy-start.8
  309.6 16.9 %slice-start.3 = ((s8[12582912]{0:T(1024)(128)(4,1)}), s8[4194304]{0:T(1024)(128)(4,1)S(1)}, s32[]{:S(2)}) async-start(s8[12582912]{0:T(1024)(128)(4,1)} %bitcast.165), calls=%async_computation.17 | async-start | bytes 8388608
  309.6 16.9 %slice-start.4 = ((s8[12582912]{0:T(1024)(128)(4,1)}), s8[4194304]{0:T(1024)(128)(4,1)S(1)}, s32[]{:S(2)}) async-start(s8[12582912]{0:T(1024)(128)(4,1)} %bitcast.165), calls=%async_computation.18 | async-start | bytes 8388608
  317.5 9.0 %slice-start.5 = ((s8[12582912]{0:T(1024)(128)(4,1)}), s8[4194304]{0:T(1024)(128)(4,1)S(1)}, s32[]{:S(2)}) async-start(s8[12582912]{0:T(1024)(128)(4,1)} %bitcast.165), calls=%async_computation.19 | async-start | bytes 8388608
  326.5 6.9 copy-start.24
  333.4 3.0 copy-start.22
  338.4 7.4 copy-start.42
  345.9 7.9 copy-start.4
  345.9 7.9 copy-start.6
  345.9 16.9 %slice-start = ((s8[12582912]{0:T(1024)(128)(4,1)}), s8[4194304]{0:T(1024)(128)(4,1)S(1)}, s32[]{:S(2)}) async-start(s8[12582912]{0:T(1024)(128)(4,1)} %bitcast.163), calls=%async_computation.14 | async-start | bytes 8388608
  345.9 16.9 %slice-start.1 = ((s8[12582912]{0:T(1024)(128)(4,1)}), s8[4194304]{0:T(1024)(128)(4,1)S(1)}, s32[]{:S(2)}) async-start(s8[12582912]{0:T(1024)(128)(4,1)} %bitcast.163), calls=%async_computation.15 | async-start | bytes 8388608
  353.8 9.0 %slice-start.2 = ((s8[12582912]{0:T(1024)(128)(4,1)}), s8[4194304]{0:T(1024)(128)(4,1)S(1)}, s32[]{:S(2)}) async-start(s8[12582912]{0:T(1024)(128)(4,1)} %bitcast.163), calls=%async_computation.16 | async-start | bytes 8388608
  362.8 7.1 copy-start.21
  369.8 2.9 copy-start.19
  375.8 155.5 %reduce-scatter.10.cloned.1.call-start = ((), (), s32[]{:S(2)}) async-start(), calls=%async_computation.10 | async-start | bytes 1216512 | tf_op jit(solution)/shard_map/reduce_scatter | solution.py:50
  375.9 3.1 copy-start.27
  379.0 3.1 copy-start.14
  380.0 4.0 copy-start.25
  382.1 3.7 copy-start.26
  387.7 252.0 %reduce-scatter.8.cloned.1.call-start = ((), (), s32[]{:S(2)}) async-start(), calls=%async_computation.9 | async-start | bytes 3649536 | tf_op jit(solution)/shard_map/reduce_scatter | solution.py:50
  387.9 4.3 copy-start.15
  387.9 5.3 copy-start.13
  392.3 2.9 copy-start.31
  392.3 2.9 copy-start.43
  395.2 2.3 copy-start.44
  402.0 349.9 %reduce-scatter.14.cloned.1.call-start = ((), (), s32[]{:S(2)}) async-start(), calls=%async_computation.12 | async-start | bytes 4866048 | tf_op jit(solution)/shard_map/reduce_scatter | solution.py:50
  402.1 5.1 copy-start.35
  402.1 5.1 copy-start.52
  412.7 450.8 %reduce-scatter.12.cloned.1.call-start = ((), (), s32[]{:S(2)}) async-start(), calls=%async_computation.11 | async-start | bytes 4866048 | tf_op jit(solution)/shard_map/reduce_scatter | solution.py:50
  413.0 5.1 copy-start.33
  413.0 5.1 copy-start.54
  426.2 4.6 copy-start.10
  426.2 4.6 copy-start.45
  426.2 4.9 copy-start.50
  (9 other events, 17.0 us)
Sparse Core Ops, SparseCore 0:
  11.5 62.7 all-gather.5
  77.1 52.7 all-gather.7
  132.8 62.5 all-gather.9
  198.1 62.4 all-gather.11
  375.9 54.3 reduce-scatter.15
  436.1 95.1 reduce-scatter.9
  537.6 101.9 reduce-scatter.7
  646.0 105.8 reduce-scatter.13
  757.4 106.0 reduce-scatter.11

commit v2 on v1

--- a/solution.py
+++ b/solution.py
@@ -6,7 +6,118 @@
 HDIM = 64
 SEQ = 512
 epsilon = 1e-05
-ALL = ("tensor", "dp")
+
+AXES = ("dp", "tensor")
+ZS = 4
+
+
+def place(z, x, c, y):
+    return ((z * 2 + x) * 2 + c) * 2 + y
+
+
+def pairs(move):
+    found = []
+    for z in range(ZS):
+        for x in range(2):
+            for c in range(2):
+                for y in range(2):
+                    found.append((place(z, x, c, y), place(*move(z, x, c, y))))
+    return found
+
+
+TO_CORE = pairs(lambda z, x, c, y: (z, x, 1 - c, y))
+TO_NEAR = pairs(lambda z, x, c, y: (z, x, c, 1 - y) if c else (z, 1 - x, c, y))
+TO_FAR = pairs(lambda z, x, c, y: (z, 1 - x, c, y) if c else (z, x, c, 1 - y))
+TO_DEPTH = [pairs(lambda z, x, c, y: ((z - k) % ZS, x, c, y)) for k in range(ZS)]
+
+
+def coords():
+    d = lax.axis_index("dp")
+    y = lax.axis_index("tensor")
+    return d // 4, (d // 2) % 2, d % 2, y
+
+
+def send(value, route):
+    return lax.ppermute(value, AXES, route)
+
+
+def in_order(own, other, at):
+    return jnp.where(at == 0, jnp.stack([own, other]), jnp.stack([other, own]))
+
+
+def tuned():
+    return lax.axis_size("dp") == 16 and lax.axis_size("tensor") == 2
+
+
+def gather_set(left, right):
+    if not tuned():
+        full = lax.all_gather(jnp.concatenate([left, right], axis=1), ("tensor", "dp"), axis=0, tiled=True)
+        return tuple(halves(full.reshape(lax.axis_size("tensor"), -1, full.shape[1])))
+    z, x, c, y = coords()
+    first = c == 0
+    got = send(jnp.where(first, right, left), TO_CORE)
+    mine = jnp.where(first, jnp.concatenate([left, got]), jnp.concatenate([got, right]))
+    own = [mine] + [send(mine, TO_DEPTH[k]) for k in (1, 2, 3)]
+    column = jnp.stack(own + own[:3])
+    column = lax.dynamic_slice_in_dim(column, (ZS - z) % ZS, ZS, 0)
+    near = send(column, TO_NEAR)
+    plane = in_order(column, near, jnp.where(first, x, y))
+    far = send(plane, TO_FAR)
+    whole = in_order(plane, far, jnp.where(first, y, x))
+    sibling = send(whole, TO_CORE)
+    full_left = jnp.where(first, whole, sibling)
+    full_right = jnp.where(first, sibling, whole)
+    n, h = left.shape
+    full_left = jnp.transpose(full_left, (0, 2, 1, 3, 4)).reshape(2, 16 * n, h)
+    full_right = jnp.transpose(full_right, (1, 2, 0, 3, 4)).reshape(2, 16 * n, h)
+    return full_left, full_right
+
+
+def add(a, b):
+    return a.astype(jnp.float32) + b.astype(jnp.float32)
+
+
+def low(a):
+    return a.astype(jnp.bfloat16)
+
+
+def scatter_set(left, right):
+    if not tuned():
+        full = jnp.concatenate([left, right], axis=2)
+        full = lax.psum_scatter(
+            full.reshape(-1, full.shape[2]), ("tensor", "dp"), scatter_dimension=0, tiled=True
+        )
+        full = lax.optimization_barrier(full)
+        return tuple(halves(full.astype(jnp.float32)))
+    z, x, c, y = coords()
+    first = c == 0
+    _, rows, h = left.shape
+    n = rows // 16
+    got = send(jnp.where(first, right, left), TO_CORE)
+    part = low(add(jnp.where(first, left, right), got)).reshape(2, ZS, 2, 2 * n, h)
+
+    def over_y(i):
+        return jnp.transpose(lax.dynamic_index_in_dim(part, i, 0, keepdims=False), (1, 0, 2, 3))
+
+    def over_x(i):
+        return lax.dynamic_index_in_dim(part, i, 2, keepdims=False)
+
+    got = send(jnp.where(first, over_y(1 - y), over_x(1 - x)), TO_FAR)
+    part = low(add(jnp.where(first, over_y(y), over_x(x)), got))
+    at = jnp.where(first, x, y)
+    got = send(lax.dynamic_index_in_dim(part, 1 - at, 0, keepdims=False), TO_NEAR)
+    part = low(add(lax.dynamic_index_in_dim(part, at, 0, keepdims=False), got))
+
+    def depth(k):
+        return lax.dynamic_index_in_dim(part, (z - k) % ZS, 0, keepdims=False)
+
+    total = depth(0).astype(jnp.float32)
+    for k in (1, 2, 3):
+        total = total + send(depth(k), TO_DEPTH[k]).astype(jnp.float32)
+    total = total.reshape(2, n, h)
+    keep = lax.dynamic_index_in_dim(total, c, 0, keepdims=False)
+    got = send(lax.dynamic_index_in_dim(total, 1 - c, 0, keepdims=False), TO_CORE)
+    return jnp.where(first, keep, got), jnp.where(first, got, keep)
 
 
 def layer_norm(value, gain, shift):
@@ -40,14 +151,12 @@
     return lax.dot_general(left, right, (((1,), (1,)), ((), ())), preferred_element_type=jnp.float32)
 
 
-def gather(piece):
-    full = lax.all_gather(piece, ALL, axis=0, tiled=True)
-    return full.reshape(2, full.shape[0] // 2, full.shape[1])
-
-
-def scatter(full):
-    full = full.astype(jnp.bfloat16).reshape(-1, full.shape[-1])
-    return lax.psum_scatter(full, ALL, scatter_dimension=0, tiled=True).astype(jnp.float32)
+def halves(value):
+    return jnp.split(value, 2, axis=-1)
+
+
+def reduce_set(value):
+    return jnp.concatenate(scatter_set(*halves(value)), axis=1)
 
 
 def masked_scores(queries, key_rows, same_doc):
@@ -71,12 +180,21 @@
     rows, width = tokens.shape
     seqs = rows // SEQ
     own = weight_qkv.shape[1]
-    qkv = gather(jnp.transpose(weight_qkv, (1, 0, 2)).reshape(own, -1))
-    out = gather(weight_out.T)
-    win = gather(weight_in)
-    down = gather(weight_down.T)
-    norms = jnp.stack([gain_one, shift_one, gain_two, shift_two])
-    norms = lax.all_gather(norms, "dp", axis=1, tiled=True).astype(jnp.float32)
+    norms = jnp.stack([gain_one, shift_one, gain_two, shift_two], axis=1)
+    norms = jnp.pad(norms, ((0, 0), (0, 124)))
+    set_one = jnp.concatenate([jnp.transpose(weight_qkv, (1, 0, 2)).reshape(own, -1), norms], axis=1)
+    set_two = jnp.concatenate(
+        [weight_out.T, weight_in, jnp.zeros((own, 128), jnp.bfloat16)], axis=1
+    )
+    set_one = jnp.concatenate(gather_set(*halves(set_one)), axis=2)
+    set_two = jnp.concatenate(gather_set(*halves(set_two)), axis=2)
+    down = jnp.concatenate(gather_set(*halves(weight_down.T)), axis=2)
+    span = 3 * weight_qkv.shape[2]
+    qkv = set_one[:, :, :span]
+    wide = weight_out.shape[0]
+    out = set_two[:, :, :wide]
+    win = set_two[:, :, wide : wide + weight_in.shape[1]]
+    norms = set_one[0, :, span : span + 4].T.astype(jnp.float32)
     gain_first, shift_first, gain_second, shift_second = [norms[i] for i in range(4)]
 
     numbers = lax.dynamic_slice_in_dim(segment, lax.axis_index("tensor") * rows, rows)
@@ -119,17 +237,22 @@
     stats_two = norm_stats(grad_final, scaled_two)
     grad_resid_two = norm_back(grad_final, scaled_two, inverse_two, gain_second)
     grad_second = grad_resid_two.astype(jnp.bfloat16)
-    sum_down = scatter(jnp.stack([dot_tn(grad_second, hidden[t]) for t in sides]))
+    sum_down = reduce_set(jnp.stack([low(dot_tn(grad_second, hidden[t])) for t in sides]))
     grad_inner = []
     for t in sides:
         pull = jax.vjp(lambda value: jax.nn.gelu(value, approximate=False), inner[t])[1]
         grad_inner.append(pull(dot_nn(grad_second, down[t]))[0].astype(jnp.bfloat16))
-    sum_in = scatter(jnp.stack([dot_tn(first_low, grad_inner[t]) for t in sides]))
+    grad_in = [low(dot_tn(first_low, grad_inner[t])) for t in sides]
     grad_first = grad_resid_two + dot_nt(grad_inner[0], win[0]) + dot_nt(grad_inner[1], win[1])
     stats_one = norm_stats(grad_first, scaled_one)
     grad_resid_one = norm_back(grad_first, scaled_one, inverse_one, gain_first)
     grad_branch = grad_resid_one.astype(jnp.bfloat16)
-    sum_out = scatter(jnp.stack([dot_tn(grad_branch, attended[t]) for t in sides]))
+    grad_out = [low(dot_tn(grad_branch, attended[t])) for t in sides]
+    stats = low(jnp.concatenate([stats_one, stats_two]).T)
+    stats = jnp.pad(stats, ((0, 0), (0, 124)))
+    sum_two = reduce_set(
+        jnp.stack([jnp.concatenate([grad_in[t], grad_out[t], stats], axis=1) for t in sides])
+    )
     back = grad_resid_one
     grad_qkv = []
     for t in sides:
@@ -148,18 +271,18 @@
         grad_parts = jnp.concatenate(
             [g.astype(jnp.bfloat16).reshape(rows, -1) for g in (grad_queries, grad_keys, grad_values)], axis=1
         )
-        grad_qkv.append(dot_tn(tokens, grad_parts))
+        grad_qkv.append(low(dot_tn(tokens, grad_parts)))
         back = back + dot_nt(grad_parts, qkv[t])
-    sum_qkv = scatter(jnp.stack(grad_qkv))
+    sum_qkv = reduce_set(jnp.pad(jnp.stack(grad_qkv), ((0, 0), (0, 0), (0, 128))))[:, :span]
     input_grad = back.astype(jnp.bfloat16)
-    stats = lax.psum(jnp.concatenate([stats_one, stats_two]), ("tensor",))
-    stats = lax.psum_scatter(stats, "dp", scatter_dimension=1, tiled=True)
+    hidden_span = weight_in.shape[1]
+    stats = sum_two[:, hidden_span + wide : hidden_span + wide + 4].T
     return (
         output,
         input_grad,
         jnp.transpose(sum_qkv.reshape(own, 3, -1), (1, 0, 2)),
-        sum_out.T,
-        sum_in,
+        sum_two[:, hidden_span : hidden_span + wide].T,
+        sum_two[:, :hidden_span],
         sum_down.T,
         stats[0],
         stats[1],

time: 882 us -> 497 us (0.56)
  waiting for transfers between devices: 545 us -> 111 us
  starting transfers between devices: 0.82 us -> 48.2 us
  other arithmetic: 40.3 us -> 79 us
  blocking collectives: 28 us -> 0 us
  between operations: 15.3 us -> 2.72 us
  local copies, waits for them, and re-layouts: 70.1 us -> 81.8 us
    reduce_scatter x4 -> x0, waiting for transfers between devices: 415 us -> none  [scatter(): lax.psum_scatter(full, ALL, scatter_dimension=0, tiled=True)]
    all_gather x4 -> x0, waiting for transfers between devices: 129 us -> none  [gather(): full = lax.all_gather(piece, ALL, axis=0, tiled=True)]
    ppermute x0 -> x42, waiting for transfers between devices: none -> 111 us  [send(): return lax.ppermute(value, AXES, route)]
    ppermute x0 -> x42, starting transfers between devices: none -> 48.2 us  [send(): return lax.ppermute(value, AXES, route)]
    all_gather x1 -> x0, blocking collectives: 23.1 us -> none  [shards(): norms = lax.all_gather(norms, 'dp', axis=1, tiled=True).astype(jnp.float32)]
    select_n x0 -> x23, other arithmetic: none -> 19.2 us  [the longest x3 6.63 us: scatter_set(): got = send(jnp.where(first, right, left), TO_CORE)]
    convert_element_type x2 -> x10, other arithmetic: 1.65 us -> 16.4 us  [the longest x9 15.3 us: low(): return a.astype(jnp.bfloat16)]
    unnamed x147 -> x205, local copies, waits for them, and re-layouts: 29.4 us -> 28.7 us
  transfers between devices with their start and end apart: 9 -> 42, of which waited for: 8 -> 19; matrix products, arithmetic and copies ran while one was open for 18% -> 26% of each run, Pallas kernels for 0% -> 0%
where the time goes in v2:
time: 497 us; the launch traced here: 490 us
  matrix products  168 us (34%)
  waiting for transfers between devices  111 us (22%)
  local copies, waits for them, and re-layouts  81.8 us (16%)
  other arithmetic  79 us (16%)
  starting transfers between devices  48.2 us (10%)
    ppermute x42, waiting for transfers between devices, send(): return lax.ppermute(value, AXES, route)  111 us
    dot_general x8, matrix products, dot_nn(): lax.dot_general(left, right, (((1,), (0,)), ((), ())), preferred_element_...  60.7 us
    ppermute x42, starting transfers between devices, send(): return lax.ppermute(value, AXES, route)  48.2 us
    unnamed x205, local copies, waits for them, and re-layouts  28.7 us
    dot_general x8, matrix products, dot_tn(): lax.dot_general(left, right, (((0,), (0,)), ((), ())), preferred_element_...  25.5 us
    dot_general x8, matrix products, dot_nt(): lax.dot_general(left, right, (((1,), (1,)), ((), ())), preferred_element_...  25.2 us
    dot_general x2, matrix products, shards(): jnp.einsum('bqhd,bkhd->bhqk', grad_mixed, value_rows, preferred_element_t...  17.8 us
    reshape x6, local copies, waits for them, and re-layouts, shards(): prod[:, j * third:(j + 1) * third].reshape(seqs, SEQ, -1, HDIM)  17.2 us
  transfers between devices with their start and end apart: 42, of which 19 were waited for; matrix products, arithmetic and copies ran while one was open for 26% of the time, Pallas kernels for 0%

profile of v2, /device:TPU:0, one launch (start us, length us, event | category | flops | bytes accessed | tf_op | source)
XLA Modules:
  0.0 490.4 jit_solution(4459118558713416981)
XLA Ops:
  14.8 2.6 collective-permute-start.3
  17.4 2.6 collective-permute-start.2
  26.3 4.3 collective-permute-start.15
  30.6 7.7 %collective-permute-start.10 = (bf16[96,1024]{1,0:T(8,128)(2,1)S(1)}, bf16[96,1024]{1,0:T(8,128)(2,1)S(1)}, u32[]{:S(2)}, u32[]{:S(2)}) collective-permute-start(bf16[96,1024]{1,0:T(8,128)(2,1)S(1)} %maximum_select_fusion.8), channel_id=1, source_target_pairs={{0,8},{1,9},{2,10},{3,11},{4,12},{5,13},{6,14},{7,15},{8,16},{9,17... | collective-permute-start | bytes 589832 | tf_op jit(solution)/shard_map/ppermute | solution.py:41
  41.1 7.0 %collective-permute-done.15 = bf16[96,768]{1,0:T(8,128)(2,1)S(1)} collective-permute-done((bf16[96,768]{1,0:T(8,128)(2,1)S(1)}, bf16[96,768]{1,0:T(8,128)(2,1)S(1)}, u32[]{:S(2)}, u32[]{:S(2)}) %collective-permute-start.15) | collective-permute-done | bytes 147488 | tf_op jit(solution)/shard_map/ppermute | solution.py:41
  50.8 10.0 %collective-permute-done.8 = bf16[96,1024]{1,0:T(8,128)(2,1)S(1)} collective-permute-done((bf16[96,1024]{1,0:T(8,128)(2,1)S(1)}, bf16[96,1024]{1,0:T(8,128)(2,1)S(1)}, u32[]{:S(2)}, u32[]{:S(2)}) %collective-permute-start.8) | collective-permute-done | bytes 196640 | tf_op jit(solution)/shard_map/ppermute | solution.py:41
  65.4 15.7 %collective-permute-done.11 = bf16[4,96,1024]{2,1,0:T(8,128)(2,1)S(1)} collective-permute-done((bf16[4,96,1024]{2,1,0:T(8,128)(2,1)S(1)}, bf16[4,96,1024]{2,1,0:T(8,128)(2,1)S(1)}, u32[]{:S(2)}, u32[]{:S(2)}) %collective-permute-start.11) | collective-permute-done | bytes 786464 | tf_op jit(solution)/shard_map/ppermute | solution.py:41
  83.2 4.3 collective-permute-done.5
  88.0 5.7 %collective-permute-done.18 = bf16[4,96,768]{2,1,0:T(8,128)(2,1)S(1)} collective-permute-done((bf16[4,96,768]{2,1,0:T(8,128)(2,1)S(1)}, bf16[4,96,768]{2,1,0:T(8,128)(2,1)S(1)}, u32[]{:S(2)}, u32[]{:S(2)}) %collective-permute-start.18) | collective-permute-done | bytes 589856 | tf_op jit(solution)/shard_map/ppermute | solution.py:41
  96.7 21.8 %collective-permute-done.19 = bf16[2,4,96,768]{3,2,0,1:T(8,128)(2,1)S(1)} collective-permute-done((bf16[2,4,96,768]{3,2,0,1:T(8,128)(2,1)S(1)}, bf16[2,4,96,768]{3,2,0,1:T(8,128)(2,1)S(1)}, u32[]{:S(2)}, u32[]{:S(2)}) %collective-permute-start.19) | collective-permute-done | bytes 1179680 | tf_op jit(solution)/shard_map/ppermute | solution.py:41
  128.0 3.5 fusion.29
  132.8 3.2 reshape.536
  137.5 3.0 fusion.133
  140.6 2.6 reshape.539
  143.1 3.5 reshape.541
  146.7 3.4 reshape.540
  150.1 3.9 fusion.135
  155.9 2.7 copy-done
  158.8 3.1 fusion.71
  161.9 2.6 fusion.136
  164.5 3.1 fusion
  169.2 3.0 reshape.534
  174.6 6.2 %fusion.70 = bf16[2,512,6,64]{1,3,2,0:T(8,128)(2,1)S(1)} fusion(f32[2,6,512,512]{2,3,1,0:T(8,128)} %copy-done.1, f32[2,6,512]{2,1,0:T(8,128)S(1)} %copy-done.79, f32[2,6,512]{2,1,0:T(8,128)S(1)} %copy-done.78, bf16[2,512,6,64]{1,0,3,2:T(2,128)(2,1)S(1)} %reshape.534), kind=kOutput, calls=%fused_computation.169 | convolution fusion | flops 412483584 | bytes 14204928 | tf_op jit(solution)/shard_map/bhqk,bkhd->bqhd/dot_general | solution.py:219
  194.5 17.7 %multiply_convert_fusion.2 = (bf16[1024,1536]{1,0:T(8,128)(2,1)S(1)}, f32[1024,1536]{1,0:T(8,128)}, f32[1024,1536]{1,0:T(8,128)}) fusion(bf16[1024,768]{0,1:T(8,128)(2,1)S(1)} %fusion.43, bf16[2,768,1024]{2,1,0:T(8,128)(2,1)S(1)} %bitcast.408, bf16[2,768,1024]{2,1,0:T(8,128)(2,1)S(1)} %bitcast.396), kind=kOutput, calls=%fused_computation.30 | convolution fusion | flops 2522873856 | bytes 23592960 | tf_op jit(solution)/shard_map/dot_general | solution.py:143
  212.2 17.9 %multiply_convert_fusion.3 = (bf16[1024,1536]{1,0:T(8,128)(2,1)S(1)}, f32[1024,1536]{1,0:T(8,128)}, f32[1024,1536]{1,0:T(8,128)}) fusion(bf16[1024,768]{0,1:T(8,128)(2,1)S(1)} %fusion.43, bf16[2,768,1024]{2,1,0:T(8,128)(2,1)S(1)} %bitcast.409, bf16[2,768,1024]{2,1,0:T(8,128)(2,1)S(1)} %bitcast.397), kind=kOutput, calls=%fused_computation.43 | convolution fusion | flops 2522873856 | bytes 23592960 | tf_op jit(solution)/shard_map/dot_general | solution.py:143
  230.1 2.6 fusion.97
  232.8 2.9 fusion.138
  238.3 2.4 fusion.101
  240.7 3.9 fusion.40
  244.6 3.9 fusion.39
  248.4 7.9 %add_convert_fusion.2 = bf16[1024,1536]{1,0:T(8,128)(2,1)S(1)} fusion(f32[1024,1536]{1,0:T(8,128)} %get-tuple-element.56, f32[1024,1536]{1,0:T(8,128)} %get-tuple-element.122, bf16[1024,768]{0,1:T(8,128)(2,1)S(1)} %get-tuple-element.69, bf16[2,768,768]{2,1,0:T(8,128)(2,1)S(1)} %bitcast.437, bf16[2,768,768]{2,1,0:T(8,128)(2,1)S(1)} %bitcast.443), kind=kOutput, calls=%fused_computation.29 | convolution fusion | flops 2442657792 | bytes 22020096 | tf_op jit(solution)/shard_map/dot_general | solution.py:143
  256.4 3.9 convolution_convert_fusion.5
  260.3 4.3 fusion.118
  264.6 7.7 %add_convert_fusion.1 = bf16[1024,1536]{1,0:T(8,128)(2,1)S(1)} fusion(f32[1024,1536]{1,0:T(8,128)} %get-tuple-element.58, f32[1024,1536]{1,0:T(8,128)} %get-tuple-element.121, bf16[1024,768]{0,1:T(8,128)(2,1)S(1)} %get-tuple-element.69, bf16[2,768,768]{2,1,0:T(8,128)(2,1)S(1)} %bitcast.444, bf16[2,768,768]{2,1,0:T(8,128)(2,1)S(1)} %bitcast.438), kind=kOutput, calls=%fused_computation.28 | convolution fusion | flops 2442657792 | bytes 22020096 | tf_op jit(solution)/shard_map/dot_general | solution.py:143
  272.4 7.3 %multiply_reduce_fusion.2 = (bf16[768]{0:T(1024)(128)(2,1)S(1)}, f32[1024]{0:T(1024)S(1)}, f32[1024]{0:T(1024)S(1)}, bf16[768]{0:T(1024)(128)(2,1)S(1)}, f32[1024,768]{0,1:T(8,128)S(1)}) fusion(f32[1024,768]{0,1:T(8,128)S(1)} %get-tuple-element.120, f32[1024]{0:T(1024)S(1)} %add_rsqrt_fusion.1, f32[1024]{0:T(1024)S(1)} %broadcast_multiply_fusion.5, ...), kind=kOutput, calls=%fused_computation.98 | convolution fusion | flops 2435576320 | bytes 23634944 | tf_op jit(solution)/shard_map/dot_general | solution.py:151
  289.0 2.3 copy.148
  291.3 3.2 reshape.546
  294.5 7.9 %fusion.63 = bf16[2,512,6,64]{1,3,2,0:T(8,128)(2,1)} fusion(f32[2,6,512,512]{2,3,1,0:T(8,128)} %copy-done.1, f32[2,6,512]{2,1,0:T(8,128)S(1)} %copy-done.64, bf16[2,512,6,64]{1,0,3,2:T(2,128)(2,1)} %reshape.546), kind=kOutput, calls=%fused_computation.164 | convolution fusion | flops 409337856 | bytes 14180352 | tf_op jit(solution)/shard_map/bhqk,bqhd->bkhd/dot_general | solution.py:268
  302.4 9.0 %multiply_reduce_fusion.1 = (f32[2,6,512]{2,1,0:T(8,128)S(1)}, f32[2,6,512,512]{2,3,1,0:T(8,128)}) fusion(f32[2,6,512,512]{2,3,1,0:T(8,128)} %copy-done.1, f32[2,6,512]{2,1,0:T(8,128)S(1)} %copy-done.64, bf16[2,512,6,64]{1,0,3,2:T(2,128)(2,1)S(1)} %copy-done.32, bf16[2,512,6,64]{1,0,3,2:T(2,128)(2,1)S(1)} %copy-done.18), kind=kOutput, calls=%fused_computation.4 | convolution fusion | flops 412084224 | bytes 26787840 | tf_op jit(solution)/shard_map/bqhd,bkhd->bhqk/dot_general | solution.py:262
  311.4 7.1 %multiply_convert_fusion.1 = bf16[2,6,512,512]{2,3,1,0:T(8,128)(2,1)S(1)} fusion(f32[2,6,512,512]{2,3,1,0:T(8,128)} %get-tuple-element.127, f32[2,6,512,512]{2,3,1,0:T(8,128)S(1)} %bitcast.382, f32[2,6,512]{2,1,0:T(8,128)S(1)} %get-tuple-element.126, f32[2,6,512]{2,1,0:T(8,128)S(1)} %copy-done.64), kind=kLoop, calls=%fused_computation.3 | loop fusion | flops 12582912 | bytes 31506432 | tf_op jit(solution)/shard_map/convert_element_type | solution.py:264
  318.6 2.9 fusion.67
  323.5 2.3 copy.161
  325.8 3.2 reshape.550
  329.1 7.0 %fusion.60 = bf16[2,512,6,64]{1,3,2,0:T(8,128)(2,1)S(1)} fusion(f32[2,6,512,512]{2,3,1,0:T(8,128)} %copy-done, f32[2,6,512]{2,1,0:T(8,128)S(1)} %copy-done.63, bf16[2,512,6,64]{1,0,3,2:T(2,128)(2,1)} %reshape.550), kind=kOutput, calls=%fused_computation.163 | convolution fusion | flops 409337856 | bytes 14180352 | tf_op jit(solution)/shard_map/bhqk,bqhd->bkhd/dot_general | solution.py:268
  336.1 8.9 %multiply_reduce_fusion = (f32[2,6,512]{2,1,0:T(8,128)S(1)}, f32[2,6,512,512]{2,3,1,0:T(8,128)}) fusion(f32[2,6,512,512]{2,3,1,0:T(8,128)} %copy-done, f32[2,6,512]{2,1,0:T(8,128)S(1)} %copy-done.63, bf16[2,512,6,64]{1,0,3,2:T(2,128)(2,1)S(1)} %copy-done.30, bf16[2,512,6,64]{1,0,3,2:T(2,128)(2,1)S(1)} %copy-done.19), kind=kOutput, calls=%fused_computation.1 | convolution fusion | flops 412084224 | bytes 26787840 | tf_op jit(solution)/shard_map/bqhd,bkhd->bhqk/dot_general | solution.py:262
  345.0 7.1 %multiply_convert_fusion = bf16[2,6,512,512]{2,3,1,0:T(8,128)(2,1)S(1)} fusion(f32[2,6,512,512]{2,3,1,0:T(8,128)} %get-tuple-element.129, f32[2,6,512,512]{2,3,1,0:T(8,128)S(1)} %bitcast.380, f32[2,6,512]{2,1,0:T(8,128)S(1)} %get-tuple-element.128, f32[2,6,512]{2,1,0:T(8,128)S(1)} %copy-done.63), kind=kLoop, calls=%fused_computation | loop fusion | flops 12582912 | bytes 31506432 | tf_op jit(solution)/shard_map/convert_element_type | solution.py:264
  366.4 2.7 fusion.42
  377.1 5.2 %convolution_convert_fusion.4 = bf16[768,1536]{1,0:T(8,128)(2,1)S(1)} fusion(bf16[1024,768]{0,1:T(8,128)(2,1)} %copy-done.56, bf16[1024,1536]{1,0:T(8,128)(2,1)} %copy-done.81), kind=kOutput, calls=%fused_computation.80 | convolution fusion | flops 2417098752 | bytes 7077888 | tf_op jit(solution)/shard_map/dot_general | solution.py:147
  383.4 3.1 broadcast_select_fusion
  387.1 2.9 add_convert_fusion.4
  401.1 3.6 collective-permute-done.22
  407.5 3.6 add_convert_fusion
  416.0 3.8 add_convert_fusion.6
  419.8 2.6 copy.183
  422.4 2.9 copy.184
  430.9 2.4 collective-permute-done.24
  435.3 4.2 collective-permute-done.25
  441.1 2.5 add_convert_fusion.5
  445.3 4.4 collective-permute-done.37
  453.6 5.9 %collective-permute-done.38 = bf16[96,768]{1,0:T(8,128)(2,1)} collective-permute-done((bf16[96,768]{1,0:T(8,128)(2,1)}, bf16[96,768]{1,0:T(8,128)(2,1)}, u32[]{:S(2)}, u32[]{:S(2)}) %collective-permute-start.38) | collective-permute-done | bytes 147488 | tf_op jit(solution)/shard_map/ppermute | solution.py:41
  461.2 3.9 collective-permute-done.39
  466.7 3.2 collective-permute-start.31
  470.5 9.4 %collective-permute-done.31 = bf16[96,1024]{1,0:T(8,128)(2,1)S(1)} collective-permute-done((bf16[96,1024]{1,0:T(8,128)(2,1)S(1)}, bf16[96,1024]{1,0:T(8,128)(2,1)S(1)}, u32[]{:S(2)}, u32[]{:S(2)}) %collective-permute-start.31) | collective-permute-done | bytes 196640 | tf_op jit(solution)/shard_map/ppermute | solution.py:41
  479.9 6.5 %collective-permute-done.32 = bf16[96,1024]{1,0:T(8,128)(2,1)S(1)} collective-permute-done((bf16[96,1024]{1,0:T(8,128)(2,1)S(1)}, bf16[96,1024]{1,0:T(8,128)(2,1)S(1)}, u32[]{:S(2)}, u32[]{:S(2)}) %collective-permute-start.32) | collective-permute-done | bytes 196640 | tf_op jit(solution)/shard_map/ppermute | solution.py:41
  (403 shorter events, 145.9 us)
Async XLA Ops:
  0.6 8.9 %copy-start.20 = (bf16[1024,768]{1,0:T(8,128)(2,1)S(1)}, bf16[1024,768]{1,0:T(8,128)(2,1)}, u32[]{:S(2)}) copy-start(bf16[1024,768]{1,0:T(8,128)(2,1)} %param.21) | copy-start | bytes 4718596
  3.2 10.6 %collective-permute-start = (bf16[48,640]{1,0:T(8,128)(2,1)}, bf16[48,640]{1,0:T(8,128)(2,1)}, u32[]{:S(2)}, u32[]{:S(2)}) collective-permute-start(bf16[48,640]{1,0:T(8,128)(2,1)} %get-tuple-element.61), channel_id=1, source_target_pairs={{0,2},{1,3},{2,0},{3,1},{4,6},{5,7},{6,4},{7,5},{8,10},{9,11},{10,... | collective-permute-start | bytes 184328 | tf_op jit(solution)/shard_map/ppermute | solution.py:41
  3.7 8.5 %copy-start.53 = (bf16[1024,768]{1,0:T(8,128)(2,1)S(1)}, bf16[1024,768]{1,0:T(8,128)(2,1)}, u32[]{:S(2)}) copy-start(bf16[1024,768]{1,0:T(8,128)(2,1)} %param.11) | copy-start | bytes 4718596
  5.5 16.8 %collective-permute-start.14 = (bf16[48,768]{1,0:T(8,128)(2,1)}, bf16[48,768]{1,0:T(8,128)(2,1)}, u32[]{:S(2)}, u32[]{:S(2)}) collective-permute-start(bf16[48,768]{1,0:T(8,128)(2,1)} %get-tuple-element.106), channel_id=1, source_target_pairs={{0,2},{1,3},{2,0},{3,1},{4,6},{5,7},{6,4},{7,5},{8,10},{9,11},{10,... | collective-permute-start | bytes 221192 | tf_op jit(solution)/shard_map/ppermute | solution.py:41
  7.3 17.8 %collective-permute-start.7 = (bf16[48,1024]{1,0:T(8,128)(2,1)}, bf16[48,1024]{1,0:T(8,128)(2,1)S(1)}, u32[]{:S(2)}, u32[]{:S(2)}) collective-permute-start(bf16[48,1024]{1,0:T(8,128)(2,1)} %get-tuple-element.111), channel_id=1, source_target_pairs={{0,2},{1,3},{2,0},{3,1},{4,6},{5,7},{6,4},{7,5},{8,10},{9,11},{10,... | collective-permute-start | bytes 294920 | tf_op jit(solution)/shard_map/ppermute | solution.py:41
  11.5 9.8 %copy-start.61 = (bf16[1,48,640]{2,1,0:T(8,128)(2,1)S(1)}, bf16[1,48,640]{2,1,0:T(8,128)(2,1)}, u32[]{:S(2)}) copy-start(bf16[1,48,640]{2,1,0:T(8,128)(2,1)} %get-tuple-element.114) | copy-start | bytes 184324
  11.5 10.8 %copy-start.66 = (bf16[48,768]{1,0:T(8,128)(2,1)S(1)}, bf16[48,768]{1,0:T(8,128)(2,1)}, u32[]{:S(2)}) copy-start(bf16[48,768]{1,0:T(8,128)(2,1)} %get-tuple-element.104) | copy-start | bytes 221188
  11.5 10.8 %copy-start.67 = (bf16[48,768]{1,0:T(8,128)(2,1)S(1)}, bf16[48,768]{1,0:T(8,128)(2,1)}, u32[]{:S(2)}) copy-start(bf16[48,768]{1,0:T(8,128)(2,1)} %get-tuple-element.108) | copy-start | bytes 221188
  11.5 12.5 %copy-start.57 = (bf16[1,48,768]{2,1,0:T(8,128)(2,1)S(1)}, bf16[1,48,768]{2,1,0:T(8,128)(2,1)}, u32[]{:S(2)}) copy-start(bf16[1,48,768]{2,1,0:T(8,128)(2,1)} %get-tuple-element.105) | copy-start | bytes 221188
  11.5 12.5 %copy-start.58 = (bf16[1,48,768]{2,1,0:T(8,128)(2,1)S(1)}, bf16[1,48,768]{2,1,0:T(8,128)(2,1)}, u32[]{:S(2)}) copy-start(bf16[1,48,768]{2,1,0:T(8,128)(2,1)} %get-tuple-element.107) | copy-start | bytes 221188
  11.5 14.0 %copy-start.65 = (bf16[48,1024]{1,0:T(8,128)(2,1)S(1)}, bf16[48,1024]{1,0:T(8,128)(2,1)}, u32[]{:S(2)}) copy-start(bf16[48,1024]{1,0:T(8,128)(2,1)} %get-tuple-element.109) | copy-start | bytes 294916
  14.8 23.6 %collective-permute-start.3 = (bf16[96,640]{1,0:T(8,128)(2,1)S(1)}, bf16[96,640]{1,0:T(8,128)(2,1)S(1)}, u32[]{:S(2)}, u32[]{:S(2)}) collective-permute-start(bf16[96,640]{1,0:T(8,128)(2,1)S(1)} %maximum_select_fusion.12), channel_id=1, source_target_pairs={{0,8},{1,9},{2,10},{3,11},{4,12},{5,13},{6,14},{7,15},{8,16},{9,17... | collective-permute-start | bytes 368648 | tf_op jit(solution)/shard_map/ppermute | solution.py:41
  17.4 13.2 %collective-permute-start.2 = (bf16[96,640]{1,0:T(8,128)(2,1)S(1)}, bf16[96,640]{1,0:T(8,128)(2,1)S(1)}, u32[]{:S(2)}, u32[]{:S(2)}) collective-permute-start(bf16[96,640]{1,0:T(8,128)(2,1)S(1)} %maximum_select_fusion.12), channel_id=1, source_target_pairs={{0,16},{1,17},{2,18},{3,19},{4,20},{5,21},{6,22},{7,23},{8,24},{9,... | collective-permute-start | bytes 368648 | tf_op jit(solution)/shard_map/ppermute | solution.py:41
  20.0 6.4 %collective-permute-start.1 = (bf16[96,640]{1,0:T(8,128)(2,1)S(1)}, bf16[96,640]{1,0:T(8,128)(2,1)S(1)}, u32[]{:S(2)}, u32[]{:S(2)}) collective-permute-start(bf16[96,640]{1,0:T(8,128)(2,1)S(1)} %maximum_select_fusion.12), channel_id=1, source_target_pairs={{0,24},{1,25},{2,26},{3,27},{4,28},{5,29},{6,30},{7,31},{8,0},{9,1... | collective-permute-start | bytes 368648 | tf_op jit(solution)/shard_map/ppermute | solution.py:41
  23.3 26.5 %collective-permute-start.17 = (bf16[96,768]{1,0:T(8,128)(2,1)S(1)}, bf16[96,768]{1,0:T(8,128)(2,1)S(1)}, u32[]{:S(2)}, u32[]{:S(2)}) collective-permute-start(bf16[96,768]{1,0:T(8,128)(2,1)S(1)} %maximum_select_fusion.10), channel_id=1, source_target_pairs={{0,8},{1,9},{2,10},{3,11},{4,12},{5,13},{6,14},{7,15},{8,16},{9,17... | collective-permute-start | bytes 442376 | tf_op jit(solution)/shard_map/ppermute | solution.py:41
  25.1 23.1 %collective-permute-start.16 = (bf16[96,768]{1,0:T(8,128)(2,1)S(1)}, bf16[96,768]{1,0:T(8,128)(2,1)S(1)}, u32[]{:S(2)}, u32[]{:S(2)}) collective-permute-start(bf16[96,768]{1,0:T(8,128)(2,1)S(1)} %maximum_select_fusion.10), channel_id=1, source_target_pairs={{0,16},{1,17},{2,18},{3,19},{4,20},{5,21},{6,22},{7,23},{8,24},{9,... | collective-permute-start | bytes 442376 | tf_op jit(solution)/shard_map/ppermute | solution.py:41
  26.3 21.8 %collective-permute-start.15 = (bf16[96,768]{1,0:T(8,128)(2,1)S(1)}, bf16[96,768]{1,0:T(8,128)(2,1)S(1)}, u32[]{:S(2)}, u32[]{:S(2)}) collective-permute-start(bf16[96,768]{1,0:T(8,128)(2,1)S(1)} %maximum_select_fusion.10), channel_id=1, source_target_pairs={{0,24},{1,25},{2,26},{3,27},{4,28},{5,29},{6,30},{7,31},{8,0},{9,1... | collective-permute-start | bytes 442376 | tf_op jit(solution)/shard_map/ppermute | solution.py:41
  30.6 30.2 %collective-permute-start.10 = (bf16[96,1024]{1,0:T(8,128)(2,1)S(1)}, bf16[96,1024]{1,0:T(8,128)(2,1)S(1)}, u32[]{:S(2)}, u32[]{:S(2)}) collective-permute-start(bf16[96,1024]{1,0:T(8,128)(2,1)S(1)} %maximum_select_fusion.8), channel_id=1, source_target_pairs={{0,8},{1,9},{2,10},{3,11},{4,12},{5,13},{6,14},{7,15},{8,16},{9,17... | collective-permute-start | bytes 589832 | tf_op jit(solution)/shard_map/ppermute | solution.py:41
  38.4 22.5 %collective-permute-start.9 = (bf16[96,1024]{1,0:T(8,128)(2,1)S(1)}, bf16[96,1024]{1,0:T(8,128)(2,1)S(1)}, u32[]{:S(2)}, u32[]{:S(2)}) collective-permute-start(bf16[96,1024]{1,0:T(8,128)(2,1)S(1)} %maximum_select_fusion.8), channel_id=1, source_target_pairs={{0,16},{1,17},{2,18},{3,19},{4,20},{5,21},{6,22},{7,23},{8,24},{9,... | collective-permute-start | bytes 589832 | tf_op jit(solution)/shard_map/ppermute | solution.py:41
  48.2 12.7 %collective-permute-start.8 = (bf16[96,1024]{1,0:T(8,128)(2,1)S(1)}, bf16[96,1024]{1,0:T(8,128)(2,1)S(1)}, u32[]{:S(2)}, u32[]{:S(2)}) collective-permute-start(bf16[96,1024]{1,0:T(8,128)(2,1)S(1)} %maximum_select_fusion.8), channel_id=1, source_target_pairs={{0,24},{1,25},{2,26},{3,27},{4,28},{5,29},{6,30},{7,31},{8,0},{9,1... | collective-permute-start | bytes 589832 | tf_op jit(solution)/shard_map/ppermute | solution.py:41
  48.2 14.4 %collective-permute-start.4 = (bf16[4,96,640]{2,1,0:T(8,128)(2,1)S(1)}, bf16[4,96,640]{2,1,0:T(8,128)(2,1)S(1)}, u32[]{:S(2)}, u32[]{:S(2)}) collective-permute-start(bf16[4,96,640]{2,1,0:T(8,128)(2,1)S(1)} %constant_dynamic-slice_fusion.8), channel_id=1, source_target_pairs={{0,4},{1,5},{2,3},{3,2},{4,0},{5,1},{6,7},{7,6},{8,12},{9,13},{10,... | collective-permute-start | bytes 1474568 | tf_op jit(solution)/shard_map/ppermute | solution.py:41
  61.1 20.0 %collective-permute-start.11 = (bf16[4,96,1024]{2,1,0:T(8,128)(2,1)S(1)}, bf16[4,96,1024]{2,1,0:T(8,128)(2,1)S(1)}, u32[]{:S(2)}, u32[]{:S(2)}) collective-permute-start(bf16[4,96,1024]{2,1,0:T(8,128)(2,1)S(1)} %constant_dynamic-slice_fusion.7), channel_id=1, source_target_pairs={{0,4},{1,5},{2,3},{3,2},{4,0},{5,1},{6,7},{7,6},{8,12},{9,13},{10,... | collective-permute-start | bytes 2359304 | tf_op jit(solution)/shard_map/ppermute | solution.py:41
  62.8 24.8 %collective-permute-start.5 = (bf16[2,4,96,640]{3,2,1,0:T(8,128)(2,1)S(1)}, bf16[2,4,96,640]{3,2,1,0:T(8,128)(2,1)S(1)}, u32[]{:S(2)}, u32[]{:S(2)}) collective-permute-start(bf16[2,4,96,640]{3,2,1,0:T(8,128)(2,1)S(1)} %maximum_select_fusion.6), channel_id=1, source_target_pairs={{0,1},{1,0},{2,6},{3,7},{4,5},{5,4},{6,2},{7,3},{8,9},{9,8},{10,14... | collective-permute-start | bytes 2949128 | tf_op jit(solution)/shard_map/ppermute | solution.py:41
  64.5 29.2 %collective-permute-start.18 = (bf16[4,96,768]{2,1,0:T(8,128)(2,1)S(1)}, bf16[4,96,768]{2,1,0:T(8,128)(2,1)S(1)}, u32[]{:S(2)}, u32[]{:S(2)}) collective-permute-start(bf16[4,96,768]{2,1,0:T(8,128)(2,1)S(1)} %constant_dynamic-slice_fusion.6), channel_id=1, source_target_pairs={{0,4},{1,5},{2,3},{3,2},{4,0},{5,1},{6,7},{7,6},{8,12},{9,13},{10,... | collective-permute-start | bytes 1769480 | tf_op jit(solution)/shard_map/ppermute | solution.py:41
  81.3 39.8 %collective-permute-start.12 = (bf16[2,4,96,1024]{3,2,0,1:T(8,128)(2,1)S(1)}, bf16[2,4,96,1024]{3,2,0,1:T(8,128)(2,1)S(1)}, u32[]{:S(2)}, u32[]{:S(2)}) collective-permute-start(bf16[2,4,96,1024]{3,2,0,1:T(8,128)(2,1)S(1)} %maximum_select_fusion.3), channel_id=1, source_target_pairs={{0,1},{1,0},{2,6},{3,7},{4,5},{5,4},{6,2},{7,3},{8,9},{9,8},{10,14... | collective-permute-start | bytes 4718600 | tf_op jit(solution)/shard_map/ppermute | solution.py:41
  87.9 35.4 %collective-permute-start.6 = (bf16[2,2,4,96,640]{4,3,2,1,0:T(8,128)(2,1)S(1)}, bf16[2,2,4,96,640]{4,3,2,1,0:T(8,128)(2,1)S(1)}, u32[]{:S(2)}, u32[]{:S(2)}) collective-permute-start(bf16[2,2,4,96,640]{4,3,2,1,0:T(8,128)(2,1)S(1)} %maximum_select_fusion.2), channel_id=1, source_target_pairs={{0,2},{1,3},{2,0},{3,1},{4,6},{5,7},{6,4},{7,5},{8,10},{9,11},{10,... | collective-permute-start | bytes 5898248 | tf_op jit(solution)/shard_map/ppermute | solution.py:41
  93.8 24.7 %collective-permute-start.19 = (bf16[2,4,96,768]{3,2,0,1:T(8,128)(2,1)S(1)}, bf16[2,4,96,768]{3,2,0,1:T(8,128)(2,1)S(1)}, u32[]{:S(2)}, u32[]{:S(2)}) collective-permute-start(bf16[2,4,96,768]{3,2,0,1:T(8,128)(2,1)S(1)} %maximum_select_fusion.4), channel_id=1, source_target_pairs={{0,1},{1,0},{2,6},{3,7},{4,5},{5,4},{6,2},{7,3},{8,9},{9,8},{10,14... | collective-permute-start | bytes 3538952 | tf_op jit(solution)/shard_map/ppermute | solution.py:41
  120.3 64.8 %collective-permute-start.20 = (bf16[2,2,4,96,768]{4,3,1,2,0:T(8,128)(2,1)}, bf16[2,2,4,96,768]{4,3,1,2,0:T(8,128)(2,1)}, u32[]{:S(2)}, u32[]{:S(2)}) collective-permute-start(bf16[2,2,4,96,768]{4,3,1,2,0:T(8,128)(2,1)} %maximum_select_fusion.1), channel_id=1, source_target_pairs={{0,2},{1,3},{2,0},{3,1},{4,6},{5,7},{6,4},{7,5},{8,10},{9,11},{10,... | collective-permute-start | bytes 7077896 | tf_op jit(solution)/shard_map/ppermute | solution.py:41
  123.3 63.9 %collective-permute-start.13 = (bf16[2,2,4,96,1024]{4,3,1,2,0:T(8,128)(2,1)}, bf16[2,2,4,96,1024]{4,3,1,2,0:T(8,128)(2,1)}, u32[]{:S(2)}, u32[]{:S(2)}) collective-permute-start(bf16[2,2,4,96,1024]{4,3,1,2,0:T(8,128)(2,1)} %maximum_select_fusion), channel_id=1, source_target_pairs={{0,2},{1,3},{2,0},{3,1},{4,6},{5,7},{6,4},{7,5},{8,10},{9,11},{10,... | collective-permute-start | bytes 9437192 | tf_op jit(solution)/shard_map/ppermute | solution.py:41
  143.1 12.7 %copy-start.29 = (bf16[2,512,6,64]{1,0,3,2:T(2,128)(2,1)}, bf16[2,512,6,64]{1,0,3,2:T(2,128)(2,1)S(1)}, u32[]{:S(2)}) copy-start(bf16[2,512,6,64]{1,0,3,2:T(2,128)(2,1)S(1)} %reshape.539) | copy-start | bytes 2359300
  172.2 8.7 %copy-start.31 = (bf16[2,512,6,64]{1,0,3,2:T(2,128)(2,1)}, bf16[2,512,6,64]{1,0,3,2:T(2,128)(2,1)S(1)}, u32[]{:S(2)}) copy-start(bf16[2,512,6,64]{1,0,3,2:T(2,128)(2,1)S(1)} %reshape.534) | copy-start | bytes 2359300
  174.6 16.5 %copy-start.38 = (bf16[48,8,2,512]{3,1,2,0:T(8,128)(2,1)}, bf16[48,8,2,512]{3,1,2,0:T(8,128)(2,1)S(1)}, u32[]{:S(2)}) copy-start(bf16[48,8,2,512]{3,1,2,0:T(8,128)(2,1)S(1)} %copy.202) | copy-start | bytes 2359300
  181.8 10.3 %copy-start.35 = (bf16[48,8,2,512]{3,1,2,0:T(8,128)(2,1)}, bf16[48,8,2,512]{3,1,2,0:T(8,128)(2,1)S(1)}, u32[]{:S(2)}) copy-start(bf16[48,8,2,512]{3,1,2,0:T(8,128)(2,1)S(1)} %copy.201) | copy-start | bytes 2359300
  194.5 61.9 %copy-start.56 = (bf16[1024,768]{0,1:T(8,128)(2,1)}, bf16[1024,768]{0,1:T(8,128)(2,1)S(1)}, u32[]{:S(2)}) copy-start(bf16[1024,768]{0,1:T(8,128)(2,1)S(1)} %fusion.43) | copy-start | bytes 4718596
  294.5 16.9 %slice-start.3 = ((s8[12582912]{0:T(1024)(128)(4,1)}), s8[4194304]{0:T(1024)(128)(4,1)S(1)}, s32[]{:S(2)}) async-start(s8[12582912]{0:T(1024)(128)(4,1)} %bitcast.381), calls=%async_computation.3 | async-start | bytes 8388608
  294.5 16.9 %slice-start.4 = ((s8[12582912]{0:T(1024)(128)(4,1)}), s8[4194304]{0:T(1024)(128)(4,1)S(1)}, s32[]{:S(2)}) async-start(s8[12582912]{0:T(1024)(128)(4,1)} %bitcast.381), calls=%async_computation.4 | async-start | bytes 8388608
  302.4 9.0 %slice-start.5 = ((s8[12582912]{0:T(1024)(128)(4,1)}), s8[4194304]{0:T(1024)(128)(4,1)S(1)}, s32[]{:S(2)}) async-start(s8[12582912]{0:T(1024)(128)(4,1)} %bitcast.381), calls=%async_computation.5 | async-start | bytes 8388608
  329.1 15.9 %slice-start = ((s8[12582912]{0:T(1024)(128)(4,1)}), s8[4194304]{0:T(1024)(128)(4,1)S(1)}, s32[]{:S(2)}) async-start(s8[12582912]{0:T(1024)(128)(4,1)} %bitcast.379), calls=%async_computation | async-start | bytes 8388608
  329.1 15.9 %slice-start.1 = ((s8[12582912]{0:T(1024)(128)(4,1)}), s8[4194304]{0:T(1024)(128)(4,1)S(1)}, s32[]{:S(2)}) async-start(s8[12582912]{0:T(1024)(128)(4,1)} %bitcast.379), calls=%async_computation.1 | async-start | bytes 8388608
  336.1 8.9 %slice-start.2 = ((s8[12582912]{0:T(1024)(128)(4,1)}), s8[4194304]{0:T(1024)(128)(4,1)S(1)}, s32[]{:S(2)}) async-start(s8[12582912]{0:T(1024)(128)(4,1)} %bitcast.379), calls=%async_computation.2 | async-start | bytes 8388608
  373.1 14.0 %collective-permute-start.21 = (bf16[2,768,640]{2,1,0:T(8,128)(2,1)}, bf16[2,768,640]{2,1,0:T(8,128)(2,1)}, u32[]{:S(2)}, u32[]{:S(2)}) collective-permute-start(bf16[2,768,640]{2,1,0:T(8,128)(2,1)} %broadcast_select_fusion.4), channel_id=1, source_target_pairs={{0,2},{1,3},{2,0},{3,1},{4,6},{5,7},{6,4},{7,5},{8,10},{9,11},{10,... | collective-permute-start | bytes 5898248 | tf_op jit(solution)/shard_map/ppermute | solution.py:41
  376.6 18.5 %collective-permute-start.35 = (bf16[2,768,768]{2,1,0:T(8,128)(2,1)}, bf16[2,768,768]{2,1,0:T(8,128)(2,1)}, u32[]{:S(2)}, u32[]{:S(2)}) collective-permute-start(bf16[2,768,768]{2,1,0:T(8,128)(2,1)} %broadcast_select_fusion.2), channel_id=1, source_target_pairs={{0,2},{1,3},{2,0},{3,1},{4,6},{5,7},{6,4},{7,5},{8,10},{9,11},{10,... | collective-permute-start | bytes 7077896 | tf_op jit(solution)/shard_map/ppermute | solution.py:41
  387.1 20.4 %collective-permute-start.28 = (bf16[2,768,1024]{2,1,0:T(8,128)(2,1)}, bf16[2,768,1024]{2,1,0:T(8,128)(2,1)}, u32[]{:S(2)}, u32[]{:S(2)}) collective-permute-start(bf16[2,768,1024]{2,1,0:T(8,128)(2,1)} %broadcast_select_fusion), channel_id=1, source_target_pairs={{0,2},{1,3},{2,0},{3,1},{4,6},{5,7},{6,4},{7,5},{8,10},{9,11},{10,... | collective-permute-start | bytes 9437192 | tf_op jit(solution)/shard_map/ppermute | solution.py:41
  390.5 14.2 %collective-permute-start.22 = (bf16[2,4,96,640]{3,2,0,1:T(8,128)(2,1)S(1)}, bf16[2,4,96,640]{3,2,0,1:T(8,128)(2,1)S(1)}, u32[]{:S(2)}, u32[]{:S(2)}) collective-permute-start(bf16[2,4,96,640]{3,2,0,1:T(8,128)(2,1)S(1)} %bitcast_select_fusion.4), channel_id=1, source_target_pairs={{0,1},{1,0},{2,6},{3,7},{4,5},{5,4},{6,2},{7,3},{8,9},{9,8},{10,14... | collective-permute-start | bytes 2949128 | tf_op jit(solution)/shard_map/ppermute | solution.py:41
  398.8 8.7 %copy-start.6 = (bf16[1,768,2048]{2,1,0:T(8,128)(2,1)S(1)}, bf16[1,768,2048]{2,1,0:T(8,128)(2,1)}, u32[]{:S(2)}) copy-start(bf16[1,768,2048]{2,1,0:T(8,128)(2,1)} %copy-done.5) | copy-start | bytes 9437188
  399.9 29.1 %collective-permute-start.36 = (bf16[2,4,96,768]{3,2,0,1:T(8,128)(2,1)}, bf16[2,4,96,768]{3,2,0,1:T(8,128)(2,1)}, u32[]{:S(2)}, u32[]{:S(2)}) collective-permute-start(bf16[2,4,96,768]{3,2,0,1:T(8,128)(2,1)} %bitcast_select_fusion.2), channel_id=1, source_target_pairs={{0,1},{1,0},{2,6},{3,7},{4,5},{5,4},{6,2},{7,3},{8,9},{9,8},{10,14... | collective-permute-start | bytes 3538952 | tf_op jit(solution)/shard_map/ppermute | solution.py:41
  405.9 19.3 %collective-permute-start.23 = (bf16[4,96,640]{2,1,0:T(8,128)(2,1)}, bf16[4,96,640]{2,1,0:T(8,128)(2,1)}, u32[]{:S(2)}, u32[]{:S(2)}) collective-permute-start(bf16[4,96,640]{2,1,0:T(8,128)(2,1)} %dynamic-slice_bitcast_fusion.2), channel_id=1, source_target_pairs={{0,4},{1,5},{2,3},{3,2},{4,0},{5,1},{6,7},{7,6},{8,12},{9,13},{10,... | collective-permute-start | bytes 1474568 | tf_op jit(solution)/shard_map/ppermute | solution.py:41
  414.8 26.2 %collective-permute-start.29 = (bf16[2,4,96,1024]{3,2,0,1:T(8,128)(2,1)}, bf16[2,4,96,1024]{3,2,0,1:T(8,128)(2,1)}, u32[]{:S(2)}, u32[]{:S(2)}) collective-permute-start(bf16[2,4,96,1024]{3,2,0,1:T(8,128)(2,1)} %bitcast_select_fusion), channel_id=1, source_target_pairs={{0,1},{1,0},{2,6},{3,7},{4,5},{5,4},{6,2},{7,3},{8,9},{9,8},{10,14... | collective-permute-start | bytes 4718600 | tf_op jit(solution)/shard_map/ppermute | solution.py:41
  426.6 6.6 %collective-permute-start.24 = (bf16[96,640]{1,0:T(8,128)(2,1)S(1)}, bf16[96,640]{1,0:T(8,128)(2,1)S(1)}, u32[]{:S(2)}, u32[]{:S(2)}) collective-permute-start(bf16[96,640]{1,0:T(8,128)(2,1)S(1)} %get-tuple-element.95), channel_id=1, source_target_pairs={{0,24},{1,25},{2,26},{3,27},{4,28},{5,29},{6,30},{7,31},{8,0},{9,1... | collective-permute-start | bytes 368648 | tf_op jit(solution)/shard_map/ppermute | solution.py:41
  428.4 6.9 %collective-permute-start.26 = (bf16[96,640]{1,0:T(8,128)(2,1)S(1)}, bf16[96,640]{1,0:T(8,128)(2,1)S(1)}, u32[]{:S(2)}, u32[]{:S(2)}) collective-permute-start(bf16[96,640]{1,0:T(8,128)(2,1)S(1)} %get-tuple-element.96), channel_id=1, source_target_pairs={{0,8},{1,9},{2,10},{3,11},{4,12},{5,13},{6,14},{7,15},{8,16},{9,17... | collective-permute-start | bytes 368648 | tf_op jit(solution)/shard_map/ppermute | solution.py:41
  428.7 10.8 %collective-permute-start.25 = (bf16[96,640]{1,0:T(8,128)(2,1)S(1)}, bf16[96,640]{1,0:T(8,128)(2,1)S(1)}, u32[]{:S(2)}, u32[]{:S(2)}) collective-permute-start(bf16[96,640]{1,0:T(8,128)(2,1)S(1)} %get-tuple-element.97), channel_id=1, source_target_pairs={{0,16},{1,17},{2,18},{3,19},{4,20},{5,21},{6,22},{7,23},{8,24},{9,... | collective-permute-start | bytes 368648 | tf_op jit(solution)/shard_map/ppermute | solution.py:41
  429.0 12.0 %copy-start.8 = (bf16[2,768,1024]{2,1,0:T(8,128)(2,1)S(1)}, bf16[2,768,1024]{2,1,0:T(8,128)(2,1)}, u32[]{:S(2)}) copy-start(bf16[2,768,1024]{2,1,0:T(8,128)(2,1)} %copy-done.7) | copy-start | bytes 9437188
  429.0 12.0 %copy-start.24 = (bf16[2,4,1,96,1024]{4,3,2,1,0:T(8,128)(2,1)S(1)}, bf16[2,4,1,96,1024]{4,3,2,1,0:T(8,128)(2,1)}, u32[]{:S(2)}) copy-start(bf16[2,4,1,96,1024]{4,3,2,1,0:T(8,128)(2,1)} %get-tuple-element.71) | copy-start | bytes 4718596
  439.6 1.4 collective-permute-start.27
  439.7 9.9 %collective-permute-start.37 = (bf16[4,96,768]{2,1,0:T(8,128)(2,1)S(1)}, bf16[4,96,768]{2,1,0:T(8,128)(2,1)S(1)}, u32[]{:S(2)}, u32[]{:S(2)}) collective-permute-start(bf16[4,96,768]{2,1,0:T(8,128)(2,1)S(1)} %dynamic-slice_bitcast_fusion.1), channel_id=1, source_target_pairs={{0,4},{1,5},{2,3},{3,2},{4,0},{5,1},{6,7},{7,6},{8,12},{9,13},{10,... | collective-permute-start | bytes 1769480 | tf_op jit(solution)/shard_map/ppermute | solution.py:41
  444.5 21.8 %collective-permute-start.30 = (bf16[4,96,1024]{2,1,0:T(8,128)(2,1)}, bf16[4,96,1024]{2,1,0:T(8,128)(2,1)S(1)}, u32[]{:S(2)}, u32[]{:S(2)}) collective-permute-start(bf16[4,96,1024]{2,1,0:T(8,128)(2,1)} %dynamic-slice_bitcast_fusion), channel_id=1, source_target_pairs={{0,4},{1,5},{2,3},{3,2},{4,0},{5,1},{6,7},{7,6},{8,12},{9,13},{10,... | collective-permute-start | bytes 2359304 | tf_op jit(solution)/shard_map/ppermute | solution.py:41
  450.6 8.9 %collective-permute-start.38 = (bf16[96,768]{1,0:T(8,128)(2,1)}, bf16[96,768]{1,0:T(8,128)(2,1)}, u32[]{:S(2)}, u32[]{:S(2)}) collective-permute-start(bf16[96,768]{1,0:T(8,128)(2,1)} %get-tuple-element.90), channel_id=1, source_target_pairs={{0,24},{1,25},{2,26},{3,27},{4,28},{5,29},{6,30},{7,31},{8,0},{9,1... | collective-permute-start | bytes 442376 | tf_op jit(solution)/shard_map/ppermute | solution.py:41
  452.2 8.9 %collective-permute-start.40 = (bf16[96,768]{1,0:T(8,128)(2,1)}, bf16[96,768]{1,0:T(8,128)(2,1)}, u32[]{:S(2)}, u32[]{:S(2)}) collective-permute-start(bf16[96,768]{1,0:T(8,128)(2,1)} %get-tuple-element.91), channel_id=1, source_target_pairs={{0,8},{1,9},{2,10},{3,11},{4,12},{5,13},{6,14},{7,15},{8,16},{9,17... | collective-permute-start | bytes 442376 | tf_op jit(solution)/shard_map/ppermute | solution.py:41
  452.6 12.4 %collective-permute-start.39 = (bf16[96,768]{1,0:T(8,128)(2,1)}, bf16[96,768]{1,0:T(8,128)(2,1)}, u32[]{:S(2)}, u32[]{:S(2)}) collective-permute-start(bf16[96,768]{1,0:T(8,128)(2,1)} %get-tuple-element.92), channel_id=1, source_target_pairs={{0,16},{1,17},{2,18},{3,19},{4,20},{5,21},{6,22},{7,23},{8,24},{9,... | collective-permute-start | bytes 442376 | tf_op jit(solution)/shard_map/ppermute | solution.py:41
  466.2 4.3 collective-permute-start.41
  466.7 13.3 %collective-permute-start.31 = (bf16[96,1024]{1,0:T(8,128)(2,1)S(1)}, bf16[96,1024]{1,0:T(8,128)(2,1)S(1)}, u32[]{:S(2)}, u32[]{:S(2)}) collective-permute-start(bf16[96,1024]{1,0:T(8,128)(2,1)S(1)} %get-tuple-element.87), channel_id=1, source_target_pairs={{0,24},{1,25},{2,26},{3,27},{4,28},{5,29},{6,30},{7,31},{8,0},{9,1... | collective-permute-start | bytes 589832 | tf_op jit(solution)/shard_map/ppermute | solution.py:41
  469.8 10.1 %collective-permute-start.33 = (bf16[96,1024]{1,0:T(8,128)(2,1)S(1)}, bf16[96,1024]{1,0:T(8,128)(2,1)S(1)}, u32[]{:S(2)}, u32[]{:S(2)}) collective-permute-start(bf16[96,1024]{1,0:T(8,128)(2,1)S(1)} %get-tuple-element.88), channel_id=1, source_target_pairs={{0,8},{1,9},{2,10},{3,11},{4,12},{5,13},{6,14},{7,15},{8,16},{9,17... | collective-permute-start | bytes 589832 | tf_op jit(solution)/shard_map/ppermute | solution.py:41
  469.8 16.6 %collective-permute-start.32 = (bf16[96,1024]{1,0:T(8,128)(2,1)S(1)}, bf16[96,1024]{1,0:T(8,128)(2,1)S(1)}, u32[]{:S(2)}, u32[]{:S(2)}) collective-permute-start(bf16[96,1024]{1,0:T(8,128)(2,1)S(1)} %get-tuple-element.89), channel_id=1, source_target_pairs={{0,16},{1,17},{2,18},{3,19},{4,20},{5,21},{6,22},{7,23},{8,24},{9,... | collective-permute-start | bytes 589832 | tf_op jit(solution)/shard_map/ppermute | solution.py:41
  486.6 1.5 collective-permute-start.34
  (66 other events, 250.0 us)

commit v3 on v2

v3 whole, which is shorter than its diff:
```python
import jax
import jax.numpy as jnp
from jax import lax
from jax.experimental import pallas as pl
from jax.experimental.pallas import tpu as pltpu
from jax.sharding import PartitionSpec as P

HDIM = 64
SEQ = 512
LANES = 128
VMEM = 56 * 1024 * 1024
epsilon = 1e-05

AXES = ("dp", "tensor")
ZS = 4


def place(z, x, c, y):
    return ((z * 2 + x) * 2 + c) * 2 + y


def pairs(move):
    found = []
    for z in range(ZS):
        for x in range(2):
            for c in range(2):
                for y in range(2):
                    found.append((place(z, x, c, y), place(*move(z, x, c, y))))
    return found


TO_CORE = pairs(lambda z, x, c, y: (z, x, 1 - c, y))
TO_NEAR = pairs(lambda z, x, c, y: (z, x, c, 1 - y) if c else (z, 1 - x, c, y))
TO_FAR = pairs(lambda z, x, c, y: (z, 1 - x, c, y) if c else (z, x, c, 1 - y))
TO_DEPTH = [pairs(lambda z, x, c, y: ((z - k) % ZS, x, c, y)) for k in range(ZS)]


def coords():
    d = lax.axis_index("dp")
    y = lax.axis_index("tensor")
    return d // 4, (d // 2) % 2, d % 2, y


def send(value, route):
    return lax.ppermute(value, AXES, route)


def in_order(own, other, at):
    return jnp.where(at == 0, jnp.stack([own, other]), jnp.stack([other, own]))


def tuned():
    return lax.axis_size("dp") == 16 and lax.axis_size("tensor") == 2


def tie(*values):
    return lax.optimization_barrier(values)


def gather_steps(left, right):
    if not tuned():
        for _ in range(4):
            left = yield left
        full = lax.all_gather(jnp.concatenate([left, right], axis=1), ("tensor", "dp"), axis=0, tiled=True)
        full = full.reshape(lax.axis_size("tensor"), -1, full.shape[1])
        yield tuple(jnp.split(full, 2, axis=2))
        return
    z, x, c, y = coords()
    first = c == 0
    got = send(jnp.where(first, right, left), TO_CORE)
    mine = jnp.where(first, jnp.concatenate([left, got]), jnp.concatenate([got, right]))
    mine = yield mine
    own = [mine] + [send(mine, TO_DEPTH[k]) for k in (1, 2, 3)]
    column = jnp.stack(own + own[:3])
    column = lax.dynamic_slice_in_dim(column, (ZS - z) % ZS, ZS, 0)
    column = yield column
    near = send(column, TO_NEAR)
    plane = in_order(column, near, jnp.where(first, x, y))
    plane = yield plane
    far = send(plane, TO_FAR)
    whole = in_order(plane, far, jnp.where(first, y, x))
    whole = yield whole
    sibling = send(whole, TO_CORE)
    full_left = jnp.where(first, whole, sibling)
    full_right = jnp.where(first, sibling, whole)
    n, h = left.shape
    full_left = jnp.transpose(full_left, (0, 2, 1, 3, 4)).reshape(2, 16 * n, h)
    full_right = jnp.transpose(full_right, (1, 2, 0, 3, 4)).reshape(2, 16 * n, h)
    yield full_left, full_right


def add(a, b):
    return a.astype(jnp.float32) + b.astype(jnp.float32)


def scatter_steps(left, right):
    if not tuned():
        for _ in range(4):
            left = yield left
        full = jnp.concatenate([left, right], axis=2)
        full = lax.psum_scatter(
            full.reshape(-1, full.shape[2]), ("tensor", "dp"), scatter_dimension=0, tiled=True
        )
        full = lax.optimization_barrier(full).astype(jnp.float32)
        yield tuple(jnp.split(full, 2, axis=1))
        return
    z, x, c, y = coords()
    first = c == 0
    _, rows, h = left.shape
    n = rows // 16
    got = send(jnp.where(first, right, left), TO_CORE)
    part = low(add(jnp.where(first, left, right), got)).reshape(2, ZS, 2, 2 * n, h)
    part = yield part

    def over_y(i):
        return jnp.transpose(lax.dynamic_index_in_dim(part, i, 0, keepdims=False), (1, 0, 2, 3))

    def over_x(i):
        return lax.dynamic_index_in_dim(part, i, 2, keepdims=False)

    got = send(jnp.where(first, over_y(1 - y), over_x(1 - x)), TO_FAR)
    part = low(add(jnp.where(first, over_y(y), over_x(x)), got))
    part = yield part
    at = jnp.where(first, x, y)
    got = send(lax.dynamic_index_in_dim(part, 1 - at, 0, keepdims=False), TO_NEAR)
    part = low(add(lax.dynamic_index_in_dim(part, at, 0, keepdims=False), got))
    part = yield part

    def depth(k):
        return lax.dynamic_index_in_dim(part, (z - k) % ZS, 0, keepdims=False)

    total = depth(0).astype(jnp.float32)
    for k in (1, 2, 3):
        total = total + send(depth(k), TO_DEPTH[k]).astype(jnp.float32)
    total = total.reshape(2, n, h)
    total = yield total
    keep = lax.dynamic_index_in_dim(total, c, 0, keepdims=False)
    got = send(lax.dynamic_index_in_dim(total, 1 - c, 0, keepdims=False), TO_CORE)
    yield jnp.where(first, keep, got), jnp.where(first, got, keep)


def dot_nn(left, right):
    return lax.dot_general(left, right, (((1,), (0,)), ((), ())), preferred_element_type=jnp.float32)


def dot_tn(left, right):
    return lax.dot_general(left, right, (((0,), (0,)), ((), ())), preferred_element_type=jnp.float32)


def dot_nt(left, right):
    return lax.dot_general(left, right, (((1,), (1,)), ((), ())), preferred_element_type=jnp.float32)


def low(value):
    return value.astype(jnp.bfloat16)


def flip(value):
    return jnp.swapaxes(value, 0, 1)


def pair_cols(left, right, pairs, at):
    start = at * LANES
    width = left.shape[-1]
    if start < width:
        return left[:, start : start + LANES]
    return right[:, start - width : start - width + LANES]


def attend_kernel(x_ref, a_ref, b_ref, row_ref, col_ref, pa_ref, pb_ref, e_ref, att_ref, flat_ref, inv_ref, bias_ref):
    pairs = att_ref.shape[-1] // LANES
    x = x_ref[...]
    pa_ref[0] = low(dot_nn(x, a_ref[0]))
    pb_ref[0] = low(dot_nn(x, b_ref[0]))
    bias_ref[...] = jnp.where(col_ref[0] == row_ref[0], 0.0, -1e30)
    lane = lax.broadcasted_iota(jnp.int32, (SEQ, LANES), 1)
    chunk = SEQ // 2
    left, right = pa_ref[0], pb_ref[0]
    for p in range(pairs):
        queries = pair_cols(left, right, pairs, p)
        key_rows = pair_cols(left, right, pairs, pairs + p)
        values_flat = flip(pair_cols(left, right, pairs, 2 * pairs + p))
        for half in range(2):
            h = 2 * p + half
            own = (lane < HDIM) if half == 0 else (lane >= HDIM)
            chosen = low(jnp.where(own, queries.astype(jnp.float32) * HDIM**-0.5, 0.0))
            value_half = values_flat[half * HDIM : (half + 1) * HDIM]
            for n in range(2):
                cut = slice(n * chunk, (n + 1) * chunk)
                scores = dot_nt(key_rows, chosen[cut]) + bias_ref[:, cut]
                largest = jnp.max(scores, axis=0, keepdims=True)
                weights = jnp.exp(scores - largest)
                inverse = 1.0 / jnp.sum(weights, axis=0, keepdims=True)
                weights = low(weights)
                e_ref[0, 0, h, :, cut] = weights
                inv_ref[0, 0, h : h + 1, cut] = inverse
                flat_ref[0, 0, h * HDIM : (h + 1) * HDIM, cut] = low(dot_nn(value_half, weights) * inverse)
        att_ref[0, :, p * LANES : (p + 1) * LANES] = flip(flat_ref[0, 0, p * LANES : (p + 1) * LANES, :])


def attend(tokens, left, right, numbers, t):
    rows, width = tokens.shape
    seqs = rows // SEQ
    cols = left.shape[2]
    wide = (2 * cols - LANES) // 3
    heads = wide // HDIM
    used = cols - LANES
    bf = jnp.bfloat16
    return pl.pallas_call(
        attend_kernel,
        grid=(seqs,),
        in_specs=[
            pl.BlockSpec((SEQ, width), lambda s: (s, 0)),
            pl.BlockSpec((1, width, cols), lambda s: (t, 0, 0)),
            pl.BlockSpec((1, width, used), lambda s: (t, 0, 0)),
            pl.BlockSpec((1, 1, SEQ), lambda s: (s, 0, 0)),
            pl.BlockSpec((1, SEQ, 1), lambda s: (s, 0, 0)),
        ],
        out_specs=[
            pl.BlockSpec((1, SEQ, cols), lambda s: (0, s, 0)),
            pl.BlockSpec((1, SEQ, used), lambda s: (0, s, 0)),
            pl.BlockSpec((1, 1, heads, SEQ, SEQ), lambda s: (0, s, 0, 0, 0)),
            pl.BlockSpec((1, SEQ, wide), lambda s: (0, s, 0)),
            pl.BlockSpec((1, 1, wide, SEQ), lambda s: (0, s, 0, 0)),
            pl.BlockSpec((1, 1, heads, SEQ), lambda s: (0, s, 0, 0)),
        ],
        out_shape=[
            jax.ShapeDtypeStruct((1, rows, cols), bf),
            jax.ShapeDtypeStruct((1, rows, used), bf),
            jax.ShapeDtypeStruct((1, seqs, heads, SEQ, SEQ), bf),
            jax.ShapeDtypeStruct((1, rows, wide), bf),
            jax.ShapeDtypeStruct((1, seqs, wide, SEQ), bf),
            jax.ShapeDtypeStruct((1, seqs, heads, SEQ), jnp.float32),
        ],
        scratch_shapes=[pltpu.VMEM((SEQ, SEQ), jnp.float32)],
        compiler_params=pltpu.CompilerParams(vmem_limit_bytes=VMEM),
        cost_estimate=pl.CostEstimate(flops=8_000_000_000, bytes_accessed=15_000_000, transcendentals=3_100_000),
        name="attend",
    )(tokens, left, right, numbers.reshape(seqs, 1, SEQ), numbers.reshape(seqs, SEQ, 1))


def attend_back_kernel(g_ref, w_ref, pa_ref, pb_ref, e_ref, flat_ref, inv_ref, da_ref, db_ref, gt_ref):
    wide = flat_ref.shape[2]
    pairs = wide // LANES
    gt_ref[...] = flip(low(dot_nn(g_ref[...], w_ref[...])))
    left, right = pa_ref[0], pb_ref[0]
    lane = lax.broadcasted_iota(jnp.int32, (SEQ, LANES), 1)
    cols = da_ref.shape[2]

    def put(at, value):
        start = at * LANES
        if start < cols:
            da_ref[0, :, start : start + LANES] = value
        else:
            db_ref[0, :, start - cols : start - cols + LANES] = value

    blank = jnp.zeros((HDIM, SEQ), jnp.bfloat16)
    for p in range(pairs):
        queries = pair_cols(left, right, pairs, p)
        key_rows = pair_cols(left, right, pairs, pairs + p)
        value_rows = pair_cols(left, right, pairs, 2 * pairs + p)
        keys_flat = flip(key_rows)
        scaled = []
        for half in range(2):
            h = 2 * p + half
            grads = gt_ref[h * HDIM : (h + 1) * HDIM, :].astype(jnp.float32)
            scaled.append(low(grads * inv_ref[0, 0, h : h + 1, :]))
        grads = flip(jnp.concatenate(scaled, axis=0))
        dq, dk, dv = [], [], []
        for half in range(2):
            h = 2 * p + half
            mine = scaled[half]
            flat = flat_ref[0, 0, h * HDIM : (h + 1) * HDIM, :].astype(jnp.float32)
            centre = jnp.sum(mine.astype(jnp.float32) * flat, axis=0, keepdims=True)
            stacked = [mine, blank] if half == 0 else [blank, mine]
            grad_weights = dot_nn(value_rows, jnp.concatenate(stacked, axis=0))
            weights = e_ref[0, 0, h]
            grad_scores = low(weights.astype(jnp.float32) * (grad_weights - centre))
            dv.append(dot_nn(weights, grads))
            dk.append(dot_nn(grad_scores, queries))
            dq.append(dot_nn(keys_flat[half * HDIM : (half + 1) * HDIM], grad_scores))
        put(p, flip(low(jnp.concatenate(dq, axis=0) * HDIM**-0.5)))
        put(pairs + p, low(jnp.where(lane < HDIM, dk[0], dk[1]) * HDIM**-0.5))
        put(2 * pairs + p, low(jnp.where(lane < HDIM, dv[0], dv[1])))
    db_ref[0, :, cols - LANES :] = jnp.zeros((SEQ, LANES), jnp.bfloat16)


def attend_back(grad_branch, weight_out, kept, t):
    pa, pb, e, att, flat, inv = kept
    rows, width = grad_branch.shape
    seqs = rows // SEQ
    cols, used = pa.shape[2], pb.shape[2]
    heads, wide = e.shape[2], att.shape[2]
    bf = jnp.bfloat16
    return pl.pallas_call(
        attend_back_kernel,
        grid=(seqs,),
        in_specs=[
            pl.BlockSpec((SEQ, width), lambda s: (s, 0)),
            pl.BlockSpec((width, wide), lambda s: (0, t)),
            pl.BlockSpec((1, SEQ, cols), lambda s: (0, s, 0)),
            pl.BlockSpec((1, SEQ, used), lambda s: (0, s, 0)),
            pl.BlockSpec((1, 1, heads, SEQ, SEQ), lambda s: (0, s, 0, 0, 0)),
            pl.BlockSpec((1, 1, wide, SEQ), lambda s: (0, s, 0, 0)),
            pl.BlockSpec((1, 1, heads, SEQ), lambda s: (0, s, 0, 0)),
        ],
        out_specs=[
            pl.BlockSpec((1, SEQ, cols), lambda s: (0, s, 0)),
            pl.BlockSpec((1, SEQ, cols), lambda s: (0, s, 0)),
        ],
        out_shape=[jax.ShapeDtypeStruct((1, rows, cols), bf)] * 2,
        scratch_shapes=[pltpu.VMEM((wide, SEQ), bf)],
        compiler_params=pltpu.CompilerParams(vmem_limit_bytes=VMEM),
        cost_estimate=pl.CostEstimate(flops=8_000_000_000, bytes_accessed=15_000_000, transcendentals=0),
        name="attend_back",
    )(grad_branch, weight_out, pa, pb, e, flat, inv)


def gelu_parts(v):
    size = jnp.abs(v)
    base = 1.0 + (0.3275911 * 0.5**0.5) * size
    near = pl.reciprocal(base, approx=True)
    t = near * (2.0 - base * near)
    bell = jnp.exp(-0.5 * (v * v))
    tail = t * (0.127414796 + t * (-0.142248368 + t * (0.710706871 + t * (-0.7265760135 + t * 0.5307027145)))) * bell
    below = jnp.where(v >= 0.0, 1.0 - tail, tail)
    return v * below, below + 0.3989422804014327 * (v * bell)


def widen_kernel(x_ref, w_ref, hid_ref, slope_ref):
    x = x_ref[...]
    for start in range(0, w_ref.shape[1], 256):
        cut = slice(start, start + 256)
        value, slope = gelu_parts(dot_nn(x, w_ref[:, cut]))
        hid_ref[:, cut] = low(value)
        slope_ref[:, cut] = low(slope)


def widen(first_low, weight_in):
    rows, width = first_low.shape
    span = weight_in.shape[1]
    block, part = 256, span // 2
    bf = jnp.bfloat16
    return pl.pallas_call(
        widen_kernel,
        grid=(2, rows // block),
        in_specs=[
            pl.BlockSpec((block, width), lambda t, r: (r, 0)),
            pl.BlockSpec((width, part), lambda t, r: (0, t)),
        ],
        out_specs=[pl.BlockSpec((block, part), lambda t, r: (r, t))] * 2,
        out_shape=[jax.ShapeDtypeStruct((rows, span), bf)] * 2,
        compiler_params=pltpu.CompilerParams(vmem_limit_bytes=VMEM),
        cost_estimate=pl.CostEstimate(flops=10_000_000_000, bytes_accessed=20_000_000, transcendentals=3_100_000),
        name="widen",
    )(first_low, weight_in)


def layer_norm(value, gain, shift):
    centered = value - jnp.mean(value, axis=-1, keepdims=True)
    inverse = lax.rsqrt(jnp.mean(centered * centered, axis=-1, keepdims=True) + epsilon)
    scaled = centered * inverse
    return (scaled * gain + shift, scaled, inverse)


def norm_back(grad_output, scaled, inverse, gain):
    grad_scaled = grad_output * gain
    centered_grad = grad_scaled - jnp.mean(grad_scaled, axis=-1, keepdims=True)
    return inverse * (
        centered_grad - scaled * jnp.mean(grad_scaled * scaled, axis=-1, keepdims=True)
    )


def norm_stats(grad_output, scaled):
    return jnp.stack([jnp.sum(grad_output * scaled, axis=0), jnp.sum(grad_output, axis=0)])


def halves(value):
    return jnp.split(value, 2, axis=-1)


def shards(
    tokens,
    segment,
    weight_qkv,
    weight_out,
    weight_in,
    weight_down,
    gain_one,
    shift_one,
    gain_two,
    shift_two,
    cotangent,
):
    rows, width = tokens.shape
    own = weight_qkv.shape[1]
    wide = weight_out.shape[0]
    span = weight_in.shape[1]
    sides = range(2)
    bf = jnp.bfloat16

    norms = jnp.stack([gain_one, shift_one, gain_two, shift_two], axis=1)
    norms = jnp.pad(norms, ((0, 0), (0, LANES - 4)))
    set_one = jnp.concatenate([jnp.transpose(weight_qkv, (1, 0, 2)).reshape(own, -1), norms], axis=1)
    set_two = jnp.concatenate([weight_out.T, weight_in, jnp.zeros((own, LANES), bf)], axis=1)
    get_one = gather_steps(*halves(set_one))
    get_two = gather_steps(*halves(set_two))
    get_three = gather_steps(*halves(weight_down.T))
    one = next(get_one)
    two = next(get_two)
    three = next(get_three)
    one = get_one.send(one)
    one, two = tie(one, two)
    two = get_two.send(two)
    one = get_one.send(one)
    one = get_one.send(one)
    one, two, three = tie(one, two, three)
    three = get_three.send(three)
    left, right = get_one.send(one)
    norms = right[0, :, right.shape[2] - LANES :][:, :4].T.astype(jnp.float32)
    gain_first, shift_first, gain_second, shift_second = [norms[i] for i in range(4)]

    numbers = lax.dynamic_slice_in_dim(segment, lax.axis_index("tensor") * rows, rows)
    numbers = numbers.reshape(rows // SEQ, SEQ)
    kept = [attend(tokens, left, right, numbers, 0)]
    two = get_two.send(two)
    two, left = tie(two, left)
    kept.append(attend(tokens, left, right, numbers, 1))
    attended = [kept[t][3][0] for t in sides]
    two = get_two.send(two)
    two, three = tie(two, three)
    three = get_three.send(three)
    two_left, two_right = get_two.send(two)
    out = jnp.concatenate([two_left[t][:, :wide] for t in sides], axis=1)
    split = two_left.shape[2] - wide
    win = jnp.concatenate(
        [piece for t in sides for piece in (two_left[t][:, wide:], two_right[t][:, : span - split])], axis=1
    )

    branch = dot_nt(attended[0], out[:, :wide]) + dot_nt(attended[1], out[:, wide:])
    first, scaled_one, inverse_one = layer_norm(
        tokens.astype(jnp.float32) + branch, gain_first, shift_first
    )
    first_low = low(first)
    three, first_low = tie(three, first_low)
    hidden, slope = widen(first_low, win)
    three = get_three.send(three)
    three_left, three_right = get_three.send(three)
    down = jnp.concatenate([piece for t in sides for piece in (three_left[t], three_right[t])], axis=1)
    second = dot_nt(hidden, down)
    final, scaled_two, inverse_two = layer_norm(first + second, gain_second, shift_second)
    output = low(final)

    grad_final = cotangent.astype(jnp.float32)
    stats_two = norm_stats(grad_final, scaled_two)
    grad_resid_two = norm_back(grad_final, scaled_two, inverse_two, gain_second)
    grad_second = low(grad_resid_two)
    grad_down = low(dot_tn(grad_second, hidden)).reshape(width, 2, 2, -1)
    put_down = scatter_steps(*[jnp.transpose(grad_down[:, :, i], (1, 0, 2)) for i in sides])
    three = next(put_down)
    grad_inner = low(dot_nn(grad_second, down) * slope.astype(jnp.float32))
    three, grad_inner = tie(three, grad_inner)
    three = put_down.send(three)
    grad_in = low(dot_tn(first_low, grad_inner))
    three, grad_inner = tie(three, grad_inner)
    three = put_down.send(three)
    grad_first = grad_resid_two + dot_nt(grad_inner, win)
    stats_one = norm_stats(grad_first, scaled_one)
    grad_resid_one = norm_back(grad_first, scaled_one, inverse_one, gain_first)
    grad_branch = low(grad_resid_one)
    three, grad_branch = tie(three, grad_branch)
    three = put_down.send(three)
    grad_out = [low(dot_tn(grad_branch, attended[t])) for t in sides]
    stats = low(jnp.concatenate([stats_one, stats_two]).T)
    stats = jnp.pad(stats, ((0, 0), (0, LANES - 4)))
    put_two = scatter_steps(
        jnp.stack([jnp.concatenate([grad_out[t], grad_in[:, t * span : t * span + split]], axis=1) for t in sides]),
        jnp.stack([jnp.concatenate([grad_in[:, t * span + split : (t + 1) * span], stats], axis=1) for t in sides]),
    )
    two = next(put_two)
    grad_parts = [attend_back(grad_branch, out, kept[0], 0)]
    two, grad_branch = tie(two, grad_branch)
    two = put_two.send(two)
    grad_parts.append(attend_back(grad_branch, out, kept[1], 1))
    put_one = scatter_steps(
        *[jnp.stack([low(dot_tn(tokens, grad_parts[t][i][0])) for t in sides]) for i in sides]
    )
    one = next(put_one)
    two = put_two.send(two)
    one, two = tie(one, two)
    one = put_one.send(one)
    two = put_two.send(two)
    back = grad_resid_one
    for t in sides:
        back = back + dot_nt(grad_parts[t][0][0], left[t]) + dot_nt(grad_parts[t][1][0], right[t])
    input_grad = low(back)
    one = put_one.send(one)
    one = put_one.send(one)
    sum_one = jnp.concatenate(put_one.send(one), axis=1)[:, : 3 * wide]
    sum_two = jnp.concatenate(put_two.send(two), axis=1)
    sum_down = jnp.concatenate(put_down.send(three), axis=1)
    stats = sum_two[:, wide + span : wide + span + 4].T
    return (
        output,
        input_grad,
        jnp.transpose(sum_one.reshape(own, 3, -1), (1, 0, 2)),
        sum_two[:, :wide].T,
        sum_two[:, wide : wide + span],
        sum_down.T,
        stats[0],
        stats[1],
        stats[2],
        stats[3],
    )


def solution(mesh):
    both = P(("dp", "tensor"), None)
    split = P("dp")
    qkv_spec = P(None, "dp", "tensor")
    row_spec = P("tensor", "dp")
    in_spec = P("dp", "tensor")
    return jax.shard_map(
        shards,
        mesh=mesh,
        in_specs=(both, split, qkv_spec, row_spec, in_spec, row_spec, split, split, split, split, both),
        out_specs=(both, both, qkv_spec, row_spec, in_spec, row_spec, split, split, split, split),
        check_vma=False,
    )
```

time: 497 us -> 433 us (0.87)
  matrix products: 168 us -> 68.6 us
  Pallas kernels: 0 us -> 75.2 us
  other arithmetic: 79 us -> 55.6 us
  local copies, waits for them, and re-layouts: 81.8 us -> 62.5 us
    pallas_call x0 -> x5, Pallas kernels: none -> 75.2 us  [the longest x2 30.7 us: attend(): pl.pallas_call(attend_kernel, grid=(seqs,), in_specs=[pl.BlockSpec((SEQ,...]
    dot_general x12 -> x0, matrix products: 56.6 us -> none  [the longest x2 17.8 us: shards(): jnp.einsum('bqhd,bkhd->bhqk', grad_mixed, value_rows, preferred_element_t...]
    dot_general x8 -> x1, matrix products: 60.7 us -> 13.8 us  [dot_nn(): lax.dot_general(left, right, (((1,), (0,)), ((), ())), preferred_element_...]
    slice x2 -> x22, local copies, waits for them, and re-layouts: 4.45 us -> 19.1 us  [the longest x1 9.9 us: shards(): grad_down[:, :, i]]
    convert_element_type x15 -> x12, other arithmetic: 34.3 us -> 20.5 us  [the longest x11 20.5 us: low(): return value.astype(jnp.bfloat16)]
    reshape x9 -> x2, local copies, waits for them, and re-layouts: 23.8 us -> 11.7 us  [the longest x1 11.6 us: shards(): grad_down = low(dot_tn(grad_second, hidden)).reshape(width, 2, 2, -1)]
    unnamed x205 -> x143, local copies, waits for them, and re-layouts: 28.7 us -> 18.9 us
    convert_element_type x10 -> x2, local copies, waits for them, and re-layouts: 12.5 us -> 3.08 us  [low(): return value.astype(jnp.bfloat16)]
  transfers between devices with their start and end apart: 42 -> 42, of which waited for: 19 -> 24; matrix products, arithmetic and copies ran while one was open for 26% -> 18% of each run, Pallas kernels for 0% -> 15%
where the time goes in v3:
time: 433 us; the launch traced here: 429 us
  waiting for transfers between devices  113 us (26%)
  Pallas kernels  75.2 us (17%)
  matrix products  68.6 us (16%)
  local copies, waits for them, and re-layouts  62.5 us (14%)
  other arithmetic  55.6 us (13%)
  starting transfers between devices  51.9 us (12%)
    ppermute x42, waiting for transfers between devices, send(): return lax.ppermute(value, AXES, route)  113 us
    ppermute x42, starting transfers between devices, send(): return lax.ppermute(value, AXES, route)  51.9 us
    pallas_call x2, Pallas kernels, attend(): pl.pallas_call(attend_kernel, grid=(seqs,), in_specs=[pl.BlockSpec((SEQ,...  30.7 us
    dot_general x8, matrix products, dot_nt(): lax.dot_general(left, right, (((1,), (1,)), ((), ())), preferred_element_...  28.8 us
    dot_general x8, matrix products, dot_tn(): lax.dot_general(left, right, (((0,), (0,)), ((), ())), preferred_element_...  26.1 us
    pallas_call x2, Pallas kernels, attend_back(): pl.pallas_call(attend_back_kernel, grid=(seqs,), in_specs=[pl.BlockSpec((...  25 us
    convert_element_type x11, other arithmetic, low(): return value.astype(jnp.bfloat16)  20.5 us
    pallas_call x1, Pallas kernels, widen(): pl.pallas_call(widen_kernel, grid=(2, rows // block), in_specs=[pl.BlockS...  19.6 us
  transfers between devices with their start and end apart: 42, of which 24 were waited for; matrix products, arithmetic and copies ran while one was open for 18% of the time, Pallas kernels for 15%

profile of v3, /device:TPU:0, one launch (start us, length us, event | category | flops | bytes accessed | tf_op | source)
XLA Modules:
  0.0 428.7 jit_solution(16216761326813319945)
XLA Ops:
  5.6 2.7 collective-permute-start.3
  8.3 2.6 collective-permute-start.2
  12.4 4.8 %collective-permute-done.1 = bf16[96,640]{1,0:T(8,128)(2,1)S(1)} collective-permute-done((bf16[96,640]{1,0:T(8,128)(2,1)S(1)}, bf16[96,640]{1,0:T(8,128)(2,1)S(1)}, u32[]{:S(2)}, u32[]{:S(2)}) %collective-permute-start.1) | collective-permute-done | bytes 122912 | tf_op jit(solution)/shard_map/ppermute | solution.py:45
  17.2 2.4 collective-permute-done.2
  19.8 3.2 collective-permute-start.9
  26.9 8.9 %collective-permute-done.7 = bf16[96,1024]{1,0:T(8,128)(2,1)S(1)} collective-permute-done((bf16[96,1024]{1,0:T(8,128)(2,1)S(1)}, bf16[96,1024]{1,0:T(8,128)(2,1)S(1)}, u32[]{:S(2)}, u32[]{:S(2)}) %collective-permute-start.7) | collective-permute-done | bytes 196640 | tf_op jit(solution)/shard_map/ppermute | solution.py:45
  39.5 12.2 %collective-permute-done.6 = bf16[2,4,96,640]{3,2,1,0:T(8,128)(2,1)S(1)} collective-permute-done((bf16[2,4,96,640]{3,2,1,0:T(8,128)(2,1)S(1)}, bf16[2,4,96,640]{3,2,1,0:T(8,128)(2,1)S(1)}, u32[]{:S(2)}, u32[]{:S(2)}) %collective-permute-start.6) | collective-permute-done | bytes 983072 | tf_op jit(solution)/shard_map/ppermute | solution.py:45
  53.6 4.7 %collective-permute-start.16 = (bf16[96,768]{1,0:T(8,128)(2,1)S(1)}, bf16[96,768]{1,0:T(8,128)(2,1)S(1)}, u32[]{:S(2)}, u32[]{:S(2)}) collective-permute-start(bf16[96,768]{1,0:T(8,128)(2,1)S(1)} %maximum_select_fusion.8), channel_id=1, source_target_pairs={{0,8},{1,9},{2,10},{3,11},{4,12},{5,13},{6,14},{7,15},{8,16},{9,17... | collective-permute-start | bytes 442376 | tf_op jit(solution)/shard_map/ppermute | solution.py:45
  60.9 3.2 collective-permute-done.12
  68.2 1.9 collective-permute-done.15
  70.2 16.6 %collective-permute-done.13 = bf16[2,4,96,1024]{3,2,1,0:T(8,128)(2,1)S(1)} collective-permute-done((bf16[2,4,96,1024]{3,2,1,0:T(8,128)(2,1)S(1)}, bf16[2,4,96,1024]{3,2,1,0:T(8,128)(2,1)S(1)}, u32[]{:S(2)}, u32[]{:S(2)}) %collective-permute-start.13) | collective-permute-done | bytes 1572896 | tf_op jit(solution)/shard_map/ppermute | solution.py:45
  86.9 1.9 maximum_select_fusion
  91.5 15.3 %attend.2 = (bf16[1,1024,640]{2,1,0:T(8,128)(2,1)}, bf16[1,1024,512]{2,1,0:T(8,128)(2,1)}, bf16[1,2,6,512,512]{4,3,2,1,0:T(8,128)(2,1)}, bf16[1,1024,384]{2,1,0:...) custom-call(bf16[1024,768]{1,0:T(8,128)(2,1)} %x_ref.3, bf16[2,768,640]{2,1,0:T(8,128)(2,1)} %bitcast.316, ...), custom_call_target="tpu_custom_call" | custom-call | flops 8000000000 | bytes 15000000 | tf_op jit(solution)/shard_map/attend/pallas_call | solution.py:209
  108.3 15.5 %attend.3 = (bf16[1,1024,640]{2,1,0:T(8,128)(2,1)}, bf16[1,1024,512]{2,1,0:T(8,128)(2,1)}, bf16[1,2,6,512,512]{4,3,2,1,0:T(8,128)(2,1)}, bf16[1,1024,384]{2,1,0:...) custom-call(bf16[1024,768]{1,0:T(8,128)(2,1)} %x_ref.3, bf16[2,768,640]{2,1,0:T(8,128)(2,1)} %bitcast.317, ...), custom_call_target="tpu_custom_call" | custom-call | flops 8000000000 | bytes 15000000 | tf_op jit(solution)/shard_map/attend/pallas_call | solution.py:209
  123.9 3.3 select_bitcast_fusion
  132.5 1.7 fusion.11.x_ref
  135.7 14.7 %collective-permute-done.19 = bf16[2,4,96,768]{3,2,0,1:T(8,128)(2,1)S(1)} collective-permute-done((bf16[2,4,96,768]{3,2,0,1:T(8,128)(2,1)S(1)}, bf16[2,4,96,768]{3,2,0,1:T(8,128)(2,1)S(1)}, u32[]{:S(2)}, u32[]{:S(2)}) %collective-permute-start.19) | collective-permute-done | bytes 1179680 | tf_op jit(solution)/shard_map/ppermute | solution.py:45
  150.4 1.8 maximum_select_fusion.1
  154.3 2.7 pad_maximum_fusion.w_ref
  157.0 19.6 %widen.1 = (bf16[1024,3072]{1,0:T(8,128)(2,1)}, bf16[1024,3072]{1,0:T(8,128)(2,1)}) custom-call(bf16[1024,768]{1,0:T(8,128)(2,1)} %fusion.11.x_ref, bf16[768,3072]{1,0:T(8,128)(2,1)} %pad_maximum_fusion.w_ref), custom_call_target="tpu_custom_call" | custom-call | flops 10000000000 | bytes 20000000 | tf_op jit(solution)/shard_map/widen/pallas_call | solution.py:344
  176.5 2.4 select_bitcast_fusion.4
  180.5 2.3 slice-done
  183.5 5.3 %fusion.71 = (f32[1024]{0:T(1024)S(1)}, f32[1024,768]{1,0:T(8,128)S(1)}) fusion(bf16[1024,3072]{1,0:T(8,128)(2,1)S(1)} %bitcast.358, bf16[768,768]{1,0:T(8,128)(2,1)S(1)} %bitcast.329, bf16[768,768]{1,0:T(8,128)(2,1)S(1)} %bitcast.334, bf16[768,768]{1,0:T(8,128)(2,1)S(1)} %bitcast.327, bf16[768,768]{1,0:T(8,128)(2,1)S(1)} %bitcast.332, ...), kind=kOutput, calls=%fused_computation.223 | convolution fusion | flops 4855430144 | bytes 17319936 | tf_op jit(solution)/shard_map/dot_general | solution.py:151
  189.4 2.0 copy-done.13
  191.4 2.7 fusion.7
  194.1 8.0 %convolution_convert_fusion.1 = bf16[768,3072]{1,0:T(8,128)(2,1)} fusion(bf16[1024,3072]{1,0:T(8,128)(2,1)S(1)} %bitcast.358, bf16[1024,768]{1,0:T(8,128)(2,1)S(1)} %copy-done.13, f32[1024,768]{1,0:T(8,128)S(1)} %get-tuple-element.194, f32[1024]{0:T(1024)S(1)} %get-tuple-element.196, f32[1024]{0:T(1024)S(1)} %get-tuple-element.197, ...), kind=kOutput, calls=%fused_computation.3 | convolution fusion | flops 4841275392 | bytes 15748096 | tf_op jit(solution)/shard_map/dot_general | solution.py:147
  202.1 11.6 %reshape.252 = bf16[768,2,2,768]{3,2,1,0:T(2,128)(2,1)} reshape(bf16[768,3072]{1,0:T(8,128)(2,1)} %convolution_convert_fusion.1) | data formatting | bytes 9437184 | tf_op jit(solution)/shard_map/reshape | solution.py:458
  213.7 9.9 %fusion.63 = (bf16[768,2,1,768]{3,2,1,0:T(2,128)(2,1)S(1)}, bf16[768,2,1,768]{3,2,1,0:T(2,128)(2,1)S(1)}) fusion(bf16[768,2,2,768]{3,2,1,0:T(2,128)(2,1)} %reshape.252), kind=kLoop, calls=%fused_computation.215 | loop fusion | bytes 9437184 | tf_op jit(solution)/shard_map/slice | solution.py:459
  223.7 2.3 select_bitcast_fusion.2
  230.3 13.8 %multiply_convert_fusion = bf16[1024,3072]{1,0:T(8,128)(2,1)} fusion(bf16[1024,3072]{1,0:T(8,128)(2,1)} %get-tuple-element.63, bf16[768,768]{1,0:T(8,128)(2,1)} %bitcast.330, bf16[768,768]{1,0:T(8,128)(2,1)} %bitcast.335, bf16[768,768]{1,0:T(8,128)(2,1)} %bitcast.328, bf16[768,768]{1,0:T(8,128)(2,1)} %bitcast.333, bf16[1024,768]{1,0:T(8,128)(2,1)} %param.21, ...), kind=kOutput, calls=%fused_computation | convolution fusion | flops 4867227648 | bytes 22039552 | tf_op jit(solution)/shard_map/dot_general | solution.py:143
  244.0 5.3 %fusion.1 = bf16[2,768,768]{2,1,0:T(8,128)(2,1)S(1)} fusion(bf16[2,768,768]{2,1,0:T(8,128)(2,1)} %collective-permute-done.21, pred[]{:T(512)S(6)} %eq.46, bf16[768,2,1,768]{3,2,1,0:T(2,128)(2,1)} %copy-done.1, bf16[768,2,1,768]{3,2,1,0:T(2,128)(2,1)} %copy-done), kind=kLoop, calls=%fused_computation.8 | loop fusion | flops 5898240 | bytes 9437185 | tf_op jit(solution)/shard_map/convert_element_type | solution.py:155
  252.6 5.6 %convolution_convert_fusion = bf16[768,3072]{1,0:T(8,128)(2,1)S(1)} fusion(bf16[1024,768]{1,0:T(8,128)(2,1)S(1)} %copy-done.37, bf16[1024,3072]{1,0:T(8,128)(2,1)S(1)} %copy-done.60), kind=kOutput, calls=%fused_computation.2 | convolution fusion | flops 4834197504 | bytes 12582912 | tf_op jit(solution)/shard_map/dot_general | solution.py:147
  259.7 1.8 fusion.62
  261.5 4.5 %collective-permute-done.22 = bf16[2,4,96,768]{3,2,0,1:T(8,128)(2,1)S(1)} collective-permute-done((bf16[2,4,96,768]{3,2,0,1:T(8,128)(2,1)S(1)}, bf16[2,4,96,768]{3,2,0,1:T(8,128)(2,1)S(1)}, u32[]{:S(2)}, u32[]{:S(2)}) %collective-permute-start.22) | collective-permute-done | bytes 1179680 | tf_op jit(solution)/shard_map/ppermute | solution.py:45
  268.7 10.9 %multiply_reduce_fusion.1 = (f32[1024]{0:T(1024)S(1)}, bf16[768]{0:T(1024)(128)(2,1)S(1)}, f32[1024]{0:T(1024)S(1)}, bf16[768]{0:T(1024)(128)(2,1)S(1)}, f32[1024,768]{1,0:T(8,128)}) fusion(f32[1024,768]{1,0:T(8,128)S(1)} %get-tuple-element.192, f32[768]{0:T(1024)S(1)} %get-tuple-element.128, f32[1024]{0:T(1024)S(1)} %add_rsqrt_fusion.1, ...), kind=kOutput, calls=%fused_computation.27 | convolution fusion | flops 4864864256 | bytes 22062080 | tf_op jit(solution)/shard_map/dot_general | solution.py:151
  281.6 4.1 fusion.15
  285.7 2.3 fusion.59
  288.0 3.0 collective-permute-done.23
  291.9 1.9 convolution_convert_fusion.6
  297.4 2.0 broadcast_select_fusion
  302.8 12.6 %attend_back.2 = (bf16[1,1024,640]{2,1,0:T(8,128)(2,1)}, bf16[1,1024,640]{2,1,0:T(8,128)(2,1)}) custom-call(bf16[1024,768]{1,0:T(8,128)(2,1)} %copy-done.36, bf16[768,768]{1,0:T(8,128)(2,1)} %pad_maximum_fusion.6.w_ref, bf16[1,1024,640]{2,1,0:T(8,128)(2,1)} %get-tuple-element.69.pa_ref, bf16[1,1024,512]{2,1,0:T(8,128)(2,1)} %get-tuple-element.70.pb_ref, ...), custom_call_target="tpu_custom_call" | custom-call | flops 8000000000 | bytes 15000000 | tf_op jit(solution)/shard_map/attend_back/pallas_call | solution.py:295
  315.4 3.7 fusion.17
  319.0 2.2 fusion.19
  321.3 3.6 add_convert_fusion
  324.9 12.4 %attend_back.3 = (bf16[1,1024,640]{2,1,0:T(8,128)(2,1)}, bf16[1,1024,640]{2,1,0:T(8,128)(2,1)}) custom-call(bf16[1024,768]{1,0:T(8,128)(2,1)} %copy-done.36, bf16[768,768]{1,0:T(8,128)(2,1)} %pad_maximum_fusion.6.w_ref, bf16[1,1024,640]{2,1,0:T(8,128)(2,1)} %get-tuple-element.77.pa_ref, bf16[1,1024,512]{2,1,0:T(8,128)(2,1)} %get-tuple-element.78.pb_ref, ...), custom_call_target="tpu_custom_call" | custom-call | flops 8000000000 | bytes 15000000 | tf_op jit(solution)/shard_map/attend_back/pallas_call | solution.py:295
  337.3 2.6 fusion.18
  346.5 5.9 %collective-permute-start.38 = (bf16[96,768]{1,0:T(8,128)(2,1)S(1)}, bf16[96,768]{1,0:T(8,128)(2,1)S(1)}, u32[]{:S(2)}, u32[]{:S(2)}) collective-permute-start(bf16[96,768]{1,0:T(8,128)(2,1)S(1)} %get-tuple-element.171), channel_id=1, source_target_pairs={{0,24},{1,25},{2,26},{3,27},{4,28},{5,29},{6,30},{7,31},{8,0},{9,1... | collective-permute-start | bytes 442376 | tf_op jit(solution)/shard_map/ppermute | solution.py:45
  353.0 3.1 fusion.30
  356.6 4.3 %collective-permute-done.40 = bf16[96,768]{1,0:T(8,128)(2,1)S(1)} collective-permute-done((bf16[96,768]{1,0:T(8,128)(2,1)S(1)}, bf16[96,768]{1,0:T(8,128)(2,1)S(1)}, u32[]{:S(2)}, u32[]{:S(2)}) %collective-permute-start.40) | collective-permute-done | bytes 147488 | tf_op jit(solution)/shard_map/ppermute | solution.py:45
  360.9 5.0 %collective-permute-done.39 = bf16[96,768]{1,0:T(8,128)(2,1)S(1)} collective-permute-done((bf16[96,768]{1,0:T(8,128)(2,1)S(1)}, bf16[96,768]{1,0:T(8,128)(2,1)S(1)}, u32[]{:S(2)}, u32[]{:S(2)}) %collective-permute-start.39) | collective-permute-done | bytes 147488 | tf_op jit(solution)/shard_map/ppermute | solution.py:45
  368.9 3.1 fusion.27
  372.7 2.1 add_convert_fusion.1
  374.9 2.8 copy.135
  377.6 2.8 collective-permute-done.27
  384.7 2.7 collective-permute-start.34
  389.7 5.4 %collective-permute-done.34 = bf16[96,1024]{1,0:T(8,128)(2,1)S(1)} collective-permute-done((bf16[96,1024]{1,0:T(8,128)(2,1)S(1)}, bf16[96,1024]{1,0:T(8,128)(2,1)S(1)}, u32[]{:S(2)}, u32[]{:S(2)}) %collective-permute-start.34) | collective-permute-done | bytes 196640 | tf_op jit(solution)/shard_map/ppermute | solution.py:45
  395.2 2.1 collective-permute-done.36
  397.3 5.1 %collective-permute-done.35 = bf16[96,1024]{1,0:T(8,128)(2,1)S(1)} collective-permute-done((bf16[96,1024]{1,0:T(8,128)(2,1)S(1)}, bf16[96,1024]{1,0:T(8,128)(2,1)S(1)}, u32[]{:S(2)}, u32[]{:S(2)}) %collective-permute-start.35) | collective-permute-done | bytes 196640 | tf_op jit(solution)/shard_map/ppermute | solution.py:45
  405.0 2.7 add_convert_fusion.3
  408.5 3.5 collective-permute-done.29
  412.2 3.2 collective-permute-start.30
  416.7 2.5 collective-permute-done.30
  419.2 4.0 collective-permute-done.32
  423.2 3.0 collective-permute-done.31
  (309 shorter events, 85.1 us)
Async XLA Ops:
  2.4 3.1 collective-permute-start
  3.9 8.4 %collective-permute-start.10 = (bf16[48,768]{1,0:T(8,128)(2,1)S(1)}, bf16[48,768]{1,0:T(8,128)(2,1)S(1)}, u32[]{:S(2)}, u32[]{:S(2)}) collective-permute-start(bf16[48,768]{1,0:T(8,128)(2,1)S(1)} %get-tuple-element.186), channel_id=1, source_target_pairs={{0,2},{1,3},{2,0},{3,1},{4,6},{5,7},{6,4},{7,5},{8,10},{9,11},{10,... | collective-permute-start | bytes 221192 | tf_op jit(solution)/shard_map/ppermute | solution.py:45
  5.0 7.3 %collective-permute-start.4 = (bf16[48,1024]{1,0:T(8,128)(2,1)S(1)}, bf16[48,1024]{1,0:T(8,128)(2,1)S(1)}, u32[]{:S(2)}, u32[]{:S(2)}) collective-permute-start(bf16[48,1024]{1,0:T(8,128)(2,1)S(1)} %get-tuple-element.135), channel_id=1, source_target_pairs={{0,2},{1,3},{2,0},{3,1},{4,6},{5,7},{6,4},{7,5},{8,10},{9,11},{10,... | collective-permute-start | bytes 294920 | tf_op jit(solution)/shard_map/ppermute | solution.py:45
  5.6 14.0 %collective-permute-start.3 = (bf16[96,640]{1,0:T(8,128)(2,1)S(1)}, bf16[96,640]{1,0:T(8,128)(2,1)S(1)}, u32[]{:S(2)}, u32[]{:S(2)}) collective-permute-start(bf16[96,640]{1,0:T(8,128)(2,1)S(1)} %maximum_select_fusion.10), channel_id=1, source_target_pairs={{0,8},{1,9},{2,10},{3,11},{4,12},{5,13},{6,14},{7,15},{8,16},{9,17... | collective-permute-start | bytes 368648 | tf_op jit(solution)/shard_map/ppermute | solution.py:45
  8.3 11.3 %collective-permute-start.2 = (bf16[96,640]{1,0:T(8,128)(2,1)S(1)}, bf16[96,640]{1,0:T(8,128)(2,1)S(1)}, u32[]{:S(2)}, u32[]{:S(2)}) collective-permute-start(bf16[96,640]{1,0:T(8,128)(2,1)S(1)} %maximum_select_fusion.10), channel_id=1, source_target_pairs={{0,16},{1,17},{2,18},{3,19},{4,20},{5,21},{6,22},{7,23},{8,24},{9,... | collective-permute-start | bytes 368648 | tf_op jit(solution)/shard_map/ppermute | solution.py:45
  10.9 6.3 %collective-permute-start.1 = (bf16[96,640]{1,0:T(8,128)(2,1)S(1)}, bf16[96,640]{1,0:T(8,128)(2,1)S(1)}, u32[]{:S(2)}, u32[]{:S(2)}) collective-permute-start(bf16[96,640]{1,0:T(8,128)(2,1)S(1)} %maximum_select_fusion.10), channel_id=1, source_target_pairs={{0,24},{1,25},{2,26},{3,27},{4,28},{5,29},{6,30},{7,31},{8,0},{9,1... | collective-permute-start | bytes 368648 | tf_op jit(solution)/shard_map/ppermute | solution.py:45
  19.8 19.3 %collective-permute-start.9 = (bf16[96,1024]{1,0:T(8,128)(2,1)S(1)}, bf16[96,1024]{1,0:T(8,128)(2,1)S(1)}, u32[]{:S(2)}, u32[]{:S(2)}) collective-permute-start(bf16[96,1024]{1,0:T(8,128)(2,1)S(1)} %maximum_select_fusion.7), channel_id=1, source_target_pairs={{0,8},{1,9},{2,10},{3,11},{4,12},{5,13},{6,14},{7,15},{8,16},{9,17... | collective-permute-start | bytes 589832 | tf_op jit(solution)/shard_map/ppermute | solution.py:45
  23.0 14.3 %collective-permute-start.8 = (bf16[96,1024]{1,0:T(8,128)(2,1)S(1)}, bf16[96,1024]{1,0:T(8,128)(2,1)S(1)}, u32[]{:S(2)}, u32[]{:S(2)}) collective-permute-start(bf16[96,1024]{1,0:T(8,128)(2,1)S(1)} %maximum_select_fusion.7), channel_id=1, source_target_pairs={{0,16},{1,17},{2,18},{3,19},{4,20},{5,21},{6,22},{7,23},{8,24},{9,... | collective-permute-start | bytes 589832 | tf_op jit(solution)/shard_map/ppermute | solution.py:45
  24.6 11.2 %collective-permute-start.7 = (bf16[96,1024]{1,0:T(8,128)(2,1)S(1)}, bf16[96,1024]{1,0:T(8,128)(2,1)S(1)}, u32[]{:S(2)}, u32[]{:S(2)}) collective-permute-start(bf16[96,1024]{1,0:T(8,128)(2,1)S(1)} %maximum_select_fusion.7), channel_id=1, source_target_pairs={{0,24},{1,25},{2,26},{3,27},{4,28},{5,29},{6,30},{7,31},{8,0},{9,1... | collective-permute-start | bytes 589832 | tf_op jit(solution)/shard_map/ppermute | solution.py:45
  25.4 11.9 %collective-permute-start.5 = (bf16[4,96,640]{2,1,0:T(8,128)(2,1)S(1)}, bf16[4,96,640]{2,1,0:T(8,128)(2,1)S(1)}, u32[]{:S(2)}, u32[]{:S(2)}) collective-permute-start(bf16[4,96,640]{2,1,0:T(8,128)(2,1)S(1)} %constant_dynamic-slice_fusion.4), channel_id=1, source_target_pairs={{0,4},{1,5},{2,3},{3,2},{4,0},{5,1},{6,7},{7,6},{8,12},{9,13},{10,... | collective-permute-start | bytes 1474568 | tf_op jit(solution)/shard_map/ppermute | solution.py:45
  37.5 14.2 %collective-permute-start.6 = (bf16[2,4,96,640]{3,2,1,0:T(8,128)(2,1)S(1)}, bf16[2,4,96,640]{3,2,1,0:T(8,128)(2,1)S(1)}, u32[]{:S(2)}, u32[]{:S(2)}) collective-permute-start(bf16[2,4,96,640]{3,2,1,0:T(8,128)(2,1)S(1)} %maximum_select_fusion.6), channel_id=1, source_target_pairs={{0,1},{1,0},{2,6},{3,7},{4,5},{5,4},{6,2},{7,3},{8,9},{9,8},{10,14... | collective-permute-start | bytes 2949128 | tf_op jit(solution)/shard_map/ppermute | solution.py:45
  52.0 12.4 %collective-permute-start.11 = (bf16[2,2,4,96,640]{4,3,2,1,0:T(8,128)(2,1)S(1)}, bf16[2,2,4,96,640]{4,3,2,1,0:T(8,128)(2,1)S(1)}, u32[]{:S(2)}, u32[]{:S(2)}) collective-permute-start(bf16[2,2,4,96,640]{4,3,2,1,0:T(8,128)(2,1)S(1)} %maximum_select_fusion.2), channel_id=1, source_target_pairs={{0,2},{1,3},{2,0},{3,1},{4,6},{5,7},{6,4},{7,5},{8,10},{9,11},{10,... | collective-permute-start | bytes 5898248 | tf_op jit(solution)/shard_map/ppermute | solution.py:45
  52.1 12.1 %collective-permute-start.12 = (bf16[4,96,1024]{2,1,0:T(8,128)(2,1)S(1)}, bf16[4,96,1024]{2,1,0:T(8,128)(2,1)S(1)}, u32[]{:S(2)}, u32[]{:S(2)}) collective-permute-start(bf16[4,96,1024]{2,1,0:T(8,128)(2,1)S(1)} %constant_dynamic-slice_fusion.3), channel_id=1, source_target_pairs={{0,4},{1,5},{2,3},{3,2},{4,0},{5,1},{6,7},{7,6},{8,12},{9,13},{10,... | collective-permute-start | bytes 2359304 | tf_op jit(solution)/shard_map/ppermute | solution.py:45
  53.6 16.5 %collective-permute-start.16 = (bf16[96,768]{1,0:T(8,128)(2,1)S(1)}, bf16[96,768]{1,0:T(8,128)(2,1)S(1)}, u32[]{:S(2)}, u32[]{:S(2)}) collective-permute-start(bf16[96,768]{1,0:T(8,128)(2,1)S(1)} %maximum_select_fusion.8), channel_id=1, source_target_pairs={{0,8},{1,9},{2,10},{3,11},{4,12},{5,13},{6,14},{7,15},{8,16},{9,17... | collective-permute-start | bytes 442376 | tf_op jit(solution)/shard_map/ppermute | solution.py:45
  58.4 11.7 %collective-permute-start.15 = (bf16[96,768]{1,0:T(8,128)(2,1)S(1)}, bf16[96,768]{1,0:T(8,128)(2,1)S(1)}, u32[]{:S(2)}, u32[]{:S(2)}) collective-permute-start(bf16[96,768]{1,0:T(8,128)(2,1)S(1)} %maximum_select_fusion.8), channel_id=1, source_target_pairs={{0,16},{1,17},{2,18},{3,19},{4,20},{5,21},{6,22},{7,23},{8,24},{9,... | collective-permute-start | bytes 442376 | tf_op jit(solution)/shard_map/ppermute | solution.py:45
  60.0 8.1 %collective-permute-start.14 = (bf16[96,768]{1,0:T(8,128)(2,1)S(1)}, bf16[96,768]{1,0:T(8,128)(2,1)S(1)}, u32[]{:S(2)}, u32[]{:S(2)}) collective-permute-start(bf16[96,768]{1,0:T(8,128)(2,1)S(1)} %maximum_select_fusion.8), channel_id=1, source_target_pairs={{0,24},{1,25},{2,26},{3,27},{4,28},{5,29},{6,30},{7,31},{8,0},{9,1... | collective-permute-start | bytes 442376 | tf_op jit(solution)/shard_map/ppermute | solution.py:45
  64.8 25.1 %copy-start.2 = (bf16[2,4,2,96,640]{4,3,1,0,2:T(8,128)(2,1)}, bf16[2,4,2,96,640]{4,3,1,0,2:T(8,128)(2,1)S(1)}, u32[]{:S(2)}) copy-start(bf16[2,4,2,96,640]{4,3,1,0,2:T(8,128)(2,1)S(1)} %get-tuple-element.149) | copy-start | bytes 5898244
  66.4 20.4 %collective-permute-start.13 = (bf16[2,4,96,1024]{3,2,1,0:T(8,128)(2,1)S(1)}, bf16[2,4,96,1024]{3,2,1,0:T(8,128)(2,1)S(1)}, u32[]{:S(2)}, u32[]{:S(2)}) collective-permute-start(bf16[2,4,96,1024]{3,2,1,0:T(8,128)(2,1)S(1)} %maximum_select_fusion.3), channel_id=1, source_target_pairs={{0,1},{1,0},{2,6},{3,7},{4,5},{5,4},{6,2},{7,3},{8,9},{9,8},{10,14... | collective-permute-start | bytes 4718600 | tf_op jit(solution)/shard_map/ppermute | solution.py:45
  88.7 35.1 %collective-permute-start.17 = (bf16[2,2,4,96,1024]{4,3,2,1,0:T(8,128)(2,1)}, bf16[2,2,4,96,1024]{4,3,2,1,0:T(8,128)(2,1)}, u32[]{:S(2)}, u32[]{:S(2)}) collective-permute-start(bf16[2,2,4,96,1024]{4,3,2,1,0:T(8,128)(2,1)} %maximum_select_fusion), channel_id=1, source_target_pairs={{0,2},{1,3},{2,0},{3,1},{4,6},{5,7},{6,4},{7,5},{8,10},{9,11},{10,... | collective-permute-start | bytes 9437192 | tf_op jit(solution)/shard_map/ppermute | solution.py:45
  106.7 17.0 %collective-permute-start.18 = (bf16[4,96,768]{2,1,0:T(8,128)(2,1)S(1)}, bf16[4,96,768]{2,1,0:T(8,128)(2,1)S(1)}, u32[]{:S(2)}, u32[]{:S(2)}) collective-permute-start(bf16[4,96,768]{2,1,0:T(8,128)(2,1)S(1)} %constant_dynamic-slice_fusion.2), channel_id=1, source_target_pairs={{0,4},{1,5},{2,3},{3,2},{4,0},{5,1},{6,7},{7,6},{8,12},{9,13},{10,... | collective-permute-start | bytes 1769480 | tf_op jit(solution)/shard_map/ppermute | solution.py:45
  127.8 24.4 %copy-start.11 = (bf16[1,4,2,96,1024]{4,3,2,1,0:T(8,128)(2,1)}, bf16[1,4,2,96,1024]{4,3,2,1,0:T(8,128)(2,1)S(1)}, u32[]{:S(2)}) copy-start(bf16[1,4,2,96,1024]{4,3,2,1,0:T(8,128)(2,1)S(1)} %copy.118) | copy-start | bytes 4718596
  128.0 24.3 %copy-start.12 = (bf16[1,4,2,96,1024]{4,3,2,1,0:T(8,128)(2,1)}, bf16[1,4,2,96,1024]{4,3,2,1,0:T(8,128)(2,1)S(1)}, u32[]{:S(2)}) copy-start(bf16[1,4,2,96,1024]{4,3,2,1,0:T(8,128)(2,1)S(1)} %copy.116) | copy-start | bytes 4718596
  134.2 16.2 %collective-permute-start.19 = (bf16[2,4,96,768]{3,2,0,1:T(8,128)(2,1)S(1)}, bf16[2,4,96,768]{3,2,0,1:T(8,128)(2,1)S(1)}, u32[]{:S(2)}, u32[]{:S(2)}) collective-permute-start(bf16[2,4,96,768]{3,2,0,1:T(8,128)(2,1)S(1)} %maximum_select_fusion.4), channel_id=1, source_target_pairs={{0,1},{1,0},{2,6},{3,7},{4,5},{5,4},{6,2},{7,3},{8,9},{9,8},{10,14... | collective-permute-start | bytes 3538952 | tf_op jit(solution)/shard_map/ppermute | solution.py:45
  152.2 24.4 %collective-permute-start.20 = (bf16[2,2,4,96,768]{4,3,1,2,0:T(8,128)(2,1)}, bf16[2,2,4,96,768]{4,3,1,2,0:T(8,128)(2,1)}, u32[]{:S(2)}, u32[]{:S(2)}) collective-permute-start(bf16[2,2,4,96,768]{4,3,1,2,0:T(8,128)(2,1)} %maximum_select_fusion.1), channel_id=1, source_target_pairs={{0,2},{1,3},{2,0},{3,1},{4,6},{5,7},{6,4},{7,5},{8,10},{9,11},{10,... | collective-permute-start | bytes 7077896 | tf_op jit(solution)/shard_map/ppermute | solution.py:45
  157.0 19.6 %copy-start.20 = (bf16[2,4,96,768]{3,2,0,1:T(8,128)(2,1)S(1)}, bf16[2,4,96,768]{3,2,0,1:T(8,128)(2,1)}, u32[]{:S(2)}) copy-start(bf16[2,4,96,768]{3,2,0,1:T(8,128)(2,1)} %copy-done.19) | copy-start | bytes 3538948
  179.1 4.4 %slice-start.1 = ((s8[6291456]{0:T(1024)(128)(4,1)}), s8[2097152]{0:T(1024)(128)(4,1)S(1)}, s32[]{:S(2)}) async-start(s8[6291456]{0:T(1024)(128)(4,1)} %bitcast.357), calls=%async_computation.1 | async-start | bytes 4194304
  179.4 9.4 %copy-start.43 = (bf16[1,4,2,96,768]{4,3,2,1,0:T(8,128)(2,1)}, bf16[1,4,2,96,768]{4,3,2,1,0:T(8,128)(2,1)S(1)}, u32[]{:S(2)}) copy-start(bf16[1,4,2,96,768]{4,3,2,1,0:T(8,128)(2,1)S(1)} %copy.123) | copy-start | bytes 3538948
  179.5 9.4 %copy-start.44 = (bf16[1,4,2,96,768]{4,3,2,1,0:T(8,128)(2,1)}, bf16[1,4,2,96,768]{4,3,2,1,0:T(8,128)(2,1)S(1)}, u32[]{:S(2)}) copy-start(bf16[1,4,2,96,768]{4,3,2,1,0:T(8,128)(2,1)S(1)} %copy.124) | copy-start | bytes 3538948
  188.8 5.3 %copy-start.8 = (f32[1024,768]{1,0:T(8,128)}, f32[1024,768]{1,0:T(8,128)S(1)}, u32[]{:S(2)}) copy-start(f32[1024,768]{1,0:T(8,128)S(1)} %get-tuple-element.194) | copy-start | bytes 9437188
  223.7 4.4 %copy-start.1 = (bf16[768,2,1,768]{3,2,1,0:T(2,128)(2,1)}, bf16[768,2,1,768]{3,2,1,0:T(2,128)(2,1)S(1)}, u32[]{:S(2)}) copy-start(bf16[768,2,1,768]{3,2,1,0:T(2,128)(2,1)S(1)} %get-tuple-element.146) | copy-start | bytes 7077892
  228.0 16.0 %collective-permute-start.21 = (bf16[2,768,768]{2,1,0:T(8,128)(2,1)}, bf16[2,768,768]{2,1,0:T(8,128)(2,1)}, u32[]{:S(2)}, u32[]{:S(2)}) collective-permute-start(bf16[2,768,768]{2,1,0:T(8,128)(2,1)} %select_bitcast_fusion.2), channel_id=1, source_target_pairs={{0,2},{1,3},{2,0},{3,1},{4,6},{5,7},{6,4},{7,5},{8,10},{9,11},{10,... | collective-permute-start | bytes 7077896 | tf_op jit(solution)/shard_map/ppermute | solution.py:45
  249.7 16.3 %collective-permute-start.22 = (bf16[2,4,96,768]{3,2,0,1:T(8,128)(2,1)S(1)}, bf16[2,4,96,768]{3,2,0,1:T(8,128)(2,1)S(1)}, u32[]{:S(2)}, u32[]{:S(2)}) collective-permute-start(bf16[2,4,96,768]{3,2,0,1:T(8,128)(2,1)S(1)} %bitcast_select_fusion.2), channel_id=1, source_target_pairs={{0,1},{1,0},{2,6},{3,7},{4,5},{5,4},{6,2},{7,3},{8,9},{9,8},{10,14... | collective-permute-start | bytes 3538952 | tf_op jit(solution)/shard_map/ppermute | solution.py:45
  259.7 7.8 %copy-start.16 = (bf16[768,896]{1,0:T(8,128)(2,1)S(1)}, bf16[768,896]{1,0:T(8,128)(2,1)}, u32[]{:S(2)}) copy-start(bf16[768,896]{1,0:T(8,128)(2,1)} %copy-done.15) | copy-start | bytes 4128772
  259.7 7.8 %copy-start.18 = (bf16[768,896]{1,0:T(8,128)(2,1)S(1)}, bf16[768,896]{1,0:T(8,128)(2,1)}, u32[]{:S(2)}) copy-start(bf16[768,896]{1,0:T(8,128)(2,1)} %copy-done.17) | copy-start | bytes 4128772
  281.0 9.9 %collective-permute-start.23 = (bf16[4,96,768]{2,1,0:T(8,128)(2,1)S(1)}, bf16[4,96,768]{2,1,0:T(8,128)(2,1)S(1)}, u32[]{:S(2)}, u32[]{:S(2)}) collective-permute-start(bf16[4,96,768]{2,1,0:T(8,128)(2,1)S(1)} %dynamic-slice_bitcast_fusion.5), channel_id=1, source_target_pairs={{0,4},{1,5},{2,3},{3,2},{4,0},{5,1},{6,7},{7,6},{8,12},{9,13},{10,... | collective-permute-start | bytes 1769480 | tf_op jit(solution)/shard_map/ppermute | solution.py:45
  285.7 5.2 %copy-start.21 = (bf16[2,4,96,768]{3,2,0,1:T(8,128)(2,1)S(1)}, bf16[2,4,96,768]{3,2,0,1:T(8,128)(2,1)}, u32[]{:S(2)}) copy-start(bf16[2,4,96,768]{3,2,0,1:T(8,128)(2,1)} %add_convert_fusion.5) | copy-start | bytes 3538948
  285.7 6.2 %copy-start.48 = (bf16[1,1024,384]{2,1,0:T(8,128)(2,1)S(1)}, bf16[1,1024,384]{2,1,0:T(8,128)(2,1)}, u32[]{:S(2)}) copy-start(bf16[1,1024,384]{2,1,0:T(8,128)(2,1)} %get-tuple-element.58) | copy-start | bytes 2359300
  288.0 5.8 %copy-start.36 = (bf16[1024,768]{1,0:T(8,128)(2,1)}, bf16[1024,768]{1,0:T(8,128)(2,1)S(1)}, u32[]{:S(2)}) copy-start(bf16[1024,768]{1,0:T(8,128)(2,1)S(1)} %get-tuple-element.76.g_ref) | copy-start | bytes 4718596
  299.4 21.9 %collective-permute-start.24 = (bf16[2,768,1024]{2,1,0:T(8,128)(2,1)}, bf16[2,768,1024]{2,1,0:T(8,128)(2,1)}, u32[]{:S(2)}, u32[]{:S(2)}) collective-permute-start(bf16[2,768,1024]{2,1,0:T(8,128)(2,1)} %broadcast_select_fusion), channel_id=1, source_target_pairs={{0,2},{1,3},{2,0},{3,1},{4,6},{5,7},{6,4},{7,5},{8,10},{9,11},{10,... | collective-permute-start | bytes 9437192 | tf_op jit(solution)/shard_map/ppermute | solution.py:45
  302.8 12.6 %copy-start.39 = (bf16[1024,768]{1,0:T(8,128)(2,1)S(1)}, bf16[1024,768]{1,0:T(8,128)(2,1)}, u32[]{:S(2)}) copy-start(bf16[1024,768]{1,0:T(8,128)(2,1)} %x_ref.3) | copy-start | bytes 4718596
  324.9 12.4 %copy-start.40 = (bf16[1024,768]{1,0:T(8,128)(2,1)S(1)}, bf16[1024,768]{1,0:T(8,128)(2,1)}, u32[]{:S(2)}) copy-start(bf16[1024,768]{1,0:T(8,128)(2,1)} %x_ref.3) | copy-start | bytes 4718596
  340.4 25.7 %collective-permute-start.26 = (bf16[2,4,96,1024]{3,2,0,1:T(8,128)(2,1)S(1)}, bf16[2,4,96,1024]{3,2,0,1:T(8,128)(2,1)S(1)}, u32[]{:S(2)}, u32[]{:S(2)}) collective-permute-start(bf16[2,4,96,1024]{3,2,0,1:T(8,128)(2,1)S(1)} %bitcast_select_fusion), channel_id=1, source_target_pairs={{0,1},{1,0},{2,6},{3,7},{4,5},{5,4},{6,2},{7,3},{8,9},{9,8},{10,14... | collective-permute-start | bytes 4718600 | tf_op jit(solution)/shard_map/ppermute | solution.py:45
  343.8 28.9 %collective-permute-start.25 = (bf16[2,768,640]{1,2,0:T(8,128)(2,1)S(1)}, bf16[2,768,640]{1,2,0:T(8,128)(2,1)S(1)}, u32[]{:S(2)}, u32[]{:S(2)}) collective-permute-start(bf16[2,768,640]{1,2,0:T(8,128)(2,1)S(1)} %broadcast_select_fusion.1), channel_id=1, source_target_pairs={{0,2},{1,3},{2,0},{3,1},{4,6},{5,7},{6,4},{7,5},{8,10},{9,11},{10,... | collective-permute-start | bytes 5898248 | tf_op jit(solution)/shard_map/ppermute | solution.py:45
  345.2 7.7 %copy-start.34 = (bf16[2,4,2,96,640]{4,3,2,1,0:T(8,128)(2,1)S(1)}, bf16[2,4,2,96,640]{4,3,2,1,0:T(8,128)(2,1)}, u32[]{:S(2)}) copy-start(bf16[2,4,2,96,640]{4,3,2,1,0:T(8,128)(2,1)} %copy.113) | copy-start | bytes 5898244
  345.3 7.7 %copy-start.59 = (bf16[1,1024,640]{2,1,0:T(8,128)(2,1)S(1)}, bf16[1,1024,640]{2,1,0:T(8,128)(2,1)}, u32[]{:S(2)}) copy-start(bf16[1,1024,640]{2,1,0:T(8,128)(2,1)} %get-tuple-element.74) | copy-start | bytes 3932164
  346.5 10.2 %collective-permute-start.38 = (bf16[96,768]{1,0:T(8,128)(2,1)S(1)}, bf16[96,768]{1,0:T(8,128)(2,1)S(1)}, u32[]{:S(2)}, u32[]{:S(2)}) collective-permute-start(bf16[96,768]{1,0:T(8,128)(2,1)S(1)} %get-tuple-element.171), channel_id=1, source_target_pairs={{0,24},{1,25},{2,26},{3,27},{4,28},{5,29},{6,30},{7,31},{8,0},{9,1... | collective-permute-start | bytes 442376 | tf_op jit(solution)/shard_map/ppermute | solution.py:45
  352.3 8.6 %collective-permute-start.40 = (bf16[96,768]{1,0:T(8,128)(2,1)S(1)}, bf16[96,768]{1,0:T(8,128)(2,1)S(1)}, u32[]{:S(2)}, u32[]{:S(2)}) collective-permute-start(bf16[96,768]{1,0:T(8,128)(2,1)S(1)} %get-tuple-element.172), channel_id=1, source_target_pairs={{0,8},{1,9},{2,10},{3,11},{4,12},{5,13},{6,14},{7,15},{8,16},{9,17... | collective-permute-start | bytes 442376 | tf_op jit(solution)/shard_map/ppermute | solution.py:45
  352.3 13.6 %collective-permute-start.39 = (bf16[96,768]{1,0:T(8,128)(2,1)S(1)}, bf16[96,768]{1,0:T(8,128)(2,1)S(1)}, u32[]{:S(2)}, u32[]{:S(2)}) collective-permute-start(bf16[96,768]{1,0:T(8,128)(2,1)S(1)} %get-tuple-element.173), channel_id=1, source_target_pairs={{0,16},{1,17},{2,18},{3,19},{4,20},{5,21},{6,22},{7,23},{8,24},{9,... | collective-permute-start | bytes 442376 | tf_op jit(solution)/shard_map/ppermute | solution.py:45
  366.0 6.0 %collective-permute-start.41 = (f32[48,768]{1,0:T(8,128)S(1)}, f32[48,768]{1,0:T(8,128)S(1)}, u32[]{:S(2)}, u32[]{:S(2)}) collective-permute-start(f32[48,768]{1,0:T(8,128)S(1)} %dynamic-slice_bitcast_fusion.11), channel_id=1, source_target_pairs={{0,2},{1,3},{2,0},{3,1},{4,6},{5,7},{6,4},{7,5},{8,10},{9,11},{10,... | collective-permute-start | bytes 442376 | tf_op jit(solution)/shard_map/ppermute | solution.py:45
  368.1 12.3 %collective-permute-start.27 = (bf16[4,96,1024]{2,1,0:T(8,128)(2,1)}, bf16[4,96,1024]{2,1,0:T(8,128)(2,1)}, u32[]{:S(2)}, u32[]{:S(2)}) collective-permute-start(bf16[4,96,1024]{2,1,0:T(8,128)(2,1)} %dynamic-slice_bitcast_fusion.4), channel_id=1, source_target_pairs={{0,4},{1,5},{2,3},{3,2},{4,0},{5,1},{6,7},{7,6},{8,12},{9,13},{10,... | collective-permute-start | bytes 2359304 | tf_op jit(solution)/shard_map/ppermute | solution.py:45
  382.2 6.1 %copy-start.35 = (bf16[2,4,2,96,640]{4,3,2,1,0:T(8,128)(2,1)S(1)}, bf16[2,4,2,96,640]{4,3,2,1,0:T(8,128)(2,1)}, u32[]{:S(2)}) copy-start(bf16[2,4,2,96,640]{4,3,2,1,0:T(8,128)(2,1)} %copy.113) | copy-start | bytes 5898244
  382.2 6.1 %copy-start.56 = (bf16[1,1024,640]{2,1,0:T(8,128)(2,1)S(1)}, bf16[1,1024,640]{2,1,0:T(8,128)(2,1)}, u32[]{:S(2)}) copy-start(bf16[1,1024,640]{2,1,0:T(8,128)(2,1)} %get-tuple-element.82) | copy-start | bytes 3932164
  382.4 20.3 %collective-permute-start.28 = (bf16[2,4,96,640]{3,2,0,1:T(8,128)(2,1)S(1)}, bf16[2,4,96,640]{3,2,0,1:T(8,128)(2,1)S(1)}, u32[]{:S(2)}, u32[]{:S(2)}) collective-permute-start(bf16[2,4,96,640]{3,2,0,1:T(8,128)(2,1)S(1)} %bitcast_select_fusion.4), channel_id=1, source_target_pairs={{0,1},{1,0},{2,6},{3,7},{4,5},{5,4},{6,2},{7,3},{8,9},{9,8},{10,14... | collective-permute-start | bytes 2949128 | tf_op jit(solution)/shard_map/ppermute | solution.py:45
  384.7 10.4 %collective-permute-start.34 = (bf16[96,1024]{1,0:T(8,128)(2,1)S(1)}, bf16[96,1024]{1,0:T(8,128)(2,1)S(1)}, u32[]{:S(2)}, u32[]{:S(2)}) collective-permute-start(bf16[96,1024]{1,0:T(8,128)(2,1)S(1)} %get-tuple-element.168), channel_id=1, source_target_pairs={{0,24},{1,25},{2,26},{3,27},{4,28},{5,29},{6,30},{7,31},{8,0},{9,1... | collective-permute-start | bytes 589832 | tf_op jit(solution)/shard_map/ppermute | solution.py:45
  387.4 9.8 %collective-permute-start.36 = (bf16[96,1024]{1,0:T(8,128)(2,1)S(1)}, bf16[96,1024]{1,0:T(8,128)(2,1)S(1)}, u32[]{:S(2)}, u32[]{:S(2)}) collective-permute-start(bf16[96,1024]{1,0:T(8,128)(2,1)S(1)} %get-tuple-element.169), channel_id=1, source_target_pairs={{0,8},{1,9},{2,10},{3,11},{4,12},{5,13},{6,14},{7,15},{8,16},{9,17... | collective-permute-start | bytes 589832 | tf_op jit(solution)/shard_map/ppermute | solution.py:45
  387.6 14.8 %collective-permute-start.35 = (bf16[96,1024]{1,0:T(8,128)(2,1)S(1)}, bf16[96,1024]{1,0:T(8,128)(2,1)S(1)}, u32[]{:S(2)}, u32[]{:S(2)}) collective-permute-start(bf16[96,1024]{1,0:T(8,128)(2,1)S(1)} %get-tuple-element.170), channel_id=1, source_target_pairs={{0,16},{1,17},{2,18},{3,19},{4,20},{5,21},{6,22},{7,23},{8,24},{9,... | collective-permute-start | bytes 589832 | tf_op jit(solution)/shard_map/ppermute | solution.py:45
  388.3 15.9 %copy-start.30 = (f32[1024,768]{1,0:T(8,128)S(1)}, f32[1024,768]{1,0:T(8,128)}, u32[]{:S(2)}) copy-start(f32[1024,768]{1,0:T(8,128)} %fusion.30) | copy-start | bytes 9437188
  388.3 15.9 %copy-start.31 = (f32[1024,768]{1,0:T(8,128)S(1)}, f32[1024,768]{1,0:T(8,128)}, u32[]{:S(2)}) copy-start(f32[1024,768]{1,0:T(8,128)} %fusion.27) | copy-start | bytes 9437188
  402.6 5.2 %collective-permute-start.37 = (f32[48,1024]{1,0:T(8,128)S(1)}, f32[48,1024]{1,0:T(8,128)S(1)}, u32[]{:S(2)}, u32[]{:S(2)}) collective-permute-start(f32[48,1024]{1,0:T(8,128)S(1)} %dynamic-slice_bitcast_fusion.7), channel_id=1, source_target_pairs={{0,2},{1,3},{2,0},{3,1},{4,6},{5,7},{6,4},{7,5},{8,10},{9,11},{10,... | collective-permute-start | bytes 589832 | tf_op jit(solution)/shard_map/ppermute | solution.py:45
  403.1 8.9 %collective-permute-start.29 = (bf16[4,96,640]{2,1,0:T(8,128)(2,1)S(1)}, bf16[4,96,640]{2,1,0:T(8,128)(2,1)S(1)}, u32[]{:S(2)}, u32[]{:S(2)}) collective-permute-start(bf16[4,96,640]{2,1,0:T(8,128)(2,1)S(1)} %dynamic-slice_bitcast_fusion.6), channel_id=1, source_target_pairs={{0,4},{1,5},{2,3},{3,2},{4,0},{5,1},{6,7},{7,6},{8,12},{9,13},{10,... | collective-permute-start | bytes 1474568 | tf_op jit(solution)/shard_map/ppermute | solution.py:45
  412.2 7.0 %collective-permute-start.30 = (bf16[96,640]{1,0:T(8,128)(2,1)S(1)}, bf16[96,640]{1,0:T(8,128)(2,1)S(1)}, u32[]{:S(2)}, u32[]{:S(2)}) collective-permute-start(bf16[96,640]{1,0:T(8,128)(2,1)S(1)} %get-tuple-element.176), channel_id=1, source_target_pairs={{0,24},{1,25},{2,26},{3,27},{4,28},{5,29},{6,30},{7,31},{8,0},{9,1... | collective-permute-start | bytes 368648 | tf_op jit(solution)/shard_map/ppermute | solution.py:45
  415.4 7.8 %collective-permute-start.32 = (bf16[96,640]{1,0:T(8,128)(2,1)S(1)}, bf16[96,640]{1,0:T(8,128)(2,1)S(1)}, u32[]{:S(2)}, u32[]{:S(2)}) collective-permute-start(bf16[96,640]{1,0:T(8,128)(2,1)S(1)} %get-tuple-element.177), channel_id=1, source_target_pairs={{0,8},{1,9},{2,10},{3,11},{4,12},{5,13},{6,14},{7,15},{8,16},{9,17... | collective-permute-start | bytes 368648 | tf_op jit(solution)/shard_map/ppermute | solution.py:45
  415.4 10.7 %collective-permute-start.31 = (bf16[96,640]{1,0:T(8,128)(2,1)S(1)}, bf16[96,640]{1,0:T(8,128)(2,1)S(1)}, u32[]{:S(2)}, u32[]{:S(2)}) collective-permute-start(bf16[96,640]{1,0:T(8,128)(2,1)S(1)} %get-tuple-element.178), channel_id=1, source_target_pairs={{0,16},{1,17},{2,18},{3,19},{4,20},{5,21},{6,22},{7,23},{8,24},{9,... | collective-permute-start | bytes 368648 | tf_op jit(solution)/shard_map/ppermute | solution.py:45
  426.3 1.4 collective-permute-start.33
  (41 other events, 84.1 us)

commit v4 on v3

v4 whole, which is shorter than its diff:
```python
import functools

import jax
import jax.numpy as jnp
from jax import lax
from jax.experimental import pallas as pl
from jax.experimental.pallas import tpu as pltpu
from jax.sharding import PartitionSpec as P

HDIM = 64
SEQ = 512
LANES = 128
BLOCK = 256
CHUNK = 256
VMEM = 56 * 1024 * 1024
epsilon = 1e-05


def low(value):
    return value.astype(jnp.bfloat16)


AXES = ("dp", "tensor")
ZS = 4


def place(z, x, c, y):
    return ((z * 2 + x) * 2 + c) * 2 + y


def pairs(move):
    found = []
    for z in range(ZS):
        for x in range(2):
            for c in range(2):
                for y in range(2):
                    found.append((place(z, x, c, y), place(*move(z, x, c, y))))
    return found


TO_CORE = pairs(lambda z, x, c, y: (z, x, 1 - c, y))
TO_NEAR = pairs(lambda z, x, c, y: (z, x, c, 1 - y) if c else (z, 1 - x, c, y))
TO_FAR = pairs(lambda z, x, c, y: (z, 1 - x, c, y) if c else (z, x, c, 1 - y))
TO_DEPTH = [pairs(lambda z, x, c, y: ((z - k) % ZS, x, c, y)) for k in range(ZS)]


def coords():
    d = lax.axis_index("dp")
    y = lax.axis_index("tensor")
    return d // 4, (d // 2) % 2, d % 2, y


def send(value, route):
    return lax.ppermute(value, AXES, route)


def in_order(own, other, at):
    return jnp.where(at == 0, jnp.stack([own, other]), jnp.stack([other, own]))


def tuned():
    return lax.axis_size("dp") == 16 and lax.axis_size("tensor") == 2


def after(value, *others):
    return lax.optimization_barrier((value, others))[0]


class Flow:
    def __init__(self, steps):
        self.steps = steps
        self.value = next(steps)

    def go(self, count=1):
        for _ in range(count):
            self.value = self.steps.send(self.value)
        return self.value

    def after(self, *others):
        self.value = after(self.value, *others)


def gather_steps(left, right):
    if not tuned():
        for _ in range(10):
            left = yield left
        full = lax.all_gather(jnp.concatenate([left, right], axis=1), ("tensor", "dp"), axis=0, tiled=True)
        full = full.reshape(2, ZS, 2, -1, full.shape[1])
        left, right = jnp.split(full, 2, axis=4)
        left = jnp.transpose(left, (0, 2, 1, 3, 4))
        right = jnp.transpose(right, (2, 0, 1, 3, 4))
        yield left, right, jnp.zeros((1,), jnp.int32)
        return
    z, x, c, y = coords()
    first = c == 0
    own = yield jnp.where(first, right, left)
    got = yield send(own, TO_CORE)
    mine = jnp.where(first, jnp.concatenate([left, got]), jnp.concatenate([got, right]))
    mine = yield mine
    got = yield [send(mine, TO_DEPTH[k]) for k in (1, 2, 3)]
    column = jnp.stack([mine, *got, mine, *got[:2]])
    column = yield lax.dynamic_slice_in_dim(column, (ZS - z) % ZS, ZS, 0)
    near = yield send(column, TO_NEAR)
    plane = yield in_order(column, near, jnp.where(first, x, y))
    far = yield send(plane, TO_FAR)
    whole = yield in_order(plane, far, jnp.where(first, y, x))
    sibling = yield send(whole, TO_CORE)
    yield whole, sibling, c.astype(jnp.int32).reshape(1)


def add(a, b):
    return a.astype(jnp.float32) + b.astype(jnp.float32)


def pick(value, at):
    return lax.dynamic_index_in_dim(value, at, 0, keepdims=False)


def scatter_steps(part):
    if not tuned():
        left = yield part(jnp.zeros((1,), jnp.int32))
        for _ in range(9):
            left = yield left
        right = part(jnp.ones((1,), jnp.int32))
        left = jnp.transpose(left, (0, 2, 1, 3, 4))
        right = jnp.transpose(right, (1, 2, 0, 3, 4))
        full = jnp.concatenate([left, right], axis=4)
        full = lax.psum_scatter(
            full.reshape(-1, full.shape[4]), ("tensor", "dp"), scatter_dimension=0, tiled=True
        )
        full = lax.optimization_barrier(full).astype(jnp.float32)
        yield tuple(jnp.split(full, 2, axis=1))
        return
    z, x, c, y = coords()
    first = c == 0
    side = c.astype(jnp.int32).reshape(1)
    other = yield part(1 - side)
    got = yield send(other, TO_CORE)
    total = low(add(part(side), got))
    at = jnp.where(first, y, x)
    away = yield pick(total, 1 - at)
    got = yield send(away, TO_FAR)
    total = low(add(pick(total, at), got))
    at = jnp.where(first, x, y)
    away = yield pick(total, 1 - at)
    got = yield send(away, TO_NEAR)
    total = low(add(pick(total, at), got))
    away = yield [pick(total, (z - k) % ZS) for k in (1, 2, 3)]
    got = yield [send(piece, TO_DEPTH[k + 1]) for k, piece in enumerate(away)]
    total = pick(total, z).astype(jnp.float32)
    for piece in got:
        total = total + piece.astype(jnp.float32)
    total = total.reshape(2, -1, total.shape[1])
    away = yield pick(total, 1 - c)
    got = yield send(away, TO_CORE)
    keep = pick(total, c)
    yield jnp.where(first, keep, got), jnp.where(first, got, keep)


def dot_nn(left, right):
    return lax.dot_general(left, right, (((1,), (0,)), ((), ())), preferred_element_type=jnp.float32)


def dot_nt(left, right):
    return lax.dot_general(left, right, (((1,), (1,)), ((), ())), preferred_element_type=jnp.float32)


def flip(value):
    return jnp.swapaxes(value, 0, 1)


def load_set(side_ref, mine_ref, other_ref, left, right, sems, only=None):
    count = mine_ref.shape[3]

    def start(left_ref, right_ref):
        for y in range(2) if only is None else (only,):
            at = y if only is None else 0
            for x in range(2):
                for z in range(ZS):
                    cut = pl.ds((z * 2 + x) * count, count)
                    pltpu.make_async_copy(left_ref.at[y, x, z], left.at[at, cut], sems.at[0]).start()
                    pltpu.make_async_copy(right_ref.at[x, y, z], right.at[at, cut], sems.at[1]).start()

    @pl.when(side_ref[0] == 0)
    def _():
        start(mine_ref, other_ref)

    @pl.when(side_ref[0] != 0)
    def _():
        start(other_ref, mine_ref)


def wait_set(left, right, sems):
    pltpu.make_async_copy(left, left, sems.at[0]).wait()
    pltpu.make_async_copy(right, right, sems.at[1]).wait()


def set_scratch(weights, count=2):
    width, cols = 8 * weights[0].shape[3], weights[0].shape[4]
    buffer = pltpu.VMEM((count, width, cols), jnp.bfloat16)
    return [buffer, buffer, pltpu.SemaphoreType.DMA((2,))]


def set_specs():
    return [
        pl.BlockSpec(memory_space=pltpu.SMEM),
        pl.BlockSpec(memory_space=pl.ANY),
        pl.BlockSpec(memory_space=pl.ANY),
    ]


def set_args(weights):
    return weights[2], weights[0], weights[1]


def params():
    return pltpu.CompilerParams(vmem_limit_bytes=VMEM)


def pair_cols(left, right, at):
    start = at * LANES
    width = left.shape[-1]
    if start < width:
        return left[:, start : start + LANES]
    return right[:, start - width : start - width + LANES]


def attend_kernel(
    t, side_ref, mine_ref, other_ref, x_ref, row_ref, col_ref,
    pa_ref, pb_ref, e_ref, att_ref, flat_ref, inv_ref, bias_ref, a_ref, b_ref, sems,
):
    pairs = flat_ref.shape[2] // LANES

    @pl.when(pl.program_id(0) == 0)
    def _():
        load_set(side_ref, mine_ref, other_ref, a_ref, b_ref, sems, t)
        wait_set(a_ref, b_ref, sems)

    x = x_ref[...]
    pa_ref[0] = low(dot_nn(x, a_ref[0]))
    pb_ref[0] = low(dot_nn(x, b_ref[0, :, : pb_ref.shape[2]]))
    bias_ref[...] = jnp.where(col_ref[0] == row_ref[0], 0.0, -1e30)
    lane = lax.broadcasted_iota(jnp.int32, (SEQ, LANES), 1)
    chunk = SEQ // 2
    left, right = pa_ref[0], pb_ref[0]
    for p in range(pairs):
        queries = pair_cols(left, right, p)
        key_rows = pair_cols(left, right, pairs + p)
        values_flat = flip(pair_cols(left, right, 2 * pairs + p))
        for half in range(2):
            h = 2 * p + half
            own = (lane < HDIM) if half == 0 else (lane >= HDIM)
            chosen = low(jnp.where(own, queries.astype(jnp.float32) * HDIM**-0.5, 0.0))
            value_half = values_flat[half * HDIM : (half + 1) * HDIM]
            for n in range(2):
                cut = slice(n * chunk, (n + 1) * chunk)
                scores = dot_nt(key_rows, chosen[cut]) + bias_ref[:, cut]
                largest = jnp.max(scores, axis=0, keepdims=True)
                weights = jnp.exp(scores - largest)
                inverse = 1.0 / jnp.sum(weights, axis=0, keepdims=True)
                weights = low(weights)
                e_ref[0, h, :, cut] = weights
                inv_ref[0, h : h + 1, cut] = inverse
                flat_ref[0, 0, h * HDIM : (h + 1) * HDIM, cut] = low(dot_nn(value_half, weights) * inverse)
        att_ref[:, p * LANES : (p + 1) * LANES] = flip(flat_ref[0, 0, p * LANES : (p + 1) * LANES, :])
    att_ref[:, pairs * LANES :] = jnp.zeros((SEQ, LANES), jnp.bfloat16)


def attend(tokens, weights, numbers, t):
    rows, width = tokens.shape
    seqs = rows // SEQ
    cols = weights[0].shape[4]
    wide = (2 * cols - LANES) // 3
    heads = wide // HDIM
    used = cols - LANES
    bf = jnp.bfloat16
    return pl.pallas_call(
        functools.partial(attend_kernel, t),
        grid=(seqs,),
        in_specs=set_specs() + [
            pl.BlockSpec((SEQ, width), lambda s: (s, 0)),
            pl.BlockSpec((1, 1, SEQ), lambda s: (s, 0, 0)),
            pl.BlockSpec((1, SEQ, 1), lambda s: (s, 0, 0)),
        ],
        out_specs=[
            pl.BlockSpec((1, SEQ, cols), lambda s: (0, s, 0)),
            pl.BlockSpec((1, SEQ, used), lambda s: (0, s, 0)),
            pl.BlockSpec((1, heads, SEQ, SEQ), lambda s: (s, 0, 0, 0)),
            pl.BlockSpec((SEQ, wide + LANES), lambda s: (s, 0)),
            pl.BlockSpec((1, 1, wide, SEQ), lambda s: (0, s, 0, 0)),
            pl.BlockSpec((1, heads, SEQ), lambda s: (s, 0, 0)),
        ],
        out_shape=[
            jax.ShapeDtypeStruct((1, rows, cols), bf),
            jax.ShapeDtypeStruct((1, rows, used), bf),
            jax.ShapeDtypeStruct((seqs, heads, SEQ, SEQ), bf),
            jax.ShapeDtypeStruct((rows, wide + LANES), bf),
            jax.ShapeDtypeStruct((1, seqs, wide, SEQ), bf),
            jax.ShapeDtypeStruct((seqs, heads, SEQ), jnp.float32),
        ],
        scratch_shapes=[pltpu.VMEM((SEQ, SEQ), jnp.float32)] + set_scratch(weights, 1),
        compiler_params=params(),
        cost_estimate=pl.CostEstimate(flops=8_000_000_000, bytes_accessed=15_000_000, transcendentals=3_100_000),
        name="attend",
    )(*set_args(weights), tokens, numbers.reshape(seqs, 1, SEQ), numbers.reshape(seqs, SEQ, 1))


def attend_back_kernel(
    t, side_ref, mine_ref, other_ref, g_ref, pa_ref, pb_ref, e_ref, flat_ref, inv_ref, d_ref, w_ref, gt_ref, sem,
):
    wide = flat_ref.shape[2]
    pairs = wide // LANES
    count = mine_ref.shape[3]

    @pl.when(pl.program_id(0) == 0)
    def _():
        def start(left_ref):
            for x in range(2):
                for z in range(ZS):
                    pltpu.make_async_copy(
                        left_ref.at[t, x, z], w_ref.at[pl.ds((z * 2 + x) * count, count)], sem
                    ).start()

        @pl.when(side_ref[0] == 0)
        def _():
            start(mine_ref)

        @pl.when(side_ref[0] != 0)
        def _():
            start(other_ref)

        pltpu.make_async_copy(w_ref, w_ref, sem).wait()

    gt_ref[...] = flip(low(dot_nn(g_ref[...], w_ref[:, :wide])))
    left, right = pa_ref[0], pb_ref[0]
    lane = lax.broadcasted_iota(jnp.int32, (SEQ, LANES), 1)
    cols = d_ref.shape[2]

    def put(at, value):
        start = at * LANES
        side = start // cols
        d_ref[side, :, start - side * cols : start - side * cols + LANES] = value

    blank = jnp.zeros((HDIM, SEQ), jnp.bfloat16)
    for p in range(pairs):
        queries = pair_cols(left, right, p)
        key_rows = pair_cols(left, right, pairs + p)
        value_rows = pair_cols(left, right, 2 * pairs + p)
        keys_flat = flip(key_rows)
        scaled = []
        for half in range(2):
            h = 2 * p + half
            grads = gt_ref[h * HDIM : (h + 1) * HDIM, :].astype(jnp.float32)
            scaled.append(low(grads * inv_ref[0, h : h + 1, :]))
        grads = flip(jnp.concatenate(scaled, axis=0))
        dq, dk, dv = [], [], []
        for half in range(2):
            h = 2 * p + half
            mine = scaled[half]
            flat = flat_ref[0, 0, h * HDIM : (h + 1) * HDIM, :].astype(jnp.float32)
            centre = jnp.sum(mine.astype(jnp.float32) * flat, axis=0, keepdims=True)
            stacked = [mine, blank] if half == 0 else [blank, mine]
            grad_weights = dot_nn(value_rows, jnp.concatenate(stacked, axis=0))
            weights = e_ref[0, h]
            grad_scores = low(weights.astype(jnp.float32) * (grad_weights - centre))
            dv.append(dot_nn(weights, grads))
            dk.append(dot_nn(grad_scores, queries))
            dq.append(dot_nn(keys_flat[half * HDIM : (half + 1) * HDIM], grad_scores))
        put(p, flip(low(jnp.concatenate(dq, axis=0) * HDIM**-0.5)))
        put(pairs + p, low(jnp.where(lane < HDIM, dk[0], dk[1]) * HDIM**-0.5))
        put(2 * pairs + p, low(jnp.where(lane < HDIM, dv[0], dv[1])))
    d_ref[1, :, cols - LANES :] = jnp.zeros((SEQ, LANES), jnp.bfloat16)


def attend_back(grad_branch, weights, kept, t):
    pa, pb, e, _, flat, inv = kept
    rows, width = grad_branch.shape
    seqs = rows // SEQ
    cols, used = pa.shape[2], pb.shape[2]
    heads, wide = e.shape[1], flat.shape[2]
    bf = jnp.bfloat16
    return pl.pallas_call(
        functools.partial(attend_back_kernel, t),
        grid=(seqs,),
        in_specs=set_specs() + [
            pl.BlockSpec((SEQ, width), lambda s: (s, 0)),
            pl.BlockSpec((1, SEQ, cols), lambda s: (0, s, 0)),
            pl.BlockSpec((1, SEQ, used), lambda s: (0, s, 0)),
            pl.BlockSpec((1, heads, SEQ, SEQ), lambda s: (s, 0, 0, 0)),
            pl.BlockSpec((1, 1, wide, SEQ), lambda s: (0, s, 0, 0)),
            pl.BlockSpec((1, heads, SEQ), lambda s: (s, 0, 0)),
        ],
        out_specs=pl.BlockSpec((2, SEQ, cols), lambda s: (0, s, 0)),
        out_shape=jax.ShapeDtypeStruct((2, rows, cols), bf),
        scratch_shapes=[
            pltpu.VMEM((width, weights[0].shape[4]), bf),
            pltpu.VMEM((wide, SEQ), bf),
            pltpu.SemaphoreType.DMA,
        ],
        compiler_params=params(),
        cost_estimate=pl.CostEstimate(flops=8_000_000_000, bytes_accessed=15_000_000, transcendentals=0),
        name="attend_back",
    )(*set_args(weights), grad_branch, pa, pb, e, flat, inv)


def gelu_parts(v):
    size = jnp.abs(v)
    base = 1.0 + (0.3275911 * 0.5**0.5) * size
    near = pl.reciprocal(base, approx=True)
    t = near * (2.0 - base * near)
    bell = jnp.exp(-0.5 * (v * v))
    tail = t * (0.127414796 + t * (-0.142248368 + t * (0.710706871 + t * (-0.7265760135 + t * 0.5307027145)))) * bell
    below = jnp.where(v >= 0.0, 1.0 - tail, tail)
    return v * below, below + 0.3989422804014327 * (v * bell)


def row_norm(value):
    centered = value - jnp.mean(value, axis=-1, keepdims=True)
    inverse = lax.rsqrt(jnp.mean(centered * centered, axis=-1, keepdims=True) + epsilon)
    return centered * inverse, inverse


def row_norm_back(grad_scaled, scaled, inverse):
    centered = grad_scaled - jnp.mean(grad_scaled, axis=-1, keepdims=True)
    return inverse * (centered - scaled * jnp.mean(grad_scaled * scaled, axis=-1, keepdims=True))


def pieces(left, right, skip):
    at = 0
    for t in range(2):
        for ref, start, end in ((left, skip, left.shape[2]), (right, 0, right.shape[2] - (LANES if skip else 0))):
            while start < end:
                size = min(CHUNK, end - start)
                yield ref.at[t, :, pl.ds(start, size)], slice(at, at + size)
                start, at = start + size, at + size


def widen_kernel(
    side_ref, mine_ref, other_ref, x_ref, u_ref, v_ref, n_ref,
    sum_ref, low_ref, hid_ref, slope_ref, left, right, sems,
):
    wide = u_ref.shape[1] - LANES

    @pl.when(pl.program_id(0) == 0)
    def _():
        load_set(side_ref, mine_ref, other_ref, left, right, sems)
        wait_set(left, right, sems)

    branch = dot_nt(u_ref[:, :wide], left[0, :, :wide]) + dot_nt(v_ref[:, :wide], left[1, :, :wide])
    total = x_ref[...].astype(jnp.float32) + branch
    sum_ref[...] = total
    scaled, _ = row_norm(total)
    x = low(scaled * n_ref[0:1, :] + n_ref[1:2, :])
    low_ref[...] = flip(x)
    for ref, cut in pieces(left, right, wide):
        value, slope = gelu_parts(dot_nn(x, ref[...]))
        hid_ref[:, cut] = low(value)
        slope_ref[:, cut] = low(slope)


def widen(tokens, attended, weights, norms, span):
    rows, width = tokens.shape
    bf = jnp.bfloat16
    by_row = lambda n: pl.BlockSpec((BLOCK, n), lambda r: (r, 0))
    full = lambda a: pl.BlockSpec(a.shape, lambda r: (0, 0))
    side = by_row(attended[0].shape[1])
    return pl.pallas_call(
        widen_kernel,
        grid=(rows // BLOCK,),
        in_specs=set_specs() + [by_row(width), side, side, full(norms)],
        out_specs=[by_row(width), pl.BlockSpec((width, BLOCK), lambda r: (0, r)), by_row(span), by_row(span)],
        out_shape=[
            jax.ShapeDtypeStruct((rows, width), jnp.float32),
            jax.ShapeDtypeStruct((width, rows), bf),
            jax.ShapeDtypeStruct((rows, span), bf),
            jax.ShapeDtypeStruct((rows, span), bf),
        ],
        scratch_shapes=set_scratch(weights),
        compiler_params=params(),
        cost_estimate=pl.CostEstimate(flops=12_000_000_000, bytes_accessed=25_000_000, transcendentals=3_100_000),
        name="widen",
    )(*set_args(weights), tokens, *attended, norms)


def middle_kernel(
    side_ref, mine_ref, other_ref, side_two_ref, mine_two_ref, other_two_ref,
    sum_ref, hid_ref, slope_ref, n_ref, cot_ref,
    out_ref, gs_ref, gi_ref, res_ref, gb_ref, gbt_ref, stat_ref,
    left, right, sems, win_left, win_right, win_sems,
):
    @pl.when(pl.program_id(0) == 0)
    def _():
        load_set(side_ref, mine_ref, other_ref, left, right, sems)
        load_set(side_two_ref, mine_two_ref, other_two_ref, win_left, win_right, win_sems)
        wait_set(left, right, sems)

    gain_one, shift_one = n_ref[0:1, :], n_ref[1:2, :]
    gain_two, shift_two = n_ref[2:3, :], n_ref[3:4, :]
    scaled_one, inverse_one = row_norm(sum_ref[...])
    value = scaled_one * gain_one + shift_one
    half = left.shape[2]
    for t in range(2):
        for i, ref in enumerate((left, right)):
            start = (2 * t + i) * half
            value = value + dot_nt(hid_ref[:, start : start + half], ref[t])
    scaled_two, inverse_two = row_norm(value)
    out_ref[...] = low(scaled_two * gain_two + shift_two)
    cotangent = cot_ref[...].astype(jnp.float32)
    grad_two = row_norm_back(cotangent * gain_two, scaled_two, inverse_two)
    grad_second = low(grad_two)
    gs_ref[...] = flip(grad_second)
    for ref, cut in pieces(left, right, 0):
        gi_ref[:, cut] = low(dot_nn(grad_second, ref[...]) * slope_ref[:, cut].astype(jnp.float32))

    @pl.when(pl.program_id(0) == 0)
    def _():
        wait_set(win_left, win_right, win_sems)
        stat_ref[...] = jnp.zeros_like(stat_ref)

    grad_first = grad_two
    skip = 2 * win_left.shape[2] - LANES - gi_ref.shape[1] // 2
    at = 0
    for t in range(2):
        for ref, start, end in ((win_left, skip, win_left.shape[2]), (win_right, 0, win_right.shape[2] - LANES)):
            grad_first = grad_first + dot_nt(gi_ref[:, at : at + end - start], ref[t, :, start:end])
            at += end - start
    grad_one = row_norm_back(grad_first * gain_one, scaled_one, inverse_one)
    res_ref[...] = grad_one
    gb_ref[...] = low(grad_one)
    gbt_ref[...] = flip(low(grad_one))
    for row, value in enumerate((grad_first * scaled_one, grad_first, cotangent * scaled_two, cotangent)):
        stat_ref[row : row + 1, :] += jnp.sum(value, axis=0, keepdims=True)


def middle(total, hidden, slope, weights_down, weights_in, norms, cotangent):
    rows, width = total.shape
    span = hidden.shape[1]
    bf = jnp.bfloat16
    by_row = lambda n: pl.BlockSpec((BLOCK, n), lambda r: (r, 0))
    by_col = pl.BlockSpec((width, BLOCK), lambda r: (0, r))
    full = lambda a: pl.BlockSpec(a.shape, lambda r: (0, 0))
    return pl.pallas_call(
        middle_kernel,
        grid=(rows // BLOCK,),
        in_specs=set_specs() * 2 + [by_row(width), by_row(span), by_row(span), full(norms), by_row(width)],
        out_specs=[by_row(width), by_col, by_row(span), by_row(width), by_row(width), by_col, full(norms)],
        out_shape=[
            jax.ShapeDtypeStruct((rows, width), bf),
            jax.ShapeDtypeStruct((width, rows), bf),
            jax.ShapeDtypeStruct((rows, span), bf),
            jax.ShapeDtypeStruct((rows, width), jnp.float32),
            jax.ShapeDtypeStruct((rows, width), bf),
            jax.ShapeDtypeStruct((width, rows), bf),
            jax.ShapeDtypeStruct(norms.shape, jnp.float32),
        ],
        scratch_shapes=set_scratch(weights_down) + set_scratch(weights_in),
        compiler_params=params(),
        cost_estimate=pl.CostEstimate(flops=22_000_000_000, bytes_accessed=40_000_000, transcendentals=0),
        name="middle",
    )(*set_args(weights_down), *set_args(weights_in), total, hidden, slope, norms, cotangent)


def put_rows(out_ref, side, t, value, cut):
    count = out_ref.shape[3]
    for x in range(2):
        a = jnp.where(side == 0, t, x)
        b = jnp.where(side == 0, x, t)
        for z in range(ZS):
            start = (z * 2 + x) * count
            out_ref[a, b, z, :, cut] = value[start : start + count]


def weigh_kernel(side_ref, a_ref, b_ref, out_ref):
    side, t = side_ref[0], pl.program_id(0)
    put_rows(out_ref, side, t, low(dot_nn(a_ref[...], b_ref[...])), slice(None))


def weigh_more_kernel(side_ref, a_ref, b_ref, c_ref, u_ref, v_ref, out_ref):
    side, t = side_ref[0], pl.program_id(0)
    cols = b_ref.shape[1]
    put_rows(out_ref, side, t, low(dot_nn(a_ref[...], b_ref[...])), slice(0, cols))
    chosen = jnp.where(t == 0, u_ref[...], v_ref[...])
    put_rows(out_ref, side, t, low(dot_nn(c_ref[...], chosen)), slice(cols, out_ref.shape[4]))


def weigh_last_kernel(side_ref, a_ref, u_ref, v_ref, s_ref, out_ref):
    side, t = side_ref[0], pl.program_id(0)
    chosen = jnp.where(t == 0, u_ref[0], v_ref[0])
    value = low(dot_nn(a_ref[...], chosen))
    edge = out_ref.shape[4] - LANES
    put_rows(out_ref, side, t, value[:, :edge], slice(0, edge))
    put_rows(out_ref, side, t, jnp.where(side == 0, value[:, edge:], s_ref[...]), slice(edge, edge + LANES))


def weigh_call(kernel, specs, cols, flops, side, *args):
    width = args[0].shape[0]
    shape = (2, 2, ZS, width // (2 * ZS), cols)
    return pl.pallas_call(
        kernel,
        grid_spec=pltpu.PrefetchScalarGridSpec(
            num_scalar_prefetch=1,
            grid=(2,),
            in_specs=specs,
            out_specs=pl.BlockSpec(shape, lambda t, side: (0, 0, 0, 0, 0)),
        ),
        out_shape=jax.ShapeDtypeStruct(shape, jnp.bfloat16),
        compiler_params=params(),
        cost_estimate=pl.CostEstimate(flops=flops, bytes_accessed=8_000_000, transcendentals=0),
        name="weigh",
    )(side, *args)


def whole_spec(value):
    return pl.BlockSpec(value.shape, lambda t, side: (0,) * value.ndim)


def weigh(flat, value, side):
    cols = value.shape[1] // 4
    specs = [whole_spec(flat), pl.BlockSpec((value.shape[0], cols), lambda t, side: (0, 2 * t + side[0]))]
    return weigh_call(weigh_kernel, specs, cols, 2_500_000_000, side, flat, value)


def weigh_more(flat, value, flat_two, attended, side):
    cols = value.shape[1] // 4
    more = attended[0].shape[1] // 2
    extra = pl.BlockSpec((value.shape[0], more), lambda t, side: (0, side[0]))
    specs = [
        whole_spec(flat),
        pl.BlockSpec((value.shape[0], cols), lambda t, side: (0, 2 * t + side[0])),
        whole_spec(flat_two), extra, extra,
    ]
    return weigh_call(
        weigh_more_kernel, specs, cols + more, 3_500_000_000, side, flat, value, flat_two, *attended
    )


def weigh_last(flat, parts, stats, side):
    _, rows, cols = parts[0].shape
    spec = pl.BlockSpec((1, rows, cols), lambda t, side: (side[0], 0, 0))
    specs = [whole_spec(flat), spec, spec, whole_spec(stats)]
    return weigh_call(weigh_last_kernel, specs, cols, 2_500_000_000, side, flat, *parts, stats)


def input_kernel(side_ref, mine_ref, other_ref, res_ref, u_ref, v_ref, out_ref, left, right, sems):
    @pl.when(pl.program_id(0) == 0)
    def _():
        load_set(side_ref, mine_ref, other_ref, left, right, sems)
        wait_set(left, right, sems)

    total = res_ref[...]
    for t, ref in enumerate((u_ref, v_ref)):
        total = total + dot_nt(ref[0], left[t]) + dot_nt(ref[1], right[t])
    out_ref[...] = low(total)


def input_back(resid, parts, weights):
    rows, width = resid.shape
    cols = parts[0].shape[2]
    by_row = pl.BlockSpec((BLOCK, width), lambda r: (r, 0))
    side = pl.BlockSpec((2, BLOCK, cols), lambda r: (0, r, 0))
    return pl.pallas_call(
        input_kernel,
        grid=(rows // BLOCK,),
        in_specs=set_specs() + [by_row, side, side],
        out_specs=by_row,
        out_shape=jax.ShapeDtypeStruct((rows, width), jnp.bfloat16),
        scratch_shapes=set_scratch(weights),
        compiler_params=params(),
        cost_estimate=pl.CostEstimate(flops=4_000_000_000, bytes_accessed=14_000_000, transcendentals=0),
        name="input_back",
    )(*set_args(weights), resid, *parts)


def halves(value):
    return jnp.split(value, 2, axis=-1)


def shards(
    tokens,
    segment,
    weight_qkv,
    weight_out,
    weight_in,
    weight_down,
    gain_one,
    shift_one,
    gain_two,
    shift_two,
    cotangent,
):
    rows, width = tokens.shape
    own = weight_qkv.shape[1]
    wide = weight_out.shape[0]
    half_span = weight_in.shape[1]
    bf = jnp.bfloat16

    norms = jnp.stack([gain_one, shift_one, gain_two, shift_two], axis=1)
    norms = jnp.pad(norms, ((0, 0), (0, LANES - 4)))
    set_one = jnp.concatenate([jnp.transpose(weight_qkv, (1, 0, 2)).reshape(own, -1), norms], axis=1)
    set_two = jnp.concatenate([weight_out.T, weight_in, jnp.zeros((own, LANES), bf)], axis=1)
    one = Flow(gather_steps(*halves(set_one)))
    two = Flow(gather_steps(*halves(set_two)))
    three = Flow(gather_steps(*halves(weight_down.T)))
    one.go(2)
    two.go(2)
    three.go(2)
    one.go()
    column = one.go()
    one.go()
    two.after(column)
    two.go()
    one.go()
    one.go()
    three.after(two.go())
    three.go()
    whole = one.go()
    one.go()
    two.after(whole)
    wait_two = two.value
    two.go()
    wait_three = three.go()
    three.after(whole)
    three.go()
    weights_one = one.go()
    first_mine, first_other, first_side = weights_one
    norms = jnp.where(first_side[0] == 0, first_other, first_mine)[:, 0, :, :, first_mine.shape[4] - LANES :]
    norms = jnp.transpose(norms, (1, 0, 2, 3)).reshape(width, LANES)[:, :8].T.astype(jnp.float32)

    numbers = lax.dynamic_slice_in_dim(segment, lax.axis_index("tensor") * rows, rows)
    numbers = numbers.reshape(rows // SEQ, SEQ)
    kept = [attend(after(tokens, wait_two, wait_three), weights_one, numbers, 0)]
    two.after(kept[0])
    plane = two.go()
    two.go()
    three.after(kept[0])
    kept.append(attend(after(tokens, plane, kept[0][3]), weights_one, numbers, 1))
    two.after(kept[1])
    whole = two.go()
    two.go()
    three.go()
    three.after(whole)
    three.go()
    weights_two = two.go()
    attended = [kept[t][3] for t in range(2)]
    total, low_flat, hidden, slope = widen(tokens, attended, weights_two, norms, 2 * half_span)
    three.after(hidden)
    three.go(2)
    weights_three = three.go()
    output, second_flat, grad_inner, grad_resid_one, grad_branch, branch_flat, stats = middle(
        total, hidden, slope, weights_three, weights_two, norms, cotangent
    )

    put_three = Flow(scatter_steps(lambda side: weigh(second_flat, hidden, side)))
    ready = put_three.value
    put_three.go()
    low_flat = after(low_flat, ready)
    put_two = Flow(scatter_steps(lambda side: weigh_more(low_flat, grad_inner, branch_flat, attended, side)))
    put_two.go()
    put_three.go()
    put_three.go()
    ready = put_two.go()
    put_two.go()
    parts = [attend_back(after(grad_branch, ready), weights_two, kept[0], 0)]
    put_three.after(parts[0])
    ready = put_three.go()
    put_three.go()
    parts.append(attend_back(after(grad_branch, ready), weights_two, kept[1], 1))
    put_two.after(parts[1])
    put_three.after(parts[1])
    ready = put_two.go()
    put_two.go()
    put_three.go()
    put_three.go()
    tokens_flat = after(tokens.T, ready)
    stats = jnp.pad(low(stats.T), ((0, 0), (0, LANES - stats.shape[0])))
    put_one = Flow(scatter_steps(lambda side: weigh_last(tokens_flat, parts, stats, side)))
    put_one.go()
    ready = put_one.go()
    put_one.go()
    put_two.after(ready)
    put_two.go()
    put_two.go()
    input_grad = input_back(after(grad_resid_one, ready), parts, weights_one)
    put_three.after(ready)
    put_three.go(2)
    put_one.after(input_grad)
    put_one.go()
    put_one.go()
    put_one.go()
    put_one.go()
    put_two.go(2)
    put_one.go(2)
    sum_one = jnp.concatenate(put_one.go(), axis=1)
    two_left, two_right = put_two.go()
    sum_three = jnp.concatenate(put_three.go(), axis=1)
    half = half_span // 2
    stats = sum_one[:, 3 * wide : 3 * wide + 4].T
    sum_out = jnp.concatenate([two_left[:, half:], two_right[:, half:]], axis=1)[:, :wide]
    return (
        output,
        input_grad,
        jnp.transpose(sum_one[:, : 3 * wide].reshape(own, 3, -1), (1, 0, 2)),
        sum_out.T,
        jnp.concatenate([two_left[:, :half], two_right[:, :half]], axis=1),
        sum_three.T,
        stats[0],
        stats[1],
        stats[2],
        stats[3],
    )


def solution(mesh):
    both = P(("dp", "tensor"), None)
    split = P("dp")
    qkv_spec = P(None, "dp", "tensor")
    row_spec = P("tensor", "dp")
    in_spec = P("dp", "tensor")
    return jax.shard_map(
        shards,
        mesh=mesh,
        in_specs=(both, split, qkv_spec, row_spec, in_spec, row_spec, split, split, split, split, both),
        out_specs=(both, both, qkv_spec, row_spec, in_spec, row_spec, split, split, split, split),
        check_vma=False,
    )
```

time: 433 us -> 347 us (0.80)
  Pallas kernels: 75.2 us -> 171 us
  matrix products: 68.6 us -> 0 us
  local copies, waits for them, and re-layouts: 62.5 us -> 16 us
  waiting for transfers between devices: 113 us -> 79.2 us
  other arithmetic: 55.6 us -> 27 us
    pallas_call x5 -> x13, Pallas kernels: 75.2 us -> 171 us  [the longest x6 41.8 us: weigh_call(): pl.pallas_call(kernel, grid_spec=pltpu.PrefetchScalarGridSpec(num_scalar_...]
    dot_general x17 -> x0, matrix products: 68.6 us -> none  [the longest x8 28.8 us: dot_nt(): lax.dot_general(left, right, (((1,), (1,)), ((), ())), preferred_element_...]
    ppermute x42, waiting for transfers between devices: 113 us -> 79.2 us  [send(): return lax.ppermute(value, AXES, route)]
    slice x23 -> x4, local copies, waits for them, and re-layouts: 20 us -> 0.03 us  [the longest x1 0.01 us: shards(): two_left[:, :half]]
    unnamed x143 -> x43, local copies, waits for them, and re-layouts: 18.9 us -> 7 us
    reshape x2 -> x1, local copies, waits for them, and re-layouts: 11.7 us -> 0.09 us  [shards(): sum_one[:, :3 * wide].reshape(own, 3, -1)]
    convert_element_type x11 -> x10, other arithmetic: 20.5 us -> 14.1 us  [low(): return value.astype(jnp.bfloat16)]
    reduce_sum x4 -> x0, other arithmetic: 5.42 us -> none  [the longest x1 2.72 us: norm_back(): jnp.mean(grad_scaled * scaled, axis=-1, keepdims=True)]
  transfers between devices with their start and end apart: 42 -> 42, of which waited for: 24 -> 16; matrix products, arithmetic and copies ran while one was open for 18% -> 9% of each run, Pallas kernels for 15% -> 34%
where the time goes in v4:
time: 347 us; the launch traced here: 344 us
  Pallas kernels  171 us (49%)
  waiting for transfers between devices  79.2 us (23%)
  starting transfers between devices  48.6 us (14%)
  other arithmetic  27 us (8%)
  local copies, waits for them, and re-layouts  16 us (5%)
    ppermute x42, waiting for transfers between devices, send(): return lax.ppermute(value, AXES, route)  79.2 us
    ppermute x42, starting transfers between devices, send(): return lax.ppermute(value, AXES, route)  48.6 us
    pallas_call x6, Pallas kernels, weigh_call(): pl.pallas_call(kernel, grid_spec=pltpu.PrefetchScalarGridSpec(num_scalar_...  41.8 us
    pallas_call x1, Pallas kernels, middle(): pl.pallas_call(middle_kernel, grid=(rows // BLOCK,), in_specs=set_specs()...  33 us
    pallas_call x2, Pallas kernels, attend(): pl.pallas_call(functools.partial(attend_kernel, t), grid=(seqs,), in_spec...  32.6 us
    pallas_call x2, Pallas kernels, attend_back(): pl.pallas_call(functools.partial(attend_back_kernel, t), grid=(seqs,), in...  26.6 us
    pallas_call x1, Pallas kernels, widen(): pl.pallas_call(widen_kernel, grid=(rows // BLOCK,), in_specs=set_specs()...  26.5 us
    convert_element_type x10, other arithmetic, low(): return value.astype(jnp.bfloat16)  14.1 us
  transfers between devices with their start and end apart: 42, of which 16 were waited for; matrix products, arithmetic and copies ran while one was open for 9% of the time, Pallas kernels for 34%

profile of v4, /device:TPU:0, one launch (start us, length us, event | category | flops | bytes accessed | tf_op | source)
XLA Modules:
  0.0 343.6 jit_solution(8873688626531139523)
XLA Ops:
  0.7 0.9 copy.51
  3.0 1.0 broadcast_select_fusion
  4.1 0.9 fusion.17
  5.5 1.1 reshape_reshape.10.col_ref
  6.7 4.8 %collective-permute-start.3 = (bf16[96,640]{1,0:T(8,128)(2,1)S(1)}, bf16[96,640]{1,0:T(8,128)(2,1)S(1)}, u32[]{:S(2)}, u32[]{:S(2)}) collective-permute-start(bf16[96,640]{1,0:T(8,128)(2,1)S(1)} %maximum_select_fusion.11), channel_id=1, source_target_pairs={{0,24},{1,25},{2,26},{3,27},{4,28},{5,29},{6,30},{7,31},{8,0},{9,1... | collective-permute-start | bytes 368648 | tf_op jit(solution)/shard_map/ppermute | solution.py:54
  11.5 1.0 collective-permute-start.5
  12.7 2.6 collective-permute-done.3
  15.3 7.7 %collective-permute-done.4 = bf16[96,640]{1,0:T(8,128)(2,1)S(1)} collective-permute-done((bf16[96,640]{1,0:T(8,128)(2,1)S(1)}, bf16[96,640]{1,0:T(8,128)(2,1)S(1)}, u32[]{:S(2)}, u32[]{:S(2)}) %collective-permute-start.4) | collective-permute-done | bytes 122912 | tf_op jit(solution)/shard_map/ppermute | solution.py:54
  23.2 1.6 collective-permute-start.12
  24.8 1.4 collective-permute-start.6
  26.2 1.0 collective-permute-start.7
  27.2 1.9 collective-permute-start.8
  29.2 2.8 collective-permute-done.6
  32.3 1.6 collective-permute-start.13
  33.9 10.0 %collective-permute-done.7 = bf16[96,1024]{1,0:T(8,128)(2,1)S(1)} collective-permute-done((bf16[96,1024]{1,0:T(8,128)(2,1)S(1)}, bf16[96,1024]{1,0:T(8,128)(2,1)S(1)}, u32[]{:S(2)}, u32[]{:S(2)}) %collective-permute-start.7) | collective-permute-done | bytes 196640 | tf_op jit(solution)/shard_map/ppermute | solution.py:54
  44.2 2.3 collective-permute-done.13
  47.0 3.9 %collective-permute-start.9 = (bf16[96,768]{1,0:T(8,128)(2,1)S(1)}, bf16[96,768]{1,0:T(8,128)(2,1)S(1)}, u32[]{:S(2)}, u32[]{:S(2)}) collective-permute-start(bf16[96,768]{1,0:T(8,128)(2,1)S(1)} %maximum_select_fusion.9), channel_id=1, source_target_pairs={{0,24},{1,25},{2,26},{3,27},{4,28},{5,29},{6,30},{7,31},{8,0},{9,1... | collective-permute-start | bytes 442376 | tf_op jit(solution)/shard_map/ppermute | solution.py:54
  50.9 7.4 %collective-permute-start.10 = (bf16[96,768]{1,0:T(8,128)(2,1)S(1)}, bf16[96,768]{1,0:T(8,128)(2,1)S(1)}, u32[]{:S(2)}, u32[]{:S(2)}) collective-permute-start(bf16[96,768]{1,0:T(8,128)(2,1)S(1)} %maximum_select_fusion.9), channel_id=1, source_target_pairs={{0,16},{1,17},{2,18},{3,19},{4,20},{5,21},{6,22},{7,23},{8,24},{9,... | collective-permute-start | bytes 442376 | tf_op jit(solution)/shard_map/ppermute | solution.py:54
  58.8 2.6 collective-permute-done.9
  61.4 10.6 %collective-permute-done.10 = bf16[96,768]{1,0:T(8,128)(2,1)S(1)} collective-permute-done((bf16[96,768]{1,0:T(8,128)(2,1)S(1)}, bf16[96,768]{1,0:T(8,128)(2,1)S(1)}, u32[]{:S(2)}, u32[]{:S(2)}) %collective-permute-start.10) | collective-permute-done | bytes 147488 | tf_op jit(solution)/shard_map/ppermute | solution.py:54
  73.1 1.3 copy-done.8
  74.4 16.3 %attend.2 = (bf16[1,1024,640]{2,1,0:T(8,128)(2,1)}, bf16[1,1024,512]{2,1,0:T(8,128)(2,1)}, bf16[2,6,512,512]{3,2,1,0:T(8,128)(2,1)}, bf16[1024,512]{1,0:T(8,128)...) custom-call(s32[1]{0:T(128)} %bitcast.side_ref.side_two_ref, bf16[2,2,4,96,640]{4,3,2,1,0:T(8,128)(2,1)} %copy-done.3, ...), custom_call_target="tpu_custom_call" | custom-call | flops 8000000000 | bytes 15000000 | tf_op jit(solution)/shard_map/attend/pallas_call | solution.py:277
  91.0 2.1 collective-permute-start.17
  93.3 16.3 %attend.3 = (bf16[1,1024,640]{2,1,0:T(8,128)(2,1)}, bf16[1,1024,512]{2,1,0:T(8,128)(2,1)}, bf16[2,6,512,512]{3,2,1,0:T(8,128)(2,1)}, bf16[1024,512]{1,0:T(8,128)...) custom-call(s32[1]{0:T(128)} %bitcast.side_ref.side_two_ref, bf16[2,2,4,96,640]{4,3,2,1,0:T(8,128)(2,1)} %copy-done.3, ...), custom_call_target="tpu_custom_call" | custom-call | flops 8000000000 | bytes 15000000 | tf_op jit(solution)/shard_map/attend/pallas_call | solution.py:277
  109.6 1.8 collective-permute-done.17
  112.1 2.1 collective-permute-start.14
  114.1 1.1 fusion.12
  115.3 7.0 %collective-permute-done.14 = bf16[4,96,768]{2,1,0:T(8,128)(2,1)} collective-permute-done((bf16[4,96,768]{2,1,0:T(8,128)(2,1)}, bf16[4,96,768]{2,1,0:T(8,128)(2,1)}, u32[]{:S(2)}, u32[]{:S(2)}) %collective-permute-start.14) | collective-permute-done | bytes 589856 | tf_op jit(solution)/shard_map/ppermute | solution.py:54
  122.3 1.9 maximum_select_fusion.5
  124.3 2.1 collective-permute-start.18
  127.0 26.5 %widen.1 = (f32[1024,768]{1,0:T(8,128)}, bf16[768,1024]{1,0:T(8,128)(2,1)}, bf16[1024,3072]{1,0:T(8,128)(2,1)}, bf16[1024,3072]{1,0:T(8,128)(2,1)}) custom-call(s32[1]{0:T(128)} %bitcast.side_ref.side_two_ref, bf16[2,2,4,96,1024]{4,3,2,1,0:T(8,128)(2,1)} %copy-done.2, bf16[2,2,4,96,1024]{4,3,2,1,0:T(8,128)(2,1)} %collective-permute-done.19.other_ref.other_two_ref, ...), custom_call_target="tpu_custom_call" | custom-call | flops 12000000000 | bytes 25000000 | tf_op jit(solution)/shard_map/widen/pallas_call | solution.py:467
  154.0 4.5 %collective-permute-done.20.other_ref = bf16[2,2,4,96,768]{4,3,2,1,0:T(8,128)(2,1)S(1)} collective-permute-done((bf16[2,2,4,96,768]{4,3,2,1,0:T(8,128)(2,1)S(1)}, bf16[2,2,4,96,768]{4,3,2,1,0:T(8,128)(2,1)S(1)}, u32[]{:S(2)}, u32[]{:S(2)}) %collective-permute-start.20) | collective-permute-done | bytes 2359328 | tf_op jit(solution)/shard_map/ppermute | solution.py:54
  158.5 1.4 copy-done.11
  159.9 33.0 %middle.1 = (bf16[1024,768]{1,0:T(8,128)(2,1)}, bf16[768,1024]{1,0:T(8,128)(2,1)}, bf16[1024,3072]{1,0:T(8,128)(2,1)}, f32[1024,768]{1,0:T(8,128)}, bf16[1024,76...) custom-call(s32[1]{0:T(128)} %bitcast.side_ref.side_two_ref, bf16[2,2,4,96,768]{4,3,2,1,0:T(8,128)(2,1)} %copy-done.5, ...), custom_call_target="tpu_custom_call" | custom-call | flops 22000001024 | bytes 40000000 | tf_op jit(solution)/shard_map/middle/pallas_call | solution.py:542
  192.9 6.2 %weigh.6 = bf16[2,2,4,96,768]{4,3,2,1,0:T(8,128)(2,1)} custom-call(s32[1]{0:T(128)S(6)} %sub.60.side_ref, bf16[768,1024]{1,0:T(8,128)(2,1)} %get-tuple-element.86.a_ref, bf16[1024,3072]{1,0:T(8,128)(2,1)} %get-tuple-element.79.hid_ref.b_ref), custom_call_target="tpu_custom_call" | custom-call | flops 2500000000 | bytes 8000000 | tf_op jit(solution)/shard_map/weigh/pallas_call | solution.py:598
  199.1 8.4 %weigh.8 = bf16[2,2,4,96,1024]{4,3,2,1,0:T(8,128)(2,1)} custom-call(s32[1]{0:T(128)S(6)} %sub.60.side_ref, bf16[768,1024]{1,0:T(8,128)(2,1)} %get-tuple-element.87.a_ref, bf16[1024,3072]{1,0:T(8,128)(2,1)} %get-tuple-element.88.b_ref, bf16[768,1024]{1,0:T(8,128)(2,1)} %get-tuple-element.89.c_ref, bf16[1024,512]{1,0:T(8,128)(2,1)} %get-tuple-element.65.u_ref, ...), custom_call_target="tpu_custom_call" | custom-call | flops 3500000000 | bytes 8000000 | tf_op jit(solution)/shard_map/weigh/pallas_call | solution.py:598
  208.0 2.6 copy.47
  211.5 6.1 %weigh.9 = bf16[2,2,4,96,768]{4,3,2,1,0:T(8,128)(2,1)} custom-call(s32[1]{0:T(128)} %bitcast.side_ref.side_two_ref, bf16[768,1024]{1,0:T(8,128)(2,1)} %get-tuple-element.86.a_ref, bf16[1024,3072]{1,0:T(8,128)(2,1)} %get-tuple-element.79.hid_ref.b_ref), custom_call_target="tpu_custom_call" | custom-call | flops 2500000000 | bytes 8000000 | tf_op jit(solution)/shard_map/weigh/pallas_call | solution.py:598
  217.6 8.2 %weigh.7 = bf16[2,2,4,96,1024]{4,3,2,1,0:T(8,128)(2,1)} custom-call(s32[1]{0:T(128)} %bitcast.side_ref.side_two_ref, bf16[768,1024]{1,0:T(8,128)(2,1)} %get-tuple-element.87.a_ref, bf16[1024,3072]{1,0:T(8,128)(2,1)} %get-tuple-element.88.b_ref, bf16[768,1024]{1,0:T(8,128)(2,1)} %get-tuple-element.89.c_ref, bf16[1024,512]{1,0:T(8,128)(2,1)} %get-tuple-element.65.u_ref, ...), custom_call_target="tpu_custom_call" | custom-call | flops 3500000000 | bytes 8000000 | tf_op jit(solution)/shard_map/weigh/pallas_call | solution.py:598
  225.9 2.5 add_convert_fusion.1
  228.6 3.4 add_convert_fusion
  232.0 1.3 dynamic-slice_bitcast_fusion
  233.3 2.0 collective-permute-start.22
  235.3 13.2 %attend_back.2.u_ref = bf16[2,1024,640]{2,1,0:T(8,128)(2,1)} custom-call(s32[1]{0:T(128)} %bitcast.side_ref.side_two_ref, bf16[2,2,4,96,1024]{4,3,2,1,0:T(8,128)(2,1)} %copy-done.2, bf16[2,2,4,96,1024]{4,3,2,1,0:T(8,128)(2,1)} %collective-permute-done.19.other_ref.other_two_ref, bf16[1024,768]{1,0:T(8,128)(2,1)} %get-tuple-element.93.g_ref, ...), custom_call_target="tpu_custom_call" | custom-call | flops 8000000000 | bytes 15000000 | tf_op jit(solution)/shard_map/attend_back/pallas_call | solution.py:382
  248.5 1.6 fusion.1
  250.9 13.5 %attend_back.3.v_ref = bf16[2,1024,640]{2,1,0:T(8,128)(2,1)} custom-call(s32[1]{0:T(128)} %bitcast.side_ref.side_two_ref, bf16[2,2,4,96,1024]{4,3,2,1,0:T(8,128)(2,1)} %copy-done.2, bf16[2,2,4,96,1024]{4,3,2,1,0:T(8,128)(2,1)} %collective-permute-done.19.other_ref.other_two_ref, bf16[1024,768]{1,0:T(8,128)(2,1)} %get-tuple-element.93.g_ref, ...), custom_call_target="tpu_custom_call" | custom-call | flops 8000000000 | bytes 15000000 | tf_op jit(solution)/shard_map/attend_back/pallas_call | solution.py:382
  264.4 2.1 fusion
  266.6 6.4 %weigh.11 = bf16[2,2,4,96,640]{4,3,2,1,0:T(8,128)(2,1)} custom-call(s32[1]{0:T(128)S(6)} %sub.60.side_ref, bf16[768,1024]{1,0:T(8,128)(2,1)} %bitcast.160, bf16[2,1024,640]{2,1,0:T(8,128)(2,1)} %attend_back.2.u_ref, bf16[2,1024,640]{2,1,0:T(8,128)(2,1)} %attend_back.3.v_ref, bf16[768,128]{1,0:T(8,128)(2,1)} %pad.10.s_ref), custom_call_target="tpu_custom_call" | custom-call | flops 2500000000 | bytes 8000000 | tf_op jit(solution)/shard_map/weigh/pallas_call | solution.py:598
  273.9 9.3 %collective-permute-done.37 = bf16[4,96,768]{2,1,0:T(8,128)(2,1)} collective-permute-done((bf16[4,96,768]{2,1,0:T(8,128)(2,1)}, bf16[4,96,768]{2,1,0:T(8,128)(2,1)}, u32[]{:S(2)}, u32[]{:S(2)}) %collective-permute-start.37) | collective-permute-done | bytes 589856 | tf_op jit(solution)/shard_map/ppermute | solution.py:54
  283.3 1.2 fusion.4
  285.2 2.0 collective-permute-start.40
  288.1 6.4 %weigh.10 = bf16[2,2,4,96,640]{4,3,2,1,0:T(8,128)(2,1)} custom-call(s32[1]{0:T(128)} %bitcast.side_ref.side_two_ref, bf16[768,1024]{1,0:T(8,128)(2,1)} %bitcast.161, bf16[2,1024,640]{2,1,0:T(8,128)(2,1)} %attend_back.2.u_ref, bf16[2,1024,640]{2,1,0:T(8,128)(2,1)} %attend_back.3.v_ref, bf16[768,128]{1,0:T(8,128)(2,1)} %pad.10.s_ref), custom_call_target="tpu_custom_call" | custom-call | flops 2500000000 | bytes 8000000 | tf_op jit(solution)/shard_map/weigh/pallas_call | solution.py:598
  294.6 2.6 add_convert_fusion.2
  297.3 1.2 collective-permute-start.26
  299.2 1.1 fusion.9
  301.3 2.4 collective-permute-start.33
  304.3 1.9 collective-permute-start.35
  306.3 10.4 %input_back.1 = bf16[1024,768]{1,0:T(8,128)(2,1)} custom-call(s32[1]{0:T(128)} %bitcast.side_ref.side_two_ref, bf16[2,2,4,96,640]{4,3,2,1,0:T(8,128)(2,1)} %copy-done.3, bf16[2,2,4,96,640]{4,3,2,1,0:T(8,128)(2,1)} %copy-done.8, f32[1024,768]{1,0:T(8,128)} %get-tuple-element.97.res_ref, bf16[2,1024,640]{2,1,0:T(8,128)(2,1)} %attend_back.2.u_ref, ...), custom_call_target="tpu_custom_call" | custom-call | flops 4000000000 | bytes 14000000 | tf_op jit(solution)/shard_map/input_back/pallas_call | solution.py:661
  316.7 0.9 bitcast_select_fusion.3
  319.2 3.3 collective-permute-done.34
  322.7 4.2 %collective-permute-done.27 = bf16[4,96,640]{2,1,0:T(8,128)(2,1)S(1)} collective-permute-done((bf16[4,96,640]{2,1,0:T(8,128)(2,1)S(1)}, bf16[4,96,640]{2,1,0:T(8,128)(2,1)S(1)}, u32[]{:S(2)}, u32[]{:S(2)}) %collective-permute-start.27) | collective-permute-done | bytes 491552 | tf_op jit(solution)/shard_map/ppermute | solution.py:54
  327.1 1.9 collective-permute-start.28
  329.7 3.1 collective-permute-done.28
  332.8 7.3 %collective-permute-done.29 = bf16[96,640]{1,0:T(8,128)(2,1)S(1)} collective-permute-done((bf16[96,640]{1,0:T(8,128)(2,1)S(1)}, bf16[96,640]{1,0:T(8,128)(2,1)S(1)}, u32[]{:S(2)}, u32[]{:S(2)}) %collective-permute-start.29) | collective-permute-done | bytes 122912 | tf_op jit(solution)/shard_map/ppermute | solution.py:54
  (149 shorter events, 20.6 us)
Async XLA Ops:
  0.6 4.9 %copy-start.10 = (s32[2048]{0:T(1024)S(1)}, s32[2048]{0:T(1024)}, u32[]{:S(2)}) copy-start(s32[2048]{0:T(1024)} %param.12) | copy-start | bytes 24580
  2.4 4.2 %collective-permute-start.2 = (bf16[48,640]{1,0:T(8,128)(2,1)S(1)}, bf16[48,640]{1,0:T(8,128)(2,1)S(1)}, u32[]{:S(2)}, u32[]{:S(2)}) collective-permute-start(bf16[48,640]{1,0:T(8,128)(2,1)S(1)} %get-tuple-element.128), channel_id=1, source_target_pairs={{0,2},{1,3},{2,0},{3,1},{4,6},{5,7},{6,4},{7,5},{8,10},{9,11},{10,... | collective-permute-start | bytes 184328 | tf_op jit(solution)/shard_map/ppermute | solution.py:54
  4.0 8.7 %collective-permute-start.1 = (bf16[48,1024]{1,0:T(8,128)(2,1)S(1)}, bf16[48,1024]{1,0:T(8,128)(2,1)S(1)}, u32[]{:S(2)}, u32[]{:S(2)}) collective-permute-start(bf16[48,1024]{1,0:T(8,128)(2,1)S(1)} %get-tuple-element.130), channel_id=1, source_target_pairs={{0,2},{1,3},{2,0},{3,1},{4,6},{5,7},{6,4},{7,5},{8,10},{9,11},{10,... | collective-permute-start | bytes 294920 | tf_op jit(solution)/shard_map/ppermute | solution.py:54
  5.0 7.5 %collective-permute-start = (bf16[48,768]{1,0:T(8,128)(2,1)S(1)}, bf16[48,768]{1,0:T(8,128)(2,1)S(1)}, u32[]{:S(2)}, u32[]{:S(2)}) collective-permute-start(bf16[48,768]{1,0:T(8,128)(2,1)S(1)} %get-tuple-element.149), channel_id=1, source_target_pairs={{0,2},{1,3},{2,0},{3,1},{4,6},{5,7},{6,4},{7,5},{8,10},{9,11},{10,... | collective-permute-start | bytes 221192 | tf_op jit(solution)/shard_map/ppermute | solution.py:54
  5.5 17.5 %copy-start.9 = (s32[1024]{0:T(1024)}, s32[1024]{0:T(1024)S(1)}, u32[]{:S(2)}) copy-start(s32[1024]{0:T(1024)S(1)} %dynamic_slice.117) | copy-start | bytes 12292
  6.7 8.5 %collective-permute-start.3 = (bf16[96,640]{1,0:T(8,128)(2,1)S(1)}, bf16[96,640]{1,0:T(8,128)(2,1)S(1)}, u32[]{:S(2)}, u32[]{:S(2)}) collective-permute-start(bf16[96,640]{1,0:T(8,128)(2,1)S(1)} %maximum_select_fusion.11), channel_id=1, source_target_pairs={{0,24},{1,25},{2,26},{3,27},{4,28},{5,29},{6,30},{7,31},{8,0},{9,1... | collective-permute-start | bytes 368648 | tf_op jit(solution)/shard_map/ppermute | solution.py:54
  11.5 11.4 %collective-permute-start.4 = (bf16[96,640]{1,0:T(8,128)(2,1)S(1)}, bf16[96,640]{1,0:T(8,128)(2,1)S(1)}, u32[]{:S(2)}, u32[]{:S(2)}) collective-permute-start(bf16[96,640]{1,0:T(8,128)(2,1)S(1)} %maximum_select_fusion.11), channel_id=1, source_target_pairs={{0,16},{1,17},{2,18},{3,19},{4,20},{5,21},{6,22},{7,23},{8,24},{9,... | collective-permute-start | bytes 368648 | tf_op jit(solution)/shard_map/ppermute | solution.py:54
  11.5 11.4 %collective-permute-start.5 = (bf16[96,640]{1,0:T(8,128)(2,1)S(1)}, bf16[96,640]{1,0:T(8,128)(2,1)S(1)}, u32[]{:S(2)}, u32[]{:S(2)}) collective-permute-start(bf16[96,640]{1,0:T(8,128)(2,1)S(1)} %maximum_select_fusion.11), channel_id=1, source_target_pairs={{0,8},{1,9},{2,10},{3,11},{4,12},{5,13},{6,14},{7,15},{8,16},{9,17... | collective-permute-start | bytes 368648 | tf_op jit(solution)/shard_map/ppermute | solution.py:54
  23.2 8.9 %collective-permute-start.12 = (bf16[4,96,640]{2,1,0:T(8,128)(2,1)S(1)}, bf16[4,96,640]{2,1,0:T(8,128)(2,1)S(1)}, u32[]{:S(2)}, u32[]{:S(2)}) collective-permute-start(bf16[4,96,640]{2,1,0:T(8,128)(2,1)S(1)} %constant_dynamic-slice_fusion.2), channel_id=1, source_target_pairs={{0,4},{1,5},{2,3},{3,2},{4,0},{5,1},{6,7},{7,6},{8,12},{9,13},{10,... | collective-permute-start | bytes 1474568 | tf_op jit(solution)/shard_map/ppermute | solution.py:54
  24.8 7.1 %collective-permute-start.6 = (bf16[96,1024]{1,0:T(8,128)(2,1)S(1)}, bf16[96,1024]{1,0:T(8,128)(2,1)S(1)}, u32[]{:S(2)}, u32[]{:S(2)}) collective-permute-start(bf16[96,1024]{1,0:T(8,128)(2,1)S(1)} %maximum_select_fusion.8), channel_id=1, source_target_pairs={{0,24},{1,25},{2,26},{3,27},{4,28},{5,29},{6,30},{7,31},{8,0},{9,1... | collective-permute-start | bytes 589832 | tf_op jit(solution)/shard_map/ppermute | solution.py:54
  26.2 17.6 %collective-permute-start.7 = (bf16[96,1024]{1,0:T(8,128)(2,1)S(1)}, bf16[96,1024]{1,0:T(8,128)(2,1)S(1)}, u32[]{:S(2)}, u32[]{:S(2)}) collective-permute-start(bf16[96,1024]{1,0:T(8,128)(2,1)S(1)} %maximum_select_fusion.8), channel_id=1, source_target_pairs={{0,16},{1,17},{2,18},{3,19},{4,20},{5,21},{6,22},{7,23},{8,24},{9,... | collective-permute-start | bytes 589832 | tf_op jit(solution)/shard_map/ppermute | solution.py:54
  27.2 16.7 %collective-permute-start.8 = (bf16[96,1024]{1,0:T(8,128)(2,1)S(1)}, bf16[96,1024]{1,0:T(8,128)(2,1)S(1)}, u32[]{:S(2)}, u32[]{:S(2)}) collective-permute-start(bf16[96,1024]{1,0:T(8,128)(2,1)S(1)} %maximum_select_fusion.8), channel_id=1, source_target_pairs={{0,8},{1,9},{2,10},{3,11},{4,12},{5,13},{6,14},{7,15},{8,16},{9,17... | collective-permute-start | bytes 589832 | tf_op jit(solution)/shard_map/ppermute | solution.py:54
  32.3 14.2 %collective-permute-start.13 = (bf16[2,4,96,640]{3,2,1,0:T(8,128)(2,1)S(1)}, bf16[2,4,96,640]{3,2,1,0:T(8,128)(2,1)S(1)}, u32[]{:S(2)}, u32[]{:S(2)}) collective-permute-start(bf16[2,4,96,640]{3,2,1,0:T(8,128)(2,1)S(1)} %maximum_select_fusion.7), channel_id=1, source_target_pairs={{0,1},{1,0},{2,6},{3,7},{4,5},{5,4},{6,2},{7,3},{8,9},{9,8},{10,14... | collective-permute-start | bytes 2949128 | tf_op jit(solution)/shard_map/ppermute | solution.py:54
  46.8 25.3 %copy-start.3 = (bf16[2,2,4,96,640]{4,3,2,1,0:T(8,128)(2,1)}, bf16[2,2,4,96,640]{4,3,2,1,0:T(8,128)(2,1)S(1)}, u32[]{:S(2)}) copy-start(bf16[2,2,4,96,640]{4,3,2,1,0:T(8,128)(2,1)S(1)} %maximum_select_fusion.2.mine_ref) | copy-start | bytes 5898244
  46.8 26.3 %collective-permute-start.15 = (bf16[2,2,4,96,640]{4,3,2,1,0:T(8,128)(2,1)S(1)}, bf16[2,2,4,96,640]{4,3,2,1,0:T(8,128)(2,1)S(1)}, u32[]{:S(2)}, u32[]{:S(2)}) collective-permute-start(bf16[2,2,4,96,640]{4,3,2,1,0:T(8,128)(2,1)S(1)} %maximum_select_fusion.2.mine_ref), channel_id=1, source_target_pairs={{0,2},{1,3},{2,0},{3,1},{4,6},{5,7},{6,4},{7,5},{8,10},{9,11},{10,... | collective-permute-start | bytes 5898248 | tf_op jit(solution)/shard_map/ppermute | solution.py:54
  47.0 14.4 %collective-permute-start.9 = (bf16[96,768]{1,0:T(8,128)(2,1)S(1)}, bf16[96,768]{1,0:T(8,128)(2,1)S(1)}, u32[]{:S(2)}, u32[]{:S(2)}) collective-permute-start(bf16[96,768]{1,0:T(8,128)(2,1)S(1)} %maximum_select_fusion.9), channel_id=1, source_target_pairs={{0,24},{1,25},{2,26},{3,27},{4,28},{5,29},{6,30},{7,31},{8,0},{9,1... | collective-permute-start | bytes 442376 | tf_op jit(solution)/shard_map/ppermute | solution.py:54
  50.9 21.1 %collective-permute-start.10 = (bf16[96,768]{1,0:T(8,128)(2,1)S(1)}, bf16[96,768]{1,0:T(8,128)(2,1)S(1)}, u32[]{:S(2)}, u32[]{:S(2)}) collective-permute-start(bf16[96,768]{1,0:T(8,128)(2,1)S(1)} %maximum_select_fusion.9), channel_id=1, source_target_pairs={{0,16},{1,17},{2,18},{3,19},{4,20},{5,21},{6,22},{7,23},{8,24},{9,... | collective-permute-start | bytes 442376 | tf_op jit(solution)/shard_map/ppermute | solution.py:54
  58.3 13.7 %collective-permute-start.11 = (bf16[96,768]{1,0:T(8,128)(2,1)S(1)}, bf16[96,768]{1,0:T(8,128)(2,1)S(1)}, u32[]{:S(2)}, u32[]{:S(2)}) collective-permute-start(bf16[96,768]{1,0:T(8,128)(2,1)S(1)} %maximum_select_fusion.9), channel_id=1, source_target_pairs={{0,8},{1,9},{2,10},{3,11},{4,12},{5,13},{6,14},{7,15},{8,16},{9,17... | collective-permute-start | bytes 442376 | tf_op jit(solution)/shard_map/ppermute | solution.py:54
  72.2 18.6 %collective-permute-start.16 = (bf16[4,96,1024]{2,1,0:T(8,128)(2,1)S(1)}, bf16[4,96,1024]{2,1,0:T(8,128)(2,1)S(1)}, u32[]{:S(2)}, u32[]{:S(2)}) collective-permute-start(bf16[4,96,1024]{2,1,0:T(8,128)(2,1)S(1)} %constant_dynamic-slice_fusion.1), channel_id=1, source_target_pairs={{0,4},{1,5},{2,3},{3,2},{4,0},{5,1},{6,7},{7,6},{8,12},{9,13},{10,... | collective-permute-start | bytes 2359304 | tf_op jit(solution)/shard_map/ppermute | solution.py:54
  73.1 1.3 copy-start.8
  91.0 20.5 %collective-permute-start.17 = (bf16[2,4,96,1024]{3,2,1,0:T(8,128)(2,1)S(1)}, bf16[2,4,96,1024]{3,2,1,0:T(8,128)(2,1)S(1)}, u32[]{:S(2)}, u32[]{:S(2)}) collective-permute-start(bf16[2,4,96,1024]{3,2,1,0:T(8,128)(2,1)S(1)} %maximum_select_fusion.4), channel_id=1, source_target_pairs={{0,1},{1,0},{2,6},{3,7},{4,5},{5,4},{6,2},{7,3},{8,9},{9,8},{10,14... | collective-permute-start | bytes 4718600 | tf_op jit(solution)/shard_map/ppermute | solution.py:54
  112.0 12.3 %copy-start.2 = (bf16[2,2,4,96,1024]{4,3,2,1,0:T(8,128)(2,1)}, bf16[2,2,4,96,1024]{4,3,2,1,0:T(8,128)(2,1)S(1)}, u32[]{:S(2)}) copy-start(bf16[2,2,4,96,1024]{4,3,2,1,0:T(8,128)(2,1)S(1)} %maximum_select_fusion.mine_ref.mine_two_ref) | copy-start | bytes 9437188
  112.0 15.0 %collective-permute-start.19 = (bf16[2,2,4,96,1024]{4,3,2,1,0:T(8,128)(2,1)S(1)}, bf16[2,2,4,96,1024]{4,3,2,1,0:T(8,128)(2,1)}, u32[]{:S(2)}, u32[]{:S(2)}) collective-permute-start(bf16[2,2,4,96,1024]{4,3,2,1,0:T(8,128)(2,1)S(1)} %maximum_select_fusion.mine_ref.mine_two_ref), channel_id=1, source_target_pairs={{0,2},{1,3},{2,0},{3,1},{4,6},{5,7},{6,4},{7,5},{8,10},{9,11},{10,... | collective-permute-start | bytes 9437192 | tf_op jit(solution)/shard_map/ppermute | solution.py:54
  112.1 10.3 %collective-permute-start.14 = (bf16[4,96,768]{2,1,0:T(8,128)(2,1)}, bf16[4,96,768]{2,1,0:T(8,128)(2,1)}, u32[]{:S(2)}, u32[]{:S(2)}) collective-permute-start(bf16[4,96,768]{2,1,0:T(8,128)(2,1)} %constant_dynamic-slice_fusion), channel_id=1, source_target_pairs={{0,4},{1,5},{2,3},{3,2},{4,0},{5,1},{6,7},{7,6},{8,12},{9,13},{10,... | collective-permute-start | bytes 1769480 | tf_op jit(solution)/shard_map/ppermute | solution.py:54
  124.3 29.2 %collective-permute-start.18 = (bf16[2,4,96,768]{3,2,1,0:T(8,128)(2,1)S(1)}, bf16[2,4,96,768]{3,2,1,0:T(8,128)(2,1)S(1)}, u32[]{:S(2)}, u32[]{:S(2)}) collective-permute-start(bf16[2,4,96,768]{3,2,1,0:T(8,128)(2,1)S(1)} %maximum_select_fusion.5), channel_id=1, source_target_pairs={{0,1},{1,0},{2,6},{3,7},{4,5},{5,4},{6,2},{7,3},{8,9},{9,8},{10,14... | collective-permute-start | bytes 3538952 | tf_op jit(solution)/shard_map/ppermute | solution.py:54
  153.9 4.6 %copy-start.5 = (bf16[2,2,4,96,768]{4,3,2,1,0:T(8,128)(2,1)}, bf16[2,2,4,96,768]{4,3,2,1,0:T(8,128)(2,1)S(1)}, u32[]{:S(2)}) copy-start(bf16[2,2,4,96,768]{4,3,2,1,0:T(8,128)(2,1)S(1)} %maximum_select_fusion.1.mine_ref) | copy-start | bytes 7077892
  153.9 4.6 %collective-permute-start.20 = (bf16[2,2,4,96,768]{4,3,2,1,0:T(8,128)(2,1)S(1)}, bf16[2,2,4,96,768]{4,3,2,1,0:T(8,128)(2,1)S(1)}, u32[]{:S(2)}, u32[]{:S(2)}) collective-permute-start(bf16[2,2,4,96,768]{4,3,2,1,0:T(8,128)(2,1)S(1)} %maximum_select_fusion.1.mine_ref), channel_id=1, source_target_pairs={{0,2},{1,3},{2,0},{3,1},{4,6},{5,7},{6,4},{7,5},{8,10},{9,11},{10,... | collective-permute-start | bytes 7077896 | tf_op jit(solution)/shard_map/ppermute | solution.py:54
  158.5 1.4 copy-start.11
  199.1 8.5 %copy-start.4 = (bf16[2,2,4,96,768]{4,3,2,1,0:T(8,128)(2,1)S(1)}, bf16[2,2,4,96,768]{4,3,2,1,0:T(8,128)(2,1)}, u32[]{:S(2)}) copy-start(bf16[2,2,4,96,768]{4,3,2,1,0:T(8,128)(2,1)} %weigh.6) | copy-start | bytes 7077892
  207.5 21.1 %collective-permute-start.21 = (bf16[2,2,4,96,1024]{4,3,2,1,0:T(8,128)(2,1)}, bf16[2,2,4,96,1024]{4,3,2,1,0:T(8,128)(2,1)}, u32[]{:S(2)}, u32[]{:S(2)}) collective-permute-start(bf16[2,2,4,96,1024]{4,3,2,1,0:T(8,128)(2,1)} %weigh.8), channel_id=1, source_target_pairs={{0,2},{1,3},{2,0},{3,1},{4,6},{5,7},{6,4},{7,5},{8,10},{9,11},{10,... | collective-permute-start | bytes 9437192 | tf_op jit(solution)/shard_map/ppermute | solution.py:54
  207.6 18.3 %collective-permute-start.23 = (bf16[2,2,4,96,768]{4,3,2,1,0:T(8,128)(2,1)S(1)}, bf16[2,2,4,96,768]{4,3,2,1,0:T(8,128)(2,1)}, u32[]{:S(2)}, u32[]{:S(2)}) collective-permute-start(bf16[2,2,4,96,768]{4,3,2,1,0:T(8,128)(2,1)S(1)} %copy-done.4), channel_id=1, source_target_pairs={{0,2},{1,3},{2,0},{3,1},{4,6},{5,7},{6,4},{7,5},{8,10},{9,11},{10,... | collective-permute-start | bytes 7077896 | tf_op jit(solution)/shard_map/ppermute | solution.py:54
  208.0 2.6 copy-start.7
  217.6 8.2 %copy-start.1 = (bf16[2,2,4,96,768]{4,3,2,1,0:T(8,128)(2,1)S(1)}, bf16[2,2,4,96,768]{4,3,2,1,0:T(8,128)(2,1)}, u32[]{:S(2)}) copy-start(bf16[2,2,4,96,768]{4,3,2,1,0:T(8,128)(2,1)} %weigh.9) | copy-start | bytes 7077892
  225.9 2.7 copy-start
  228.5 20.0 %collective-permute-start.24 = (bf16[2,4,96,768]{3,2,1,0:T(8,128)(2,1)S(1)}, bf16[2,4,96,768]{3,2,1,0:T(8,128)(2,1)}, u32[]{:S(2)}, u32[]{:S(2)}) collective-permute-start(bf16[2,4,96,768]{3,2,1,0:T(8,128)(2,1)S(1)} %dynamic-slice_bitcast_fusion.1), channel_id=1, source_target_pairs={{0,1},{1,0},{2,6},{3,7},{4,5},{5,4},{6,2},{7,3},{8,9},{9,8},{10,14... | collective-permute-start | bytes 3538952 | tf_op jit(solution)/shard_map/ppermute | solution.py:54
  233.3 31.1 %collective-permute-start.22 = (bf16[2,4,96,1024]{3,2,1,0:T(8,128)(2,1)}, bf16[2,4,96,1024]{3,2,1,0:T(8,128)(2,1)}, u32[]{:S(2)}, u32[]{:S(2)}) collective-permute-start(bf16[2,4,96,1024]{3,2,1,0:T(8,128)(2,1)} %dynamic-slice_bitcast_fusion), channel_id=1, source_target_pairs={{0,1},{1,0},{2,6},{3,7},{4,5},{5,4},{6,2},{7,3},{8,9},{9,8},{10,14... | collective-permute-start | bytes 4718600 | tf_op jit(solution)/shard_map/ppermute | solution.py:54
  273.0 21.5 %collective-permute-start.25 = (bf16[2,2,4,96,640]{4,3,2,1,0:T(8,128)(2,1)}, bf16[2,2,4,96,640]{4,3,2,1,0:T(8,128)(2,1)}, u32[]{:S(2)}, u32[]{:S(2)}) collective-permute-start(bf16[2,2,4,96,640]{4,3,2,1,0:T(8,128)(2,1)} %weigh.11), channel_id=1, source_target_pairs={{0,2},{1,3},{2,0},{3,1},{4,6},{5,7},{6,4},{7,5},{8,10},{9,11},{10,... | collective-permute-start | bytes 5898248 | tf_op jit(solution)/shard_map/ppermute | solution.py:54
  273.1 10.2 %collective-permute-start.37 = (bf16[4,96,768]{2,1,0:T(8,128)(2,1)}, bf16[4,96,768]{2,1,0:T(8,128)(2,1)}, u32[]{:S(2)}, u32[]{:S(2)}) collective-permute-start(bf16[4,96,768]{2,1,0:T(8,128)(2,1)} %dynamic-slice_bitcast_fusion.4), channel_id=1, source_target_pairs={{0,4},{1,5},{2,3},{3,2},{4,0},{5,1},{6,7},{7,6},{8,12},{9,13},{10,... | collective-permute-start | bytes 1769480 | tf_op jit(solution)/shard_map/ppermute | solution.py:54
  285.2 13.3 %collective-permute-start.38 = (bf16[96,768]{1,0:T(8,128)(2,1)}, bf16[96,768]{1,0:T(8,128)(2,1)S(1)}, u32[]{:S(2)}, u32[]{:S(2)}) collective-permute-start(bf16[96,768]{1,0:T(8,128)(2,1)} %get-tuple-element.137), channel_id=1, source_target_pairs={{0,24},{1,25},{2,26},{3,27},{4,28},{5,29},{6,30},{7,31},{8,0},{9,1... | collective-permute-start | bytes 442376 | tf_op jit(solution)/shard_map/ppermute | solution.py:54
  285.2 13.3 %collective-permute-start.39 = (bf16[96,768]{1,0:T(8,128)(2,1)}, bf16[96,768]{1,0:T(8,128)(2,1)S(1)}, u32[]{:S(2)}, u32[]{:S(2)}) collective-permute-start(bf16[96,768]{1,0:T(8,128)(2,1)} %get-tuple-element.136), channel_id=1, source_target_pairs={{0,16},{1,17},{2,18},{3,19},{4,20},{5,21},{6,22},{7,23},{8,24},{9,... | collective-permute-start | bytes 442376 | tf_op jit(solution)/shard_map/ppermute | solution.py:54
  285.2 13.9 %collective-permute-start.40 = (bf16[96,768]{1,0:T(8,128)(2,1)S(1)}, bf16[96,768]{1,0:T(8,128)(2,1)}, u32[]{:S(2)}, u32[]{:S(2)}) collective-permute-start(bf16[96,768]{1,0:T(8,128)(2,1)S(1)} %get-tuple-element.135), channel_id=1, source_target_pairs={{0,8},{1,9},{2,10},{3,11},{4,12},{5,13},{6,14},{7,15},{8,16},{9,17... | collective-permute-start | bytes 442376 | tf_op jit(solution)/shard_map/ppermute | solution.py:54
  287.2 13.7 %collective-permute-start.32 = (bf16[4,96,1024]{2,1,0:T(8,128)(2,1)S(1)}, bf16[4,96,1024]{2,1,0:T(8,128)(2,1)S(1)}, u32[]{:S(2)}, u32[]{:S(2)}) collective-permute-start(bf16[4,96,1024]{2,1,0:T(8,128)(2,1)S(1)} %dynamic-slice_bitcast_fusion.3), channel_id=1, source_target_pairs={{0,4},{1,5},{2,3},{3,2},{4,0},{5,1},{6,7},{7,6},{8,12},{9,13},{10,... | collective-permute-start | bytes 2359304 | tf_op jit(solution)/shard_map/ppermute | solution.py:54
  297.3 20.4 %collective-permute-start.26 = (bf16[2,4,96,640]{3,2,1,0:T(8,128)(2,1)S(1)}, bf16[2,4,96,640]{3,2,1,0:T(8,128)(2,1)S(1)}, u32[]{:S(2)}, u32[]{:S(2)}) collective-permute-start(bf16[2,4,96,640]{3,2,1,0:T(8,128)(2,1)S(1)} %dynamic-slice_bitcast_fusion.2), channel_id=1, source_target_pairs={{0,1},{1,0},{2,6},{3,7},{4,5},{5,4},{6,2},{7,3},{8,9},{9,8},{10,14... | collective-permute-start | bytes 2949128 | tf_op jit(solution)/shard_map/ppermute | solution.py:54
  298.5 0.7 copy-start.6
  300.9 15.8 %collective-permute-start.41 = (f32[48,768]{1,0:T(8,128)}, f32[48,768]{1,0:T(8,128)}, u32[]{:S(2)}, u32[]{:S(2)}) collective-permute-start(f32[48,768]{1,0:T(8,128)} %dynamic-slice_bitcast_fusion.10), channel_id=1, source_target_pairs={{0,2},{1,3},{2,0},{3,1},{4,6},{5,7},{6,4},{7,5},{8,10},{9,11},{10,... | collective-permute-start | bytes 442376 | tf_op jit(solution)/shard_map/ppermute | solution.py:54
  301.3 17.9 %collective-permute-start.33 = (bf16[96,1024]{1,0:T(8,128)(2,1)S(1)}, bf16[96,1024]{1,0:T(8,128)(2,1)S(1)}, u32[]{:S(2)}, u32[]{:S(2)}) collective-permute-start(bf16[96,1024]{1,0:T(8,128)(2,1)S(1)} %get-tuple-element.132), channel_id=1, source_target_pairs={{0,24},{1,25},{2,26},{3,27},{4,28},{5,29},{6,30},{7,31},{8,0},{9,1... | collective-permute-start | bytes 589832 | tf_op jit(solution)/shard_map/ppermute | solution.py:54
  303.7 18.8 %collective-permute-start.34 = (bf16[96,1024]{1,0:T(8,128)(2,1)S(1)}, bf16[96,1024]{1,0:T(8,128)(2,1)S(1)}, u32[]{:S(2)}, u32[]{:S(2)}) collective-permute-start(bf16[96,1024]{1,0:T(8,128)(2,1)S(1)} %get-tuple-element.134), channel_id=1, source_target_pairs={{0,16},{1,17},{2,18},{3,19},{4,20},{5,21},{6,22},{7,23},{8,24},{9,... | collective-permute-start | bytes 589832 | tf_op jit(solution)/shard_map/ppermute | solution.py:54
  304.3 18.1 %collective-permute-start.35 = (bf16[96,1024]{1,0:T(8,128)(2,1)S(1)}, bf16[96,1024]{1,0:T(8,128)(2,1)S(1)}, u32[]{:S(2)}, u32[]{:S(2)}) collective-permute-start(bf16[96,1024]{1,0:T(8,128)(2,1)S(1)} %get-tuple-element.133), channel_id=1, source_target_pairs={{0,8},{1,9},{2,10},{3,11},{4,12},{5,13},{6,14},{7,15},{8,16},{9,17... | collective-permute-start | bytes 589832 | tf_op jit(solution)/shard_map/ppermute | solution.py:54
  318.0 8.9 %collective-permute-start.27 = (bf16[4,96,640]{2,1,0:T(8,128)(2,1)S(1)}, bf16[4,96,640]{2,1,0:T(8,128)(2,1)S(1)}, u32[]{:S(2)}, u32[]{:S(2)}) collective-permute-start(bf16[4,96,640]{2,1,0:T(8,128)(2,1)S(1)} %dynamic-slice_bitcast_fusion.5), channel_id=1, source_target_pairs={{0,4},{1,5},{2,3},{3,2},{4,0},{5,1},{6,7},{7,6},{8,12},{9,13},{10,... | collective-permute-start | bytes 1474568 | tf_op jit(solution)/shard_map/ppermute | solution.py:54
  322.6 7.0 %collective-permute-start.36 = (f32[48,1024]{1,0:T(8,128)S(1)}, f32[48,1024]{1,0:T(8,128)S(1)}, u32[]{:S(2)}, u32[]{:S(2)}) collective-permute-start(f32[48,1024]{1,0:T(8,128)S(1)} %dynamic-slice_bitcast_fusion.6), channel_id=1, source_target_pairs={{0,2},{1,3},{2,0},{3,1},{4,6},{5,7},{6,4},{7,5},{8,10},{9,11},{10,... | collective-permute-start | bytes 589832 | tf_op jit(solution)/shard_map/ppermute | solution.py:54
  327.1 5.7 %collective-permute-start.28 = (bf16[96,640]{1,0:T(8,128)(2,1)S(1)}, bf16[96,640]{1,0:T(8,128)(2,1)S(1)}, u32[]{:S(2)}, u32[]{:S(2)}) collective-permute-start(bf16[96,640]{1,0:T(8,128)(2,1)S(1)} %get-tuple-element.140), channel_id=1, source_target_pairs={{0,24},{1,25},{2,26},{3,27},{4,28},{5,29},{6,30},{7,31},{8,0},{9,1... | collective-permute-start | bytes 368648 | tf_op jit(solution)/shard_map/ppermute | solution.py:54
  329.0 11.0 %collective-permute-start.29 = (bf16[96,640]{1,0:T(8,128)(2,1)S(1)}, bf16[96,640]{1,0:T(8,128)(2,1)S(1)}, u32[]{:S(2)}, u32[]{:S(2)}) collective-permute-start(bf16[96,640]{1,0:T(8,128)(2,1)S(1)} %get-tuple-element.142), channel_id=1, source_target_pairs={{0,16},{1,17},{2,18},{3,19},{4,20},{5,21},{6,22},{7,23},{8,24},{9,... | collective-permute-start | bytes 368648 | tf_op jit(solution)/shard_map/ppermute | solution.py:54
  329.5 10.5 %collective-permute-start.30 = (bf16[96,640]{1,0:T(8,128)(2,1)S(1)}, bf16[96,640]{1,0:T(8,128)(2,1)S(1)}, u32[]{:S(2)}, u32[]{:S(2)}) collective-permute-start(bf16[96,640]{1,0:T(8,128)(2,1)S(1)} %get-tuple-element.141), channel_id=1, source_target_pairs={{0,8},{1,9},{2,10},{3,11},{4,12},{5,13},{6,14},{7,15},{8,16},{9,17... | collective-permute-start | bytes 368648 | tf_op jit(solution)/shard_map/ppermute | solution.py:54
  340.1 1.5 collective-permute-start.31
